TPU v7x, 32 devices: a whole 2x2x4 slice. The times are simulated.
32 devices in a mesh: fsdp: 32 (over z, y, x, core).
Axes of the slice: x: 2, y: 2, z: 4, core: 2. Of those that a mesh axis runs over, the one named last changes fastest.
Arguments:
- inputs: bfloat16 [8192, 2048], P('fsdp'), may hold values from -6 to 6
- positions: int32 [8192], P('fsdp'), may hold values from 0 to 199, as said below
- norm1_gain: bfloat16 [2048], P('fsdp'), may hold values from 0.5 to 1.5
- norm1_bias: bfloat16 [2048], P('fsdp'), may hold values from -4 to 4
- qkv_weight: bfloat16 [2048, 6144], P('fsdp'), may hold values from -0.125 to 0.125
- qkv_bias: bfloat16 [6144], P('fsdp'), may hold values from -4 to 4
- out_weight: bfloat16 [2048, 2048], P('fsdp'), may hold values from -0.5 to 0.5
- norm2_gain: bfloat16 [2048], P('fsdp'), may hold values from 0.5 to 1.5
- norm2_bias: bfloat16 [2048], P('fsdp'), may hold values from -4 to 4
- gate_weight: bfloat16 [2048, 5632], P('fsdp'), may hold values from -0.125 to 0.125
- up_weight: bfloat16 [2048, 5632], P('fsdp'), may hold values from -0.125 to 0.125
- down_weight: bfloat16 [5632, 2048], P('fsdp'), may hold values from -0.078125 to 0.078125
- out_grad: bfloat16 [8192, 2048], P('fsdp'), may hold values from -6 to 6
Outputs:
- block_out: bfloat16 [8192, 2048], P('fsdp')
- input_grad: float32 [8192, 2048], P('fsdp')
- norm1_gain_grad: float32 [2048], P('fsdp')
- norm1_bias_grad: float32 [2048], P('fsdp')
- qkv_weight_grad: float32 [2048, 6144], P('fsdp')
- qkv_bias_grad: float32 [6144], P('fsdp')
- out_weight_grad: float32 [2048, 2048], P('fsdp')
- norm2_gain_grad: float32 [2048], P('fsdp')
- norm2_bias_grad: float32 [2048], P('fsdp')
- gate_weight_grad: float32 [2048, 5632], P('fsdp')
- up_weight_grad: float32 [2048, 5632], P('fsdp')
- down_weight_grad: float32 [5632, 2048], P('fsdp')
Inputs may be any that keep to these rules, and one draw needn't show every extreme that they name: `positions`: positions count up by one from 0 inside each document; a document begins where the position is 0, every packed sequence of 256 tokens (tokens k * 256 onward) begins a document, and documents never cross sequences.
All inputs are finite; a program needn't handle non-finite values.
Results may differ from a plain program's by a relative error of at most 0.012.
Values may be sent and summed in bfloat16 or wider, within the bound.
A program may use at most 448 MiB of HBM per device.

v0:
```python
import jax
import jax.numpy as jnp
from jax import lax
from jax.sharding import PartitionSpec as P

D = 2048
HEADS = 32
HEAD_DIM = 64
ROT = 16


EPS = 1e-05
HIGHEST = lax.Precision.HIGHEST


def normalize(stream):
    average = jnp.mean(stream, axis=-1, keepdims=True)
    centered = stream - average
    variance = jnp.mean(centered * centered, axis=-1, keepdims=True)
    inverse = lax.rsqrt(variance + EPS)
    return (centered * inverse, inverse)


def norm_back(grad_norm, normed, inverse):
    return inverse * (
        grad_norm
        - jnp.mean(grad_norm, axis=-1, keepdims=True)
        - normed * jnp.mean(grad_norm * normed, axis=-1, keepdims=True)
    )


def rotate_pairs(heads, places, sign):
    half_rot = ROT // 2
    frequency = 10000.0 ** (-jnp.arange(half_rot, dtype=jnp.float32) / half_rot)
    angles = places.astype(jnp.float32)[:, None] * frequency[None, :]
    cosine = jnp.cos(angles)[:, None, :]
    sine_part = sign * jnp.sin(angles)[:, None, :]
    front_part = heads[..., :half_rot]
    back_part = heads[..., half_rot:ROT]
    return jnp.concatenate(
        [
            front_part * cosine - back_part * sine_part,
            back_part * cosine + front_part * sine_part,
            heads[..., ROT:],
        ],
        axis=-1,
    )


def by_groups(heads):
    group_heads = min(8, HEADS)
    shaped = heads.reshape(heads.shape[0], HEADS // group_heads, group_heads, HEAD_DIM)
    return jnp.moveaxis(shaped, 1, 0)


def from_groups(grouped):
    return jnp.moveaxis(grouped, 0, 1).reshape(grouped.shape[1], HEADS, HEAD_DIM)


def attend_group(block_items, allowed):
    query_part, key_part, value_part = block_items
    scores = (
        jnp.einsum("qhd,khd->hqk", query_part, key_part, preferred_element_type=jnp.float32) * 0.125
    )
    masked = jnp.where(allowed[None], scores, -1e30)
    row_max = jnp.max(masked, axis=-1, keepdims=True)
    exponent = jnp.exp(masked - row_max)
    row_total = jnp.sum(exponent, axis=-1, keepdims=True)
    soft_probs = (exponent / row_total).astype(jnp.bfloat16)
    mixed_part = jnp.einsum(
        "hqk,khd->qhd", soft_probs, value_part, preferred_element_type=jnp.float32
    )
    return (mixed_part, (row_max + jnp.log(row_total))[..., 0])


def attend_back(block_items, allowed):
    query_part, key_part, value_part, grad_part, row_delta, log_total = block_items
    scores = (
        jnp.einsum("qhd,khd->hqk", query_part, key_part, preferred_element_type=jnp.float32) * 0.125
    )
    soft_probs = jnp.where(allowed[None], jnp.exp(scores - log_total[..., None]), 0.0)
    grad_probs = jnp.einsum(
        "qhd,khd->hqk", grad_part, value_part.astype(jnp.float32), precision=HIGHEST
    )
    rounded_probs = soft_probs.astype(jnp.bfloat16).astype(jnp.float32)
    grad_value = jnp.einsum("hqk,qhd->khd", rounded_probs, grad_part, precision=HIGHEST)
    grad_scores = (soft_probs * (grad_probs - row_delta[..., None])).astype(jnp.bfloat16)
    grad_query = 0.125 * jnp.einsum(
        "hqk,khd->qhd", grad_scores, key_part, preferred_element_type=jnp.float32
    )
    grad_key = 0.125 * jnp.einsum(
        "hqk,qhd->khd", grad_scores, query_part, preferred_element_type=jnp.float32
    )
    return (grad_query, grad_key, grad_value)


def shards(
    inputs,
    positions,
    norm1_gain,
    norm1_bias,
    qkv_weight,
    qkv_bias,
    out_weight,
    norm2_gain,
    norm2_bias,
    gate_weight,
    up_weight,
    down_weight,
    out_grad,
):
    tok_rows = inputs.shape[0]
    gain_one, bias_one, w_qkv, b_qkv, w_out = (
        lax.all_gather(norm1_gain, "fsdp", axis=0, tiled=True),
        lax.all_gather(norm1_bias, "fsdp", axis=0, tiled=True),
        lax.all_gather(qkv_weight, "fsdp", axis=0, tiled=True),
        lax.all_gather(qkv_bias, "fsdp", axis=0, tiled=True),
        lax.all_gather(out_weight, "fsdp", axis=0, tiled=True),
    )
    stream = inputs.astype(jnp.float32)
    normed_one, inverse_one = normalize(stream)
    h_one = (normed_one * gain_one.astype(jnp.float32) + bias_one.astype(jnp.float32)).astype(
        jnp.bfloat16
    )
    qkv_pre = jnp.dot(h_one, w_qkv, preferred_element_type=jnp.float32) + b_qkv.astype(jnp.float32)
    qkv_heads = qkv_pre.reshape(tok_rows, 3, HEADS, HEAD_DIM)
    query_low = rotate_pairs(qkv_heads[:, 0], positions, 1.0).astype(jnp.bfloat16)
    key_all = rotate_pairs(qkv_heads[:, 1], positions, 1.0).astype(jnp.bfloat16)
    value_all = qkv_heads[:, 2].astype(jnp.bfloat16)
    token_index = jnp.arange(tok_rows, dtype=jnp.int32)
    allowed = (token_index[None, :] <= token_index[:, None]) & (
        token_index[None, :] >= (token_index - positions)[:, None]
    )
    mixed_grouped, log_grouped = lax.map(
        lambda block_items: attend_group(block_items, allowed),
        (by_groups(query_low), by_groups(key_all), by_groups(value_all)),
    )
    mixed_heads = from_groups(mixed_grouped)
    attn_low = mixed_heads.reshape(tok_rows, D).astype(jnp.bfloat16)
    resid = stream + jnp.dot(attn_low, w_out, preferred_element_type=jnp.float32)
    gain_two, bias_two, w_gate, w_up, w_down = (
        lax.all_gather(norm2_gain, "fsdp", axis=0, tiled=True),
        lax.all_gather(norm2_bias, "fsdp", axis=0, tiled=True),
        lax.all_gather(gate_weight, "fsdp", axis=0, tiled=True),
        lax.all_gather(up_weight, "fsdp", axis=0, tiled=True),
        lax.all_gather(down_weight, "fsdp", axis=0, tiled=True),
    )
    normed_two, inverse_two = normalize(resid)
    h_two = (normed_two * gain_two.astype(jnp.float32) + bias_two.astype(jnp.float32)).astype(
        jnp.bfloat16
    )
    gate_pre = jnp.dot(h_two, w_gate, preferred_element_type=jnp.float32)
    up_pre = jnp.dot(h_two, w_up, preferred_element_type=jnp.float32)
    sigmoid_gate = jax.nn.sigmoid(gate_pre)
    silu_gate = gate_pre * sigmoid_gate
    hidden = (silu_gate * up_pre).astype(jnp.bfloat16)
    block_out = (resid + jnp.dot(hidden, w_down, preferred_element_type=jnp.float32)).astype(
        jnp.bfloat16
    )
    gain_two, w_gate, w_up, w_down = (
        lax.all_gather(norm2_gain, "fsdp", axis=0, tiled=True),
        lax.all_gather(gate_weight, "fsdp", axis=0, tiled=True),
        lax.all_gather(up_weight, "fsdp", axis=0, tiled=True),
        lax.all_gather(down_weight, "fsdp", axis=0, tiled=True),
    )
    grad_down_w = jnp.einsum("tf,td->fd", hidden, out_grad, preferred_element_type=jnp.float32)
    grad_hidden = jnp.einsum("td,fd->tf", out_grad, w_down, preferred_element_type=jnp.float32)
    grad_gate = (
        grad_hidden * up_pre * sigmoid_gate * (1.0 + gate_pre * (1.0 - sigmoid_gate))
    ).astype(jnp.bfloat16)
    grad_up = (grad_hidden * silu_gate).astype(jnp.bfloat16)
    grad_gate_w = jnp.einsum("td,tf->df", h_two, grad_gate, preferred_element_type=jnp.float32)
    grad_up_w = jnp.einsum("td,tf->df", h_two, grad_up, preferred_element_type=jnp.float32)
    grad_htwo = jnp.einsum(
        "tf,df->td", grad_gate, w_gate, preferred_element_type=jnp.float32
    ) + jnp.einsum("tf,df->td", grad_up, w_up, preferred_element_type=jnp.float32)
    grad_gain_two = jnp.sum(grad_htwo * normed_two, axis=0)
    grad_bias_two = jnp.sum(grad_htwo, axis=0)
    grad_resid = out_grad.astype(jnp.float32) + norm_back(
        grad_htwo * gain_two.astype(jnp.float32), normed_two, inverse_two
    )
    mlp_sums = (
        lax.psum_scatter(grad_gain_two, "fsdp", scatter_dimension=0, tiled=True),
        lax.psum_scatter(grad_bias_two, "fsdp", scatter_dimension=0, tiled=True),
        lax.psum_scatter(grad_gate_w, "fsdp", scatter_dimension=0, tiled=True),
        lax.psum_scatter(grad_up_w, "fsdp", scatter_dimension=0, tiled=True),
        lax.psum_scatter(grad_down_w, "fsdp", scatter_dimension=0, tiled=True),
    )
    gain_one, w_qkv, w_out = (
        lax.all_gather(norm1_gain, "fsdp", axis=0, tiled=True),
        lax.all_gather(qkv_weight, "fsdp", axis=0, tiled=True),
        lax.all_gather(out_weight, "fsdp", axis=0, tiled=True),
    )
    grad_branch = grad_resid.astype(jnp.bfloat16)
    grad_out_w = jnp.einsum("ti,td->id", attn_low, grad_branch, preferred_element_type=jnp.float32)
    grad_att = jnp.einsum(
        "td,id->ti", grad_branch, w_out, preferred_element_type=jnp.float32
    ).reshape(tok_rows, HEADS, HEAD_DIM)
    group_heads = min(8, HEADS)
    row_delta = jnp.sum(grad_att * mixed_heads, axis=-1)
    delta_grouped = row_delta.reshape(tok_rows, HEADS // group_heads, group_heads).transpose(
        1, 2, 0
    )
    query_grouped, key_grouped, value_grouped = lax.map(
        lambda block_items: attend_back(block_items, allowed),
        (
            by_groups(query_low),
            by_groups(key_all),
            by_groups(value_all),
            by_groups(grad_att),
            delta_grouped,
            log_grouped,
        ),
    )
    grad_query = from_groups(query_grouped)
    grad_key = from_groups(key_grouped)
    grad_value = from_groups(value_grouped)
    grad_qkv = (
        jnp.stack(
            [
                rotate_pairs(grad_query, positions, -1.0),
                rotate_pairs(grad_key, positions, -1.0),
                grad_value,
            ],
            axis=1,
        )
        .reshape(tok_rows, 3 * D)
        .astype(jnp.bfloat16)
    )
    grad_qkv_w = jnp.einsum("td,tk->dk", h_one, grad_qkv, preferred_element_type=jnp.float32)
    grad_qkv_b = jnp.sum(grad_qkv.astype(jnp.float32), axis=0)
    grad_hone = jnp.einsum("tk,dk->td", grad_qkv, w_qkv, preferred_element_type=jnp.float32)
    grad_gain_one = jnp.sum(grad_hone * normed_one, axis=0)
    grad_bias_one = jnp.sum(grad_hone, axis=0)
    input_grad = grad_resid + norm_back(
        grad_hone * gain_one.astype(jnp.float32), normed_one, inverse_one
    )
    attn_sums = (
        lax.psum_scatter(grad_gain_one, "fsdp", scatter_dimension=0, tiled=True),
        lax.psum_scatter(grad_bias_one, "fsdp", scatter_dimension=0, tiled=True),
        lax.psum_scatter(grad_qkv_w, "fsdp", scatter_dimension=0, tiled=True),
        lax.psum_scatter(grad_qkv_b, "fsdp", scatter_dimension=0, tiled=True),
        lax.psum_scatter(grad_out_w, "fsdp", scatter_dimension=0, tiled=True),
    )
    return (
        block_out,
        input_grad,
        attn_sums[0],
        attn_sums[1],
        attn_sums[2],
        attn_sums[3],
        attn_sums[4],
        mlp_sums[0],
        mlp_sums[1],
        mlp_sums[2],
        mlp_sums[3],
        mlp_sums[4],
    )


def solution(mesh):
    return jax.shard_map(
        shards,
        mesh=mesh,
        in_specs=(
            P("fsdp", None),
            P("fsdp"),
            P("fsdp"),
            P("fsdp"),
            P("fsdp", None),
            P("fsdp"),
            P("fsdp", None),
            P("fsdp"),
            P("fsdp"),
            P("fsdp", None),
            P("fsdp", None),
            P("fsdp", None),
            P("fsdp", None),
        ),
        out_specs=(
            P("fsdp", None),
            P("fsdp", None),
            P("fsdp"),
            P("fsdp"),
            P("fsdp", None),
            P("fsdp"),
            P("fsdp", None),
            P("fsdp"),
            P("fsdp"),
            P("fsdp", None),
            P("fsdp", None),
            P("fsdp", None),
        ),
        check_vma=False,
    )
```

profile of v0, /device:TPU:0, one launch (start us, length us, event | category | flops | bytes accessed | tf_op | source)
XLA Modules:
  0.0 2851.2 jit_solution(14121674478035964919)
XLA Ops:
  12.0 43.5 %all-reduce.11 = (bf16[6144]{0:T(1024)(128)(2,1)S(1)}, bf16[2048]{0:T(1024)(128)(2,1)S(1)}, bf16[2048]{0:T(1024)(128)(2,1)S(1)}, bf16[2048]{0:T(1024)(128)(2,1)S(1)}, bf16[2048]{0:T(1024)(128)(2,1)S(1)}) all-reduce(bf16[6144]{0:T(1024)(128)(2,1)S(1)} %dynamic-update-slice.2, ...), channel_id=1, replica_groups=mesh['fsdp'=32] {'fsdp'}, use_global_device_ids=true, to_apply=%add.2 | all-reduce | flops 14336 | bytes 57344
  57.0 112.9 %all-gather.6.cloned.1.call-done = bf16[2048,6144]{1,0:T(8,128)(2,1)} async-done(((bf16[64,6144]{1,0:T(8,128)(2,1)}), bf16[2048,6144]{1,0:T(8,128)(2,1)}) %all-gather.6.cloned.1.call-update) | async-done | bytes 25165840 | tf_op jit(solution)/shard_map/all_gather | solution.py:116
  169.8 13.4 convolution_add_fusion
  183.3 6.6 copy.53
  189.8 2.7 slice.99
  192.5 2.5 slice_bitcast_fusion
  197.3 13.9 while.28
  198.3 2.4 fusion.131
  201.8 2.4 fusion.131
  205.3 2.4 fusion.131
  208.8 2.4 fusion.131
  211.2 3.5 bitcast_convert_fusion
  214.7 33.6 %all-gather.8.cloned.1.call-done = bf16[2048,2048]{1,0:T(8,128)(2,1)} async-done(((bf16[64,2048]{1,0:T(8,128)(2,1)}), bf16[2048,2048]{1,0:T(8,128)(2,1)}) %all-gather.8.cloned.1.call-update) | async-done | bytes 8388624 | tf_op jit(solution)/shard_map/all_gather | solution.py:118
  248.3 6.1 fusion.73
  256.3 138.1 %all-gather.10.cloned.1.call-done = bf16[2048,5632]{1,0:T(8,128)(2,1)} async-done(((bf16[64,5632]{1,0:T(8,128)(2,1)}), bf16[2048,5632]{1,0:T(8,128)(2,1)}) %all-gather.10.cloned.1.call-update) | async-done | bytes 23068688 | tf_op jit(solution)/shard_map/all_gather | solution.py:144
  394.4 12.8 fusion.74
  407.2 132.7 %all-gather.12.cloned.1.call-done = bf16[2048,5632]{1,0:T(8,128)(2,1)} async-done(((bf16[64,5632]{1,0:T(8,128)(2,1)}), bf16[2048,5632]{1,0:T(8,128)(2,1)}) %all-gather.12.cloned.1.call-update) | async-done | bytes 23068688 | tf_op jit(solution)/shard_map/all_gather | solution.py:145
  539.9 12.8 fusion.75
  552.7 132.7 %all-gather.14.cloned.1.call-done = bf16[5632,2048]{1,0:T(8,128)(2,1)} async-done(((bf16[176,2048]{1,0:T(8,128)(2,1)}), bf16[5632,2048]{1,0:T(8,128)(2,1)}) %all-gather.14.cloned.1.call-update) | async-done | bytes 23068688 | tf_op jit(solution)/shard_map/all_gather | solution.py:146
  685.4 18.5 multiply_convert_fusion.1
  704.0 12.5 fusion.76
  716.5 14.2 multiply_reduce_fusion
  730.7 2.9 multiply_add_fusion
  735.0 8.1 fusion.66
  745.1 8.2 fusion.65
  756.4 39.2 %while.29 = (s32[]{:T(128)}, f32[4,256,8,64]{1,3,2,0:T(8,128)}, f32[4,256,8,64]{1,3,2,0:T(8,128)}, bf16[4,256,8,64]{1,3,2,0:T(8,128)(2,1)}, bf16[4,256,8,64]{1,3...) while((s32[]{:T(128)}, f32[4,256,8,64]{1,3,2,0:T(8,128)}, ...), condition=%wide.region_12.13_spmd.clone, body=%wide.region_11.12_spmd.clone.sunk | while | flops 1010761728 | bytes 13555833 | solution.py:204
  758.4 2.3 multiply_convert_fusion.5
  760.7 2.1 fusion.144
  762.8 2.2 fusion.143
  768.2 2.3 multiply_convert_fusion.5
  772.5 2.2 fusion.143
  777.9 2.3 multiply_convert_fusion.5
  782.2 2.2 fusion.143
  787.6 2.3 multiply_convert_fusion.5
  792.0 2.2 fusion.143
  800.3 3.2 convert_reduce_fusion
  803.5 22.2 fusion.70
  827.0 20.2 fusion.77
  847.3 20.4 fusion.78
  868.9 20.2 fusion.79
  889.3 14.2 fusion.63
  903.5 40.7 %all-reduce.10 = (f32[2048]{0:T(1024)S(1)}, f32[2048]{0:T(1024)S(1)}, f32[6144]{0:T(1024)S(1)}, f32[2048]{0:T(1024)S(1)}, f32[2048]{0:T(1024)S(1)}) all-reduce(f32[2048]{0:T(1024)S(1)} %get-tuple-element.158, f32[2048]{0:T(1024)S(1)} %get-tuple-element.163, f32[6144]{0:T(1024)S(1)} %reduce_sum.149, ...), channel_id=2, replica_groups=mesh['fsdp'=32] {'fsdp'}, use_global_device_ids=true, to_apply=%region_16.17.clone | all-reduce | flops 14336 | bytes 114688
  947.2 4.2 fusion.62
  952.4 16.6 fusion.50
  969.1 396.2 %reduce-scatter.6.cloned.1.call-done = f32[64,6144]{1,0:T(8,128)} async-done(((f32[2048,6144]{1,0:T(8,128)}), f32[64,6144]{1,0:T(8,128)}) %reduce-scatter.6.cloned.1.call-update) | async-done | bytes 1572880 | tf_op jit(solution)/shard_map/reduce_scatter | solution.py:241
  1365.3 486.9 %reduce-scatter.10.cloned.1.call-done = f32[64,5632]{1,0:T(8,128)} async-done(((f32[2048,5632]{1,0:T(8,128)}), f32[64,5632]{1,0:T(8,128)}) %reduce-scatter.10.cloned.1.call-update) | async-done | bytes 1441808 | tf_op jit(solution)/shard_map/reduce_scatter | solution.py:185
  1852.1 496.0 %reduce-scatter.12.cloned.1.call-done = f32[64,5632]{1,0:T(8,128)} async-done(((f32[2048,5632]{1,0:T(8,128)}), f32[64,5632]{1,0:T(8,128)}) %reduce-scatter.12.cloned.1.call-update) | async-done | bytes 1441808 | tf_op jit(solution)/shard_map/reduce_scatter | solution.py:186
  2348.1 495.8 %reduce-scatter.14.cloned.1.call-done = f32[176,2048]{1,0:T(8,128)} async-done(((f32[5632,2048]{1,0:T(8,128)}), f32[176,2048]{1,0:T(8,128)}) %reduce-scatter.14.cloned.1.call-update) | async-done | bytes 1441808 | tf_op jit(solution)/shard_map/reduce_scatter | solution.py:187
  (170 shorter events, 50.7 us)
Async XLA Ops:
  7.2 3.5 copy-start.27
  7.2 3.8 copy-start.28
  7.2 4.0 copy-start.29
  7.2 4.3 copy-start.30
  7.2 4.5 copy-start.31
  7.2 48.3 %copy-start.2 = (bf16[256,2048]{1,0:T(8,128)(2,1)S(1)}, bf16[256,2048]{1,0:T(8,128)(2,1)}, u32[]{:S(2)}) copy-start(bf16[256,2048]{1,0:T(8,128)(2,1)} %param.17) | copy-start | bytes 3145732
  7.2 162.6 %all-gather.6.cloned.1.call-start = ((), (), s32[]{:S(2)}) async-start(), calls=%async_computation.5 | async-start | bytes 25952256 | tf_op jit(solution)/shard_map/all_gather | solution.py:116
  8.0 240.3 %all-gather.8.cloned.1.call-start = ((), (), s32[]{:S(2)}) async-start(), calls=%async_computation.6 | async-start | bytes 8650752 | tf_op jit(solution)/shard_map/all_gather | solution.py:118
  8.7 47.5 %copy-start.26 = (s32[256]{0:T(256)S(1)}, s32[256]{0:T(256)}, u32[]{:S(2)}) copy-start(s32[256]{0:T(256)} %param.18) | copy-start | bytes 3076
  8.7 385.7 %all-gather.10.cloned.1.call-start = ((), (), s32[]{:S(2)}) async-start(), calls=%async_computation.7 | async-start | bytes 23789568 | tf_op jit(solution)/shard_map/all_gather | solution.py:144
  9.5 530.4 %all-gather.12.cloned.1.call-start = ((), (), s32[]{:S(2)}) async-start(), calls=%async_computation.8 | async-start | bytes 23789568 | tf_op jit(solution)/shard_map/all_gather | solution.py:145
  10.0 675.4 %all-gather.14.cloned.1.call-start = ((), (), s32[]{:S(2)}) async-start(), calls=%async_computation.9 | async-start | bytes 23789568 | tf_op jit(solution)/shard_map/all_gather | solution.py:146
  10.6 958.4 %reduce-scatter.8.cloned.1.call-start = ((), (), s32[]{:S(2)}) async-start(), calls=%async_computation.11 | async-start | bytes 17301504 | tf_op jit(solution)/shard_map/reduce_scatter | solution.py:243
  55.5 127.8 %copy-start.13 = (f32[2048]{0:T(1024)}, f32[2048]{0:T(1024)S(1)}, u32[]{:S(2)}) copy-start(f32[2048]{0:T(1024)S(1)} %convert_element_type.88) | copy-start | bytes 24580
  55.5 127.8 %copy-start.15 = (f32[2048]{0:T(1024)}, f32[2048]{0:T(1024)S(1)}, u32[]{:S(2)}) copy-start(f32[2048]{0:T(1024)S(1)} %convert_element_type.89) | copy-start | bytes 24580
  55.8 127.5 %copy-start.19 = (f32[256]{0:T(256)}, f32[256]{0:T(256)S(1)}, u32[]{:S(2)}) copy-start(f32[256]{0:T(256)S(1)} %broadcast_multiply_fusion.6) | copy-start | bytes 3076
  56.2 127.0 %copy-start.21 = (f32[256]{0:T(256)}, f32[256]{0:T(256)S(1)}, u32[]{:S(2)}) copy-start(f32[256]{0:T(256)S(1)} %add_rsqrt_fusion.1) | copy-start | bytes 3076
  57.0 138.3 %copy-start.17 = (f32[256,8]{0,1:T(8,128)}, f32[256,8]{0,1:T(8,128)S(1)}, u32[]{:S(2)}) copy-start(f32[256,8]{0,1:T(8,128)S(1)} %get-tuple-element.235) | copy-start | bytes 24580
  211.2 37.1 %copy-start.7 = (bf16[4,256,8,64]{1,3,2,0:T(8,128)(2,1)}, bf16[4,256,8,64]{1,3,2,0:T(8,128)(2,1)S(1)}, u32[]{:S(2)}) copy-start(bf16[4,256,8,64]{1,3,2,0:T(8,128)(2,1)S(1)} %get-tuple-element.445) | copy-start | bytes 3145732
  211.2 37.1 %copy-start.8 = (bf16[4,256,8,64]{1,3,2,0:T(8,128)(2,1)}, bf16[4,256,8,64]{1,3,2,0:T(8,128)(2,1)S(1)}, u32[]{:S(2)}) copy-start(bf16[4,256,8,64]{1,3,2,0:T(8,128)(2,1)S(1)} %get-tuple-element.446) | copy-start | bytes 3145732
  254.5 476.3 %copy-start = (f32[256,2048]{1,0:T(8,128)}, f32[256,2048]{1,0:T(8,128)S(1)}, u32[]{:S(2)}) copy-start(f32[256,2048]{1,0:T(8,128)S(1)} %get-tuple-element.239) | copy-start | bytes 6291460
  730.7 4.2 copy-start.10
  733.6 1.3 copy-start.3
  743.1 2.0 copy-start.4
  743.1 622.1 %reduce-scatter.6.cloned.1.call-start = ((), (), s32[]{:S(2)}) async-start(), calls=%async_computation.10 | async-start | bytes 51904512 | tf_op jit(solution)/shard_map/reduce_scatter | solution.py:241
  753.2 3.1 copy-start.6
  795.5 3.1 copy-start.18
  795.5 3.1 copy-start.23
  800.2 3.3 copy-start.14
  800.2 3.3 copy-start.16
  800.2 3.3 copy-start.20
  800.3 3.3 copy-start.22
  825.7 1.2 copy-start.9
  825.7 1026.4 %reduce-scatter.10.cloned.1.call-start = ((), (), s32[]{:S(2)}) async-start(), calls=%async_computation.12 | async-start | bytes 47579136 | tf_op jit(solution)/shard_map/reduce_scatter | solution.py:185
  847.2 1500.9 %reduce-scatter.12.cloned.1.call-start = ((), (), s32[]{:S(2)}) async-start(), calls=%async_computation.13 | async-start | bytes 47579136 | tf_op jit(solution)/shard_map/reduce_scatter | solution.py:186
  867.7 1.2 copy-start.12
  867.7 1976.2 %reduce-scatter.14.cloned.1.call-start = ((), (), s32[]{:S(2)}) async-start(), calls=%async_computation.14 | async-start | bytes 47579136 | tf_op jit(solution)/shard_map/reduce_scatter | solution.py:187
  889.2 14.2 copy-start.24
  889.2 14.2 copy-start.25
  889.2 57.9 %copy-start.5 = (f32[256,2048]{1,0:T(8,128)S(1)}, f32[256,2048]{1,0:T(8,128)}, u32[]{:S(2)}) copy-start(f32[256,2048]{1,0:T(8,128)} %copy-done.3) | copy-start | bytes 6291460
  947.2 4.3 copy-start.1
  947.2 5.2 copy-start.11
Sparse Core Ops, SparseCore 0:
  10.9 158.8 all-gather.5
  172.7 75.6 all-gather.7
  251.2 143.1 all-gather.9
  397.1 142.7 all-gather.11
  542.6 142.7 all-gather.13
  743.2 182.2 reduce-scatter.7
  932.5 432.6 reduce-scatter.5
  1368.1 483.9 reduce-scatter.9
  1855.0 493.0 reduce-scatter.11
  2350.8 493.0 reduce-scatter.13
where the time goes:
time: 2870 us; the launch traced here: 2850 us
  waiting for transfers between devices  2430 us (85%)
  matrix products  271 us (9%)
  blocking collectives  84.2 us (3%)
  local copies, waits for them, and re-layouts  29.5 us (1%)
    reduce_scatter x1, waiting for transfers between devices, shards(): lax.psum_scatter(grad_up_w, 'fsdp', scatter_dimension=0, tiled=True)  496 us
    reduce_scatter x1, waiting for transfers between devices, shards(): lax.psum_scatter(grad_down_w, 'fsdp', scatter_dimension=0, tiled=True)  496 us
    reduce_scatter x1, waiting for transfers between devices, shards(): lax.psum_scatter(grad_gate_w, 'fsdp', scatter_dimension=0, tiled=True)  487 us
    reduce_scatter x1, waiting for transfers between devices, shards(): lax.psum_scatter(grad_qkv_w, 'fsdp', scatter_dimension=0, tiled=True)  396 us
    all_gather x1, waiting for transfers between devices, shards(): lax.all_gather(gate_weight, 'fsdp', axis=0, tiled=True)  138 us
    all_gather x1, waiting for transfers between devices, shards(): lax.all_gather(down_weight, 'fsdp', axis=0, tiled=True)  133 us
    all_gather x1, waiting for transfers between devices, shards(): lax.all_gather(up_weight, 'fsdp', axis=0, tiled=True)  133 us
    all_gather x1, waiting for transfers between devices, shards(): lax.all_gather(qkv_weight, 'fsdp', axis=0, tiled=True)  113 us
  transfers between devices with their start and end apart: 10, of which 9 were waited for; matrix products, arithmetic and copies ran while one was open for 9% of the time, Pallas kernels for 0%

commit v1 on v0

--- a/solution.py
+++ b/solution.py
@@ -1,16 +1,197 @@
+import functools
+
 import jax
 import jax.numpy as jnp
 from jax import lax
+from jax.experimental import pallas as pl
+from jax.experimental.pallas import tpu as pltpu
 from jax.sharding import PartitionSpec as P
 
 D = 2048
 HEADS = 32
 HEAD_DIM = 64
 ROT = 16
-
-
 EPS = 1e-05
-HIGHEST = lax.Precision.HIGHEST
+TEAM = 8
+LOCAL = HEADS // TEAM
+MESH = pl.DeviceIdType.MESH
+BF16 = jnp.bfloat16
+F32 = jnp.float32
+ANY = pl.BlockSpec(memory_space=pl.ANY)
+VMEM = pl.BlockSpec(memory_space=pltpu.VMEM)
+
+
+def params(cid=None, limit=56):
+    extra = {} if cid is None else {"collective_id": cid, "has_side_effects": True}
+    return pltpu.CompilerParams(vmem_limit_bytes=limit * 1024 * 1024, **extra)
+
+
+def place():
+    me = lax.axis_index("fsdp")
+    mine = lax.rem(me, TEAM)
+    return mine, me - mine, mine // 2, lax.rem(mine, 2)
+
+
+def chip_at(chip, step):
+    along_x, along_y = lax.rem(chip, 2), chip // 2
+    if step & 1:
+        along_x = 1 - along_x
+    if step & 2:
+        along_y = 1 - along_y
+    return along_y * 2 + along_x
+
+
+def greet(devices):
+    barrier = pltpu.get_barrier_semaphore()
+    for device in devices:
+        pl.semaphore_signal(barrier, inc=1, device_id=(device,), device_id_type=MESH)
+    pl.semaphore_wait(barrier, len(devices))
+
+
+def remote(src, dst, send, recv, device):
+    return pltpu.make_async_remote_copy(
+        src_ref=src, dst_ref=dst, send_sem=send, recv_sem=recv, device_id=(device,), device_id_type=MESH
+    )
+
+
+def swap_kernel(x_ref, o_ref, own_sem, send_sem, recv_sem):
+    mine, base, _, _ = place()
+    greet([base + lax.rem(mine + k, TEAM) for k in range(1, TEAM)])
+    copies = []
+    for k in range(1, TEAM):
+        other = lax.rem(mine + k, TEAM)
+        copy = remote(x_ref.at[other], o_ref.at[mine], send_sem.at[k], recv_sem.at[k], base + other)
+        copy.start()
+        copies.append(copy)
+    own = pltpu.make_async_copy(x_ref.at[mine], o_ref.at[mine], own_sem)
+    own.start()
+    for copy in copies:
+        copy.wait()
+    own.wait()
+
+
+def team_swap(blocks, cid):
+    return pl.pallas_call(
+        swap_kernel,
+        out_shape=jax.ShapeDtypeStruct(blocks.shape, blocks.dtype),
+        in_specs=[ANY],
+        out_specs=ANY,
+        scratch_shapes=[pltpu.SemaphoreType.DMA] + [pltpu.SemaphoreType.DMA((TEAM,))] * 2,
+        compiler_params=params(cid),
+    )(blocks)
+
+
+def gather_kernel(x_ref, o_ref, own_sem, send_sem, recv_sem, pass_sem, passed_sem):
+    mine, base, chip, core = place()
+    sibling = base + chip * 2 + 1 - core
+    peers = {k: chip_at(chip, k) * 2 + core for k in (3, 1, 2)}
+    greet([base + peer for peer in peers.values()] + [sibling])
+    copies = {}
+    for k, peer in peers.items():
+        copies[k] = remote(x_ref, o_ref.at[mine], send_sem.at[k], recv_sem.at[k], base + peer)
+        copies[k].start()
+    copies[0] = remote(x_ref, o_ref.at[mine], send_sem.at[0], recv_sem.at[0], sibling)
+    copies[0].start()
+    own = pltpu.make_async_copy(x_ref, o_ref.at[mine], own_sem)
+    own.start()
+    passed = []
+    for k in (1, 2, 3):
+        copies[k].wait_recv()
+        block = o_ref.at[peers[k]]
+        copy = remote(block, block, pass_sem.at[k], passed_sem.at[k], sibling)
+        copy.start()
+        passed.append(copy)
+    for k in (1, 2, 3):
+        copies[k].wait_send()
+    copies[0].wait()
+    own.wait()
+    for copy in passed:
+        copy.wait()
+
+
+def team_gather(block, cid):
+    return pl.pallas_call(
+        gather_kernel,
+        out_shape=jax.ShapeDtypeStruct((TEAM,) + block.shape, block.dtype),
+        in_specs=[ANY],
+        out_specs=ANY,
+        scratch_shapes=[pltpu.SemaphoreType.DMA] + [pltpu.SemaphoreType.DMA((4,))] * 4,
+        compiler_params=params(cid),
+    )(block)
+
+
+def sum_kernel(x_ref, o_ref, own, near, far, own_sem, near_send, near_recv, far_send, far_recv):
+    mine, base, chip, core = place()
+    sibling = base + chip * 2 + 1 - core
+    chips = {k: chip_at(chip, k) for k in (3, 1, 2, 0)}
+    rows = own.shape[1]
+    loads = {}
+    for k, at in chips.items():
+        loads[k] = pltpu.make_async_copy(x_ref.at[at * 2 + core], own.at[k], own_sem.at[k])
+        loads[k].start()
+    greet([base + chips[k] * 2 + core for k in (3, 1, 2)] + [sibling])
+    nears = {}
+    for k, at in chips.items():
+        nears[k] = remote(x_ref.at[at * 2 + 1 - core], near.at[k], near_send.at[k], near_recv.at[k], sibling)
+        nears[k].start()
+    fars = {}
+    for k in (3, 1, 2):
+        loads[k].wait()
+        nears[k].wait_recv()
+
+        @pl.loop(0, rows // 16)
+        def _(i, k=k):
+            part = pl.ds(pl.multiple_of(i * 16, 16), 16)
+            own[k, part, :] = (own[k, part, :].astype(F32) + near[k, part, :].astype(F32)).astype(BF16)
+
+        fars[k] = remote(own.at[k], far.at[k - 1], far_send.at[k - 1], far_recv.at[k - 1], base + chips[k] * 2 + core)
+        fars[k].start()
+    loads[0].wait()
+    nears[0].wait_recv()
+    for k in (1, 2, 3):
+        fars[k].wait_recv()
+
+    @pl.loop(0, rows // 16)
+    def _(i):
+        part = pl.ds(pl.multiple_of(i * 16, 16), 16)
+        total = own[0, part, :].astype(F32) + near[0, part, :].astype(F32)
+        for k in range(3):
+            total = total + far[k, part, :].astype(F32)
+        o_ref[part, :] = total
+
+    for k in (3, 1, 2, 0):
+        nears[k].wait_send()
+    for k in (3, 1, 2):
+        fars[k].wait_send()
+
+
+def team_sum(blocks, cid):
+    _, rows, width = blocks.shape
+    return pl.pallas_call(
+        sum_kernel,
+        out_shape=jax.ShapeDtypeStruct((rows, width), F32),
+        in_specs=[ANY],
+        out_specs=VMEM,
+        scratch_shapes=[
+            pltpu.VMEM((4, rows, width), BF16),
+            pltpu.VMEM((4, rows, width), BF16),
+            pltpu.VMEM((3, rows, width), BF16),
+            pltpu.SemaphoreType.DMA((4,)),
+            pltpu.SemaphoreType.DMA((4,)),
+            pltpu.SemaphoreType.DMA((4,)),
+            pltpu.SemaphoreType.DMA((3,)),
+            pltpu.SemaphoreType.DMA((3,)),
+        ],
+        compiler_params=params(cid),
+    )(blocks)
+
+
+def dot(a, b, dims=((1,), (0,))):
+    return lax.dot_general(a, b, (dims, ((), ())), preferred_element_type=F32)
+
+
+NT = ((1,), (1,))
+TN = ((0,), (0,))
 
 
 def normalize(stream):
@@ -18,7 +199,7 @@
     centered = stream - average
     variance = jnp.mean(centered * centered, axis=-1, keepdims=True)
     inverse = lax.rsqrt(variance + EPS)
-    return (centered * inverse, inverse)
+    return centered * inverse, inverse
 
 
 def norm_back(grad_norm, normed, inverse):
@@ -26,6 +207,258 @@
         grad_norm
         - jnp.mean(grad_norm, axis=-1, keepdims=True)
         - normed * jnp.mean(grad_norm * normed, axis=-1, keepdims=True)
+    )
+
+
+def turn(heads, cosine, front, back, sign):
+    half, width = ROT // 2, heads.shape[-1]
+    moved = pltpu.roll(heads, width - half, 1) * front + pltpu.roll(heads, half, 1) * back
+    return heads * cosine + sign * moved
+
+
+def visible(start):
+    rows = lax.broadcasted_iota(jnp.int32, (start.shape[0],) * 2, 0)
+    columns = lax.broadcasted_iota(jnp.int32, (start.shape[0],) * 2, 1)
+    return (columns <= rows) & (columns >= start)
+
+
+def head_of(x, h):
+    lanes = lax.broadcasted_iota(jnp.int32, x.shape, 1)
+    return jnp.where((lanes >= h * HEAD_DIM) & (lanes < (h + 1) * HEAD_DIM), x, jnp.zeros_like(x))
+
+
+def soft(query, key, allowed):
+    scores = dot(query, key, NT) * 0.125
+    masked = jnp.where(allowed, scores, -1e30)
+    exponent = jnp.exp(masked - jnp.max(masked, axis=-1, keepdims=True))
+    return exponent / jnp.sum(exponent, axis=-1, keepdims=True)
+
+
+def attend_kernel(x_ref, gain_ref, bias_ref, w_ref, b_ref, wo_ref, tab_ref, start_ref, h_ref, qkv_ref, attn_ref, part_ref):
+    stream = x_ref[0].astype(F32)
+    normed, _ = normalize(stream)
+    h_one = (normed * gain_ref[...] + bias_ref[...]).astype(BF16)
+    h_ref[0] = h_one
+    qkv = dot(h_one, w_ref[...]) + b_ref[...]
+    width = LOCAL * HEAD_DIM
+    cosine, front, back = (jnp.concatenate([tab_ref[0, i]] * (width // 128), axis=1) for i in range(3))
+    query = turn(qkv[:, :width], cosine, front, back, 1.0).astype(BF16)
+    key = turn(qkv[:, width : 2 * width], cosine, front, back, 1.0).astype(BF16)
+    value = qkv[:, 2 * width :].astype(BF16)
+    qkv_ref[0, :, :width] = query
+    qkv_ref[0, :, width : 2 * width] = key
+    qkv_ref[0, :, 2 * width :] = value
+    allowed = visible(start_ref[0])
+    mixed = jnp.zeros((query.shape[0], width), F32)
+    for h in range(LOCAL):
+        probs = soft(head_of(query, h), key, allowed).astype(BF16)
+        mixed = mixed + dot(probs, head_of(value, h))
+    attn_low = mixed.astype(BF16)
+    attn_ref[0] = attn_low
+    part_ref[0] = dot(attn_low, wo_ref[...]).astype(BF16)
+
+
+def per_seq(*shape):
+    return pl.BlockSpec((1,) + shape, lambda s: (s,) + (0,) * len(shape))
+
+
+def whole(*shape):
+    return pl.BlockSpec(shape, lambda s: (0,) * len(shape))
+
+
+def attend(x_all, gain, bias, w_qkv, b_qkv, w_out, tables, start):
+    seqs, rows, _ = x_all.shape
+    width = LOCAL * HEAD_DIM
+    return pl.pallas_call(
+        attend_kernel,
+        grid=(seqs,),
+        in_specs=[
+            per_seq(rows, D),
+            whole(1, D),
+            whole(1, D),
+            whole(D, 3 * width),
+            whole(1, 3 * width),
+            whole(width, D),
+            per_seq(3, rows, 128),
+            per_seq(rows, 1),
+        ],
+        out_specs=[per_seq(rows, D), per_seq(rows, 3 * width), per_seq(rows, width), per_seq(rows, D)],
+        out_shape=[
+            jax.ShapeDtypeStruct((seqs, rows, D), BF16),
+            jax.ShapeDtypeStruct((seqs, rows, 3 * width), BF16),
+            jax.ShapeDtypeStruct((seqs, rows, width), BF16),
+            jax.ShapeDtypeStruct((seqs, rows, D), BF16),
+        ],
+        compiler_params=params(),
+    )(x_all, gain, bias, w_qkv, b_qkv, w_out, tables, start)
+
+
+def attend_back_kernel(g_ref, wo_ref, w_ref, qkv_ref, tab_ref, start_ref, gqkv_ref, part_ref, gb_ref):
+    width = LOCAL * HEAD_DIM
+    grad_att = dot(g_ref[0], wo_ref[...], NT).astype(BF16)
+    query, key, value = (qkv_ref[0, :, i * width : (i + 1) * width] for i in range(3))
+    allowed = visible(start_ref[0])
+    zero = jnp.zeros((query.shape[0], width), F32)
+    grad_query, grad_key, grad_value = zero, zero, zero
+    for h in range(LOCAL):
+        query_h, key_h, grad_h = head_of(query, h), head_of(key, h), head_of(grad_att, h)
+        probs = soft(query_h, key, allowed)
+        low = probs.astype(BF16)
+        grad_probs = dot(grad_h, value, NT)
+        delta = jnp.sum(low.astype(F32) * grad_probs, axis=-1, keepdims=True)
+        grad_scores = (probs * (grad_probs - delta)).astype(BF16)
+        grad_value = grad_value + dot(low, grad_h, TN)
+        grad_query = grad_query + dot(grad_scores, key_h)
+        grad_key = grad_key + dot(grad_scores, query_h, TN)
+    cosine, front, back = (jnp.concatenate([tab_ref[0, i]] * (width // 128), axis=1) for i in range(3))
+    grad_query = turn(grad_query * 0.125, cosine, front, back, -1.0)
+    grad_key = turn(grad_key * 0.125, cosine, front, back, -1.0)
+    grad_qkv = jnp.concatenate([grad_query, grad_key, grad_value], axis=1).astype(BF16)
+    gqkv_ref[0] = grad_qkv
+    gb_ref[0] = jnp.sum(grad_qkv.astype(F32), axis=0, keepdims=True)
+    part_ref[0] = dot(grad_qkv, w_ref[...], NT).astype(BF16)
+
+
+def attend_back(g_all, w_out, w_qkv, qkv, tables, start):
+    seqs, rows, _ = g_all.shape
+    width = LOCAL * HEAD_DIM
+    return pl.pallas_call(
+        attend_back_kernel,
+        grid=(seqs,),
+        in_specs=[
+            per_seq(rows, D),
+            whole(width, D),
+            whole(D, 3 * width),
+            per_seq(rows, 3 * width),
+            per_seq(3, rows, 128),
+            per_seq(rows, 1),
+        ],
+        out_specs=[per_seq(rows, 3 * width), per_seq(rows, D), per_seq(1, 3 * width)],
+        out_shape=[
+            jax.ShapeDtypeStruct((seqs, rows, 3 * width), BF16),
+            jax.ShapeDtypeStruct((seqs, rows, D), BF16),
+            jax.ShapeDtypeStruct((seqs, 1, 3 * width), F32),
+        ],
+        compiler_params=params(),
+    )(g_all, w_out, w_qkv, qkv, tables, start)
+
+
+def team_shards(
+    inputs, positions, norm1_gain, norm1_bias, qkv_weight, qkv_bias, out_weight, norm2_gain, norm2_bias,
+    gate_weight, up_weight, down_weight, out_grad,
+):
+    n = lax.axis_size("fsdp")
+    planes = n // TEAM
+    rows = inputs.shape[0]
+    tokens = TEAM * rows
+    depth = qkv_weight.shape[0]
+    ff = down_weight.shape[0]
+    width = LOCAL * HEAD_DIM
+    lines = [[z * TEAM + i for z in range(planes)] for i in range(TEAM)]
+    mine = lax.rem(lax.axis_index("fsdp"), TEAM)
+
+    def line_gather(x):
+        return lax.all_gather(x, "fsdp", axis=0, tiled=True, axis_index_groups=lines)
+
+    def line_sum(x):
+        return lax.psum_scatter(x, "fsdp", scatter_dimension=0, tiled=True, axis_index_groups=lines)
+
+    w_out = line_gather(out_weight)
+    vectors = jnp.concatenate([norm1_gain, norm1_bias, norm2_gain, norm2_bias, qkv_bias])
+    extra = jnp.zeros((16, 3 * width), BF16)
+    extra = extra.at[0, : vectors.shape[0]].set(vectors).at[1, :rows].set(positions.astype(BF16))
+    pieces = qkv_weight.reshape(depth, 3, planes, TEAM, HEAD_DIM).transpose(3, 0, 1, 2, 4).reshape(TEAM, depth, 3 * width)
+    pieces = jnp.concatenate([pieces, jnp.broadcast_to(extra, (TEAM,) + extra.shape)], axis=1)
+    pieces = team_swap(pieces, 0)
+    places = pieces[:, depth + 1, :rows].astype(F32)
+    gathered = line_gather(pieces).reshape(n, depth + 16, 3 * width)
+    w_qkv = gathered[:, :depth].reshape(D, 3 * width)
+    vectors = gathered[:, depth, : vectors.shape[0]].astype(F32)
+    gain_one, bias_one, gain_two, bias_two = (vectors[:, i * depth : (i + 1) * depth].reshape(1, D) for i in range(4))
+    b_qkv = vectors[:, 4 * depth :].reshape(3, planes, TEAM, HEAD_DIM)
+    b_qkv = lax.dynamic_index_in_dim(b_qkv, mine, 2, keepdims=False).reshape(1, 3 * width)
+
+    both = jnp.stack([w.reshape(depth, planes, TEAM, ff) for w in (gate_weight, up_weight)], axis=1)
+    both = both.transpose(3, 0, 1, 2, 4).reshape(TEAM, depth, 2 * planes * ff)
+    both = team_swap(both, 1)
+    w_both = line_gather(both.reshape(TEAM * depth, 2 * planes * ff))
+    w_down = line_gather(down_weight)
+    x_all = team_gather(inputs, 2)
+    g_all = team_gather(out_grad, 3)
+
+    half = ROT // 2
+    frequency = 10000.0 ** (-jnp.arange(half, dtype=F32) / half)
+    angles = places[:, :, None] * frequency
+    cosine, sine = jnp.cos(angles), jnp.sin(angles)
+    ones, zeros = (jnp.full(angles.shape[:2] + (HEAD_DIM - ROT,), v, F32) for v in (1.0, 0.0))
+    none = jnp.zeros_like(sine)
+    tables = jnp.stack(
+        [
+            jnp.concatenate([a, b, c] * (128 // HEAD_DIM), axis=-1)
+            for a, b, c in ((cosine, cosine, ones), (-sine, none, zeros), (none, sine, zeros))
+        ],
+        axis=1,
+    )
+    start = (jnp.arange(rows, dtype=jnp.int32)[None] - places.astype(jnp.int32))[:, :, None]
+
+    h_one, qkv, attn_low, part = attend(x_all, gain_one, bias_one, w_qkv, b_qkv, w_out, tables, start)
+    stream = inputs.astype(F32)
+    resid = stream + team_sum(part, 4)
+    normed_two, inverse_two = normalize(resid)
+    h_two = team_gather((normed_two * gain_two + bias_two).astype(BF16), 5).reshape(tokens, D)
+    g_rows = g_all.reshape(tokens, D)
+    pre = dot(h_two, w_both)
+    gate_pre, up_pre = pre[:, : planes * ff], pre[:, planes * ff :]
+    sigmoid = jax.nn.sigmoid(gate_pre)
+    silu = gate_pre * sigmoid
+    hidden = (silu * up_pre).astype(BF16)
+    grad_down = line_sum(dot(hidden, g_rows, TN).astype(BF16))
+    grad_hidden = dot(g_rows, w_down, NT)
+    grad_gate = (grad_hidden * up_pre * sigmoid * (1.0 + gate_pre * (1.0 - sigmoid))).astype(BF16)
+    grad_up = (grad_hidden * silu).astype(BF16)
+    grad_both = jnp.concatenate([grad_gate, grad_up], axis=1)
+    grad_w_both = line_sum(dot(h_two, grad_both, TN).astype(BF16))
+    part = dot(grad_both, w_both, NT).astype(BF16).reshape(TEAM, rows, D)
+    grad_htwo = team_sum(part, 6)
+    grad_resid = out_grad.astype(F32) + norm_back(grad_htwo * gain_two, normed_two, inverse_two)
+    branch = team_gather(grad_resid.astype(BF16), 7)
+    grad_qkv, part, grad_bias = attend_back(branch, w_out, w_qkv, qkv, tables, start)
+    grad_qkv = grad_qkv.reshape(tokens, 3 * width)
+    grad_w_qkv = line_sum(dot(h_one.reshape(tokens, D), grad_qkv, TN).astype(BF16))
+    grad_out = line_sum(dot(attn_low.reshape(tokens, width), branch.reshape(tokens, D), TN).astype(BF16))
+    grad_hone = team_sum(part, 8)
+    normed_one, inverse_one = normalize(stream)
+    input_grad = grad_resid + norm_back(grad_hone * gain_one, normed_one, inverse_one)
+
+    hidden, _ = lax.optimization_barrier((hidden, grad_hone))
+    part = dot(hidden, w_down).astype(BF16).reshape(TEAM, rows, D)
+    block_out = (resid + team_sum(part, 9)).astype(BF16)
+
+    bias = jnp.zeros((3, planes, TEAM, HEAD_DIM), F32)
+    bias = lax.dynamic_update_slice(
+        bias, jnp.sum(grad_bias, axis=0).reshape(3, planes, 1, HEAD_DIM), (0, 0, mine, 0)
+    ).reshape(n, -1)
+    sums = [jnp.sum(v, axis=0).reshape(n, depth) for v in (grad_hone * normed_one, grad_hone, grad_htwo * normed_two, grad_htwo)]
+    sums = lax.psum_scatter(jnp.concatenate(sums + [bias], axis=1), "fsdp", scatter_dimension=0, tiled=True)[0]
+    sums = [sums[i * depth : (i + 1) * depth] for i in range(4)] + [sums[4 * depth :]]
+
+    grad_w_both = team_swap(grad_w_both.reshape(TEAM, depth, 2 * planes * ff), 10)
+    grad_w_both = grad_w_both.reshape(TEAM, depth, 2, planes, ff).transpose(2, 1, 3, 0, 4).reshape(2, depth, -1).astype(F32)
+    grad_w_qkv = team_swap(grad_w_qkv.reshape(TEAM, depth, 3 * width), 11)
+    grad_w_qkv = grad_w_qkv.reshape(TEAM, depth, 3, planes, HEAD_DIM).transpose(1, 2, 3, 0, 4).reshape(depth, -1).astype(F32)
+    return (
+        block_out,
+        input_grad,
+        sums[0],
+        sums[1],
+        grad_w_qkv,
+        sums[4],
+        grad_out.astype(F32),
+        sums[2],
+        sums[3],
+        grad_w_both[0],
+        grad_w_both[1],
+        grad_down.astype(F32),
     )
 
 
@@ -57,7 +490,7 @@
     return jnp.moveaxis(grouped, 0, 1).reshape(grouped.shape[1], HEADS, HEAD_DIM)
 
 
-def attend_group(block_items, allowed):
+def plain_group(block_items, allowed):
     query_part, key_part, value_part = block_items
     scores = (
         jnp.einsum("qhd,khd->hqk", query_part, key_part, preferred_element_type=jnp.float32) * 0.125
@@ -73,17 +506,17 @@
     return (mixed_part, (row_max + jnp.log(row_total))[..., 0])
 
 
-def attend_back(block_items, allowed):
+def plain_back(block_items, allowed):
     query_part, key_part, value_part, grad_part, row_delta, log_total = block_items
     scores = (
         jnp.einsum("qhd,khd->hqk", query_part, key_part, preferred_element_type=jnp.float32) * 0.125
     )
     soft_probs = jnp.where(allowed[None], jnp.exp(scores - log_total[..., None]), 0.0)
     grad_probs = jnp.einsum(
-        "qhd,khd->hqk", grad_part, value_part.astype(jnp.float32), precision=HIGHEST
+        "qhd,khd->hqk", grad_part, value_part.astype(jnp.float32), precision=lax.Precision.HIGHEST
     )
     rounded_probs = soft_probs.astype(jnp.bfloat16).astype(jnp.float32)
-    grad_value = jnp.einsum("hqk,qhd->khd", rounded_probs, grad_part, precision=HIGHEST)
+    grad_value = jnp.einsum("hqk,qhd->khd", rounded_probs, grad_part, precision=lax.Precision.HIGHEST)
     grad_scores = (soft_probs * (grad_probs - row_delta[..., None])).astype(jnp.bfloat16)
     grad_query = 0.125 * jnp.einsum(
         "hqk,khd->qhd", grad_scores, key_part, preferred_element_type=jnp.float32
@@ -132,7 +565,7 @@
         token_index[None, :] >= (token_index - positions)[:, None]
     )
     mixed_grouped, log_grouped = lax.map(
-        lambda block_items: attend_group(block_items, allowed),
+        lambda block_items: plain_group(block_items, allowed),
         (by_groups(query_low), by_groups(key_all), by_groups(value_all)),
     )
     mixed_heads = from_groups(mixed_grouped)
@@ -202,7 +635,7 @@
         1, 2, 0
     )
     query_grouped, key_grouped, value_grouped = lax.map(
-        lambda block_items: attend_back(block_items, allowed),
+        lambda block_items: plain_back(block_items, allowed),
         (
             by_groups(query_low),
             by_groups(key_all),
@@ -259,37 +692,13 @@
 
 
 def solution(mesh):
+    devices = mesh.shape["fsdp"]
+    rows, columns = P("fsdp", None), P("fsdp")
+    body = team_shards if devices % TEAM == 0 and D == devices * HEAD_DIM else shards
     return jax.shard_map(
-        shards,
+        body,
         mesh=mesh,
-        in_specs=(
-            P("fsdp", None),
-            P("fsdp"),
-            P("fsdp"),
-            P("fsdp"),
-            P("fsdp", None),
-            P("fsdp"),
-            P("fsdp", None),
-            P("fsdp"),
-            P("fsdp"),
-            P("fsdp", None),
-            P("fsdp", None),
-            P("fsdp", None),
-            P("fsdp", None),
-        ),
-        out_specs=(
-            P("fsdp", None),
-            P("fsdp", None),
-            P("fsdp"),
-            P("fsdp"),
-            P("fsdp", None),
-            P("fsdp"),
-            P("fsdp", None),
-            P("fsdp"),
-            P("fsdp"),
-            P("fsdp", None),
-            P("fsdp", None),
-            P("fsdp", None),
-        ),
+        in_specs=(rows, columns, columns, columns, rows, columns, rows, columns, columns, rows, rows, rows, rows),
+        out_specs=(rows, rows, columns, columns, rows, columns, rows, columns, columns, rows, rows, rows),
         check_vma=False,
     )

time: 2870 us -> 855 us (0.30)
  waiting for transfers between devices: 2430 us -> 1.35 us
  Pallas kernels: 0 us -> 566 us
  matrix products: 271 us -> 114 us
  blocking collectives: 84.2 us -> 45.4 us
  local copies, waits for them, and re-layouts: 29.5 us -> 64.8 us
    reduce_scatter x5 -> x4, waiting for transfers between devices: 1870 us -> 0.01 us  [line_sum(): lax.psum_scatter(x, 'fsdp', scatter_dimension=0, tiled=True, axis_index_g...]
    pallas_call x0 -> x14, Pallas kernels: none -> 566 us  [the longest x4 218 us: team_gather(): pl.pallas_call(gather_kernel, out_shape=jax.ShapeDtypeStruct((TEAM,) + bl...]
    all_gather x5 -> x4, waiting for transfers between devices: 550 us -> 0.03 us  [line_gather(): lax.all_gather(x, 'fsdp', axis=0, tiled=True, axis_index_groups=lines)]
    dot_general x43 -> x8, matrix products: 271 us -> 114 us  [dot(): return lax.dot_general(a, b, (dims, ((), ())), preferred_element_type=F32)]
    unnamed x2 -> x1, blocking collectives: 84.2 us -> 45.4 us
  transfers between devices with their start and end apart: 10 -> 8, of which waited for: 9 -> 0; matrix products, arithmetic and copies ran while one was open for 9% -> 17% of each run, Pallas kernels for 0% -> 50%
where the time goes in v1:
time: 855 us; the launch traced here: 844 us
  Pallas kernels  566 us (66%)
  matrix products  114 us (13%)
  local copies, waits for them, and re-layouts  64.8 us (8%)
  blocking collectives  45.4 us (5%)
  other arithmetic  36.6 us (4%)
  between operations  15 us (2%)
    pallas_call x4, Pallas kernels, team_gather(): pl.pallas_call(gather_kernel, out_shape=jax.ShapeDtypeStruct((TEAM,) + bl...  218 us
    pallas_call x4, Pallas kernels, team_sum(): pl.pallas_call(sum_kernel, out_shape=jax.ShapeDtypeStruct((rows, width),...  217 us
    dot_general x8, matrix products, dot(): return lax.dot_general(a, b, (dims, ((), ())), preferred_element_type=F32)  114 us
    pallas_call x4, Pallas kernels, team_swap(): pl.pallas_call(swap_kernel, out_shape=jax.ShapeDtypeStruct(blocks.shape,...  65.7 us
    unnamed x1, blocking collectives  45.4 us
    pallas_call x1, Pallas kernels, attend_back(): pl.pallas_call(attend_back_kernel, grid=(seqs,), in_specs=[per_seq(rows,...  34.6 us
    pallas_call x1, Pallas kernels, attend(): pl.pallas_call(attend_kernel, grid=(seqs,), in_specs=[per_seq(rows, D), w...  31 us
  transfers between devices with their start and end apart: 8, of which 0 were waited for; matrix products, arithmetic and copies ran while one was open for 17% of the time, Pallas kernels for 50%

profile of v1, /device:TPU:0, one launch (start us, length us, event | category | flops | bytes accessed | tf_op | source)
XLA Modules:
  0.0 843.7 jit_solution(18088065201138825327)
XLA Ops:
  7.2 2.5 reshape.255
  12.9 15.4 %shard_map.221 = bf16[8,80,768]{2,1,0:T(8,128)(2,1)} custom-call(bf16[8,80,768]{2,1,0:T(8,128)(2,1)} %pad_maximum_fusion.4.x_ref), custom_call_target="tpu_custom_call" | custom-call | tf_op jit(solution)/shard_map/pallas_call | solution.py:74
  29.2 2.0 stack_reshape.6
  31.6 2.0 stack_reshape.7
  35.6 3.2 reshape.265.x_ref
  38.8 19.3 %shard_map.225 = bf16[8,64,1408]{2,1,0:T(8,128)(2,1)} custom-call(bf16[8,64,1408]{2,1,0:T(8,128)(2,1)} %reshape.265.x_ref), custom_call_target="tpu_custom_call" | custom-call | tf_op jit(solution)/shard_map/pallas_call | solution.py:74
  60.5 54.9 %shard_map.220.x_ref = bf16[8,256,2048]{2,1,0:T(8,128)(2,1)} custom-call(bf16[256,2048]{1,0:T(8,128)(2,1)} %x_ref.2), custom_call_target="tpu_custom_call" | custom-call | tf_op jit(solution)/shard_map/pallas_call | solution.py:113
  115.7 5.5 multiply_cosine_fusion
  121.4 4.4 concatenate.28
  125.7 4.4 concatenate.29
  131.4 54.9 %shard_map.226 = bf16[8,256,2048]{2,1,0:T(8,128)(2,1)} custom-call(bf16[256,2048]{1,0:T(8,128)(2,1)} %x_ref.3), custom_call_target="tpu_custom_call" | custom-call | tf_op jit(solution)/shard_map/pallas_call | solution.py:113
  186.4 3.0 concatenate.27
  189.4 3.5 pad_maximum_fusion.3.tab_ref
  196.1 3.9 slice.128
  200.0 31.0 %shard_map.222 = (bf16[8,256,2048]{2,1,0:T(8,128)(2,1)}, bf16[8,256,768]{2,1,0:T(8,128)(2,1)}, bf16[8,256,256]{2,1,0:T(8,128)(2,1)}, bf16[8,256,2048]{2,1,0:T(8,128)(2,1)}) custom-call(bf16[8,256,2048]{2,1,0:T(8,128)(2,1)} %shard_map.220.x_ref, f32[1,2048]{1,0:T(1,128)} %reshape.259.gain_ref, f32[1,2048]{1,0:T(1,128)} %reshape.260.bias_ref, ...), custom_call_target="tpu_custom_call" | custom-call | tf_op jit(solution)/shard_map/pallas_call | solution.py:272
  231.0 54.1 %shard_map.223 = f32[256,2048]{1,0:T(8,128)} custom-call(bf16[8,256,2048]{2,1,0:T(8,128)(2,1)} %get-tuple-element.44.x_ref), custom_call_target="tpu_custom_call" | custom-call | tf_op jit(solution)/shard_map/pallas_call | solution.py:170
  285.2 2.2 fusion.17
  289.4 53.9 %shard_map.224 = bf16[8,256,2048]{2,1,0:T(8,128)(2,1)} custom-call(bf16[256,2048]{1,0:T(8,128)(2,1)} %add_convert_fusion.1.x_ref), custom_call_target="tpu_custom_call" | custom-call | tf_op jit(solution)/shard_map/pallas_call | solution.py:113
  343.3 19.3 %fusion.20 = f32[2048,1408]{0,1:T(8,128)} fusion(bf16[2048,2048]{1,0:T(8,128)(2,1)} %bitcast.74, bf16[2048,1408]{1,0:T(8,128)(2,1)} %all-gather.9.cloned.1.call-done), kind=kOutput, calls=%fused_computation.69 | convolution fusion | flops 11811160064 | bytes 25690112 | tf_op jit(solution)/shard_map/dot_general | solution.py:190
  362.6 17.4 %multiply_convert_fusion.1 = (bf16[2048,704]{0,1:T(8,128)(2,1)}, bf16[2048,704]{0,1:T(8,128)(2,1)}, bf16[2048,704]{0,1:T(8,128)(2,1)}) fusion(f32[2048,1408]{0,1:T(8,128)} %fusion.20, bf16[2048,2048]{1,0:T(8,128)(2,1)} %bitcast.72, bf16[704,2048]{1,0:T(8,128)(2,1)} %all-gather.11.cloned.1.call-done), kind=kOutput, calls=%fused_computation.6 | convolution fusion | flops 5927206912 | bytes 31457280 | tf_op jit(solution)/shard_map/dot_general | solution.py:190
  380.0 17.5 %convolution_convert_fusion.1 = bf16[2048,2048]{1,0:T(8,128)(2,1)} fusion(bf16[2048,1408]{1,0:T(8,128)(2,1)S(1)} %copy-done.21, bf16[2048,704]{0,1:T(8,128)(2,1)} %get-tuple-element.65, bf16[2048,704]{0,1:T(8,128)(2,1)} %get-tuple-element.64), kind=kOutput, calls=%fused_computation.1 | convolution fusion | flops 11826888704 | bytes 19922944 | tf_op jit(solution)/shard_map/dot_general | solution.py:190
  397.5 54.1 %shard_map.227 = f32[256,2048]{1,0:T(8,128)} custom-call(bf16[8,256,2048]{2,1,0:T(8,128)(2,1)} %bitcast.71), custom_call_target="tpu_custom_call" | custom-call | tf_op jit(solution)/shard_map/pallas_call | solution.py:170
  451.6 2.6 multiply_reduce_fusion
  454.3 2.6 fusion.16
  456.9 54.6 %shard_map.228.g_ref = bf16[8,256,2048]{2,1,0:T(8,128)(2,1)} custom-call(bf16[256,2048]{1,0:T(8,128)(2,1)} %get-tuple-element.60.x_ref), custom_call_target="tpu_custom_call" | custom-call | tf_op jit(solution)/shard_map/pallas_call | solution.py:113
  511.5 6.7 fusion.1
  518.3 10.8 %convolution_convert_fusion.3 = bf16[704,2048]{1,0:T(8,128)(2,1)} fusion(bf16[2048,704]{0,1:T(8,128)(2,1)} %get-tuple-element.47, bf16[2048,2048]{1,0:T(8,128)(2,1)} %bitcast.73), kind=kOutput, calls=%fused_computation.10 | convolution fusion | flops 5907021824 | bytes 14155776 | tf_op jit(solution)/shard_map/dot_general | solution.py:190
  529.1 34.6 %shard_map.229 = (bf16[8,256,768]{2,1,0:T(8,128)(2,1)}, bf16[8,256,2048]{2,1,0:T(8,128)(2,1)}, f32[8,1,768]{2,1,0:T(1,128)}) custom-call(bf16[8,256,2048]{2,1,0:T(8,128)(2,1)} %shard_map.228.g_ref, bf16[256,2048]{1,0:T(8,128)(2,1)} %all-gather.7.cloned.1.call-done.wo_ref, bf16[2048,768]{1,0:T(8,128)(2,1)} %bitcast.67, ...), custom_call_target="tpu_custom_call" | custom-call | tf_op jit(solution)/shard_map/pallas_call | solution.py:325
  563.7 11.5 %bitcast_convert_fusion = bf16[2048,768]{1,0:T(8,128)(2,1)} fusion(bf16[8,256,2048]{2,1,0:T(8,128)(2,1)} %get-tuple-element.49, bf16[8,256,768]{2,1,0:T(8,128)(2,1)} %get-tuple-element.50), kind=kOutput, calls=%fused_computation.3 | convolution fusion | flops 6444023808 | bytes 14680064 | tf_op jit(solution)/shard_map/dot_general | solution.py:190
  575.2 19.4 %convolution_convert_fusion.2 = bf16[2048,1408]{1,0:T(8,128)(2,1)} fusion(bf16[2048,2048]{1,0:T(8,128)(2,1)} %bitcast.75, bf16[2048,704]{0,1:T(8,128)(2,1)} %get-tuple-element.65, bf16[2048,704]{0,1:T(8,128)(2,1)} %get-tuple-element.64), kind=kOutput, calls=%fused_computation.2 | convolution fusion | flops 11825577984 | bytes 19922944 | tf_op jit(solution)/shard_map/dot_general | solution.py:190
  595.4 54.2 %shard_map.230 = f32[256,2048]{1,0:T(8,128)} custom-call(bf16[8,256,2048]{2,1,0:T(8,128)(2,1)} %get-tuple-element.46.x_ref), custom_call_target="tpu_custom_call" | custom-call | tf_op jit(solution)/shard_map/pallas_call | solution.py:170
  649.7 2.6 fusion.11
  652.7 11.4 %convolution_convert_fusion = bf16[2048,2048]{1,0:T(8,128)(2,1)} fusion(bf16[2048,704]{0,1:T(8,128)(2,1)} %get-tuple-element.47, bf16[704,2048]{1,0:T(8,128)(2,1)} %all-gather.11.cloned.1.call-done), kind=kOutput, calls=%fused_computation | convolution fusion | flops 5909774336 | bytes 14155776 | tf_op jit(solution)/shard_map/dot_general | solution.py:190
  664.2 54.1 %shard_map.231 = f32[256,2048]{1,0:T(8,128)} custom-call(bf16[8,256,2048]{2,1,0:T(8,128)(2,1)} %bitcast.70), custom_call_target="tpu_custom_call" | custom-call | tf_op jit(solution)/shard_map/pallas_call | solution.py:170
  718.4 45.4 %all-reduce.1 = f32[32,448]{1,0:T(8,128)S(1)} all-reduce(f32[32,448]{1,0:T(8,128)S(1)} %concatenate.31), channel_id=2, replica_groups=mesh['fsdp'=32] {'fsdp'}, use_global_device_ids=true, to_apply=%region_13.14.clone | all-reduce | flops 14336 | bytes 114688
  765.1 2.8 add_convert_fusion
  767.9 2.1 fusion.10
  771.8 2.4 convert_element_type.141
  774.1 12.0 %shard_map.232 = bf16[8,64,768]{2,1,0:T(8,128)(2,1)} custom-call(bf16[8,64,768]{2,1,0:T(8,128)(2,1)} %bitcast.82), custom_call_target="tpu_custom_call" | custom-call | tf_op jit(solution)/shard_map/pallas_call | solution.py:74
  786.2 3.7 reshape.282
  789.9 3.7 copy.54
  793.6 1.9 reshape.280
  795.5 18.9 %shard_map.233 = bf16[8,64,1408]{2,1,0:T(8,128)(2,1)} custom-call(bf16[8,64,1408]{2,1,0:T(8,128)(2,1)} %bitcast.81), custom_call_target="tpu_custom_call" | custom-call | tf_op jit(solution)/shard_map/pallas_call | solution.py:74
  814.5 8.6 %reshape.281 = f32[8,64,2,4,176]{4,3,2,1,0:T(4,128)} reshape(bf16[8,64,1408]{2,1,0:T(8,128)(2,1)} %shard_map.233) | data formatting | bytes 4325376 | tf_op jit(solution)/shard_map/convert_element_type | solution.py:446
  823.1 4.3 fusion.18
  828.6 2.6 squeeze.12
  831.2 2.8 copy.56
  834.0 2.6 squeeze.6
  (127 shorter events, 21.3 us)
Async XLA Ops:
  7.2 185.8 %all-gather.5.cloned.1.call-start = ((), (), s32[]{:S(2)}) async-start(), calls=%async_computation.4 | async-start | bytes 4915200 | tf_op jit(solution)/shard_map/all_gather | solution.py:361
  9.7 1.6 copy-start.16
  9.8 1.6 copy-start.17
  9.8 1.6 copy-start.18
  9.8 1.6 copy-start.19
  9.8 1.6 copy-start.20
  9.8 1.8 copy-start.22
  11.4 17.7 %copy-start.9 = (bf16[64,5632]{1,0:T(8,128)(2,1)S(1)}, bf16[64,5632]{1,0:T(8,128)(2,1)}, u32[]{:S(2)}) copy-start(bf16[64,5632]{1,0:T(8,128)(2,1)} %param.26) | copy-start | bytes 2162692
  28.3 3.3 copy-start.10
  28.4 171.7 %all-gather.7.cloned.1.call-start = ((), (), s32[]{:S(2)}) async-start(), calls=%async_computation.5 | async-start | bytes 1310720 | tf_op jit(solution)/shard_map/all_gather | solution.py:361
  29.1 314.2 %all-gather.9.cloned.1.call-start = ((), (), s32[]{:S(2)}) async-start(), calls=%async_computation.6 | async-start | bytes 7208960 | tf_op jit(solution)/shard_map/all_gather | solution.py:361
  58.1 304.5 %all-gather.11.cloned.1.call-start = ((), (), s32[]{:S(2)}) async-start(), calls=%async_computation.7 | async-start | bytes 3604480 | tf_op jit(solution)/shard_map/all_gather | solution.py:361
  58.6 711.3 %reduce-scatter.7.cloned.1.call-start = ((), (), s32[]{:S(2)}) async-start(), calls=%async_computation.9 | async-start | bytes 1310720 | tf_op jit(solution)/shard_map/reduce_scatter | solution.py:364
  60.5 55.0 %copy-start = (bf16[256,2048]{1,0:T(8,128)(2,1)S(1)}, bf16[256,2048]{1,0:T(8,128)(2,1)}, u32[]{:S(2)}) copy-start(bf16[256,2048]{1,0:T(8,128)(2,1)} %x_ref.2) | copy-start | bytes 3145732
  131.4 153.8 %copy-start.14 = (f32[256]{0:T(256)}, f32[256]{0:T(256)S(1)}, u32[]{:S(2)}) copy-start(f32[256]{0:T(256)S(1)} %broadcast_multiply_fusion.2) | copy-start | bytes 3076
  186.4 3.0 copy-start.7
  194.0 6.0 copy-start.11
  231.0 54.2 %copy-start.1 = (bf16[256,2048]{1,0:T(8,128)(2,1)S(1)}, bf16[256,2048]{1,0:T(8,128)(2,1)}, u32[]{:S(2)}) copy-start(bf16[256,2048]{1,0:T(8,128)(2,1)} %x_ref.2) | copy-start | bytes 3145732
  362.6 17.4 %copy-start.21 = (bf16[2048,1408]{1,0:T(8,128)(2,1)S(1)}, bf16[2048,1408]{1,0:T(8,128)(2,1)}, u32[]{:S(2)}) copy-start(bf16[2048,1408]{1,0:T(8,128)(2,1)} %all-gather.9.cloned.1.call-done) | copy-start | bytes 17301508
  451.6 2.7 copy-start.3
  451.6 2.7 copy-start.6
  456.8 54.6 %copy-start.8 = (bf16[8,256,256]{2,1,0:T(8,128)(2,1)S(1)}, bf16[8,256,256]{2,1,0:T(8,128)(2,1)}, u32[]{:S(2)}) copy-start(bf16[8,256,256]{2,1,0:T(8,128)(2,1)} %get-tuple-element.51) | copy-start | bytes 3145732
  518.2 253.6 %reduce-scatter.11.cloned.1.call-start = ((), (), s32[]{:S(2)}) async-start(), calls=%async_computation.11 | async-start | bytes 3604480 | tf_op jit(solution)/shard_map/reduce_scatter | solution.py:364
  529.1 245.1 %reduce-scatter.5.cloned.1.call-start = ((), (), s32[]{:S(2)}) async-start(), calls=%async_computation.8 | async-start | bytes 3932160 | tf_op jit(solution)/shard_map/reduce_scatter | solution.py:364
  575.2 220.3 %reduce-scatter.9.cloned.1.call-start = ((), (), s32[]{:S(2)}) async-start(), calls=%async_computation.10 | async-start | bytes 7208960 | tf_op jit(solution)/shard_map/reduce_scatter | solution.py:364
  594.6 0.7 copy-start.12
  595.4 54.2 %copy-start.2 = (bf16[256,2048]{1,0:T(8,128)(2,1)S(1)}, bf16[256,2048]{1,0:T(8,128)(2,1)}, u32[]{:S(2)}) copy-start(bf16[256,2048]{1,0:T(8,128)(2,1)} %x_ref.2) | copy-start | bytes 3145732
  595.4 54.2 %copy-start.15 = (f32[256]{0:T(256)S(1)}, f32[256]{0:T(256)}, u32[]{:S(2)}) copy-start(f32[256]{0:T(256)} %copy-done.14) | copy-start | bytes 3076
  649.6 2.7 copy-start.13
  763.8 4.1 copy-start.4
  763.8 4.1 copy-start.5
Sparse Core Ops, SparseCore 0:
  28.5 78.0 all-gather.4
  108.2 26.4 all-gather.6
  136.3 106.1 all-gather.8
  243.9 57.4 all-gather.10
  518.3 26.7 reduce-scatter.6
  547.4 54.8 reduce-scatter.10
  604.7 60.0 reduce-scatter.4
  667.2 103.3 reduce-scatter.8

commit v2 on v1

--- a/solution.py
+++ b/solution.py
@@ -21,6 +21,10 @@
 VMEM = pl.BlockSpec(memory_space=pltpu.VMEM)
 
 
+def lasting(us):
+    return pl.CostEstimate(flops=0, bytes_accessed=int(us * 3.6e6), transcendentals=0)
+
+
 def params(cid=None, limit=56):
     extra = {} if cid is None else {"collective_id": cid, "has_side_effects": True}
     return pltpu.CompilerParams(vmem_limit_bytes=limit * 1024 * 1024, **extra)
@@ -54,136 +58,441 @@
     )
 
 
-def swap_kernel(x_ref, o_ref, own_sem, send_sem, recv_sem):
+class Swap:
+    sems = [pltpu.SemaphoreType.DMA, pltpu.SemaphoreType.DMA((TEAM,)), pltpu.SemaphoreType.DMA((TEAM,))]
+
+    def __init__(self, src, out, sems, same=False):
+        own_sem, send, recv = sems
+        mine, base, _, _ = place()
+        others = [lax.rem(mine + k, TEAM) for k in range(1, TEAM)]
+        self.near = [base + other for other in others]
+        self.copies = [
+            remote(src if same else src.at[other], out.at[mine], send.at[k], recv.at[k], base + other)
+            for k, other in enumerate(others)
+        ]
+        self.copies.append(pltpu.make_async_copy(src if same else src.at[mine], out.at[mine], own_sem))
+
+    def start(self):
+        for copy in self.copies:
+            copy.start()
+
+    def finish(self):
+        for copy in self.copies:
+            copy.wait()
+
+
+def slices(ref, pieces, size):
+    return jnp.concatenate([ref[:, i * size : (i + 1) * size] for i in pieces], axis=1)
+
+
+def open_kernel(planes, w_ref, small_ref, pieces_ref, all_ref, made, *sems):
+    swap, gather = Swap(made, pieces_ref, sems[:3]), Swap(small_ref, all_ref, sems[3:], same=True)
+    for i in range(TEAM):
+        made[i] = slices(w_ref, [s * HEADS + z * TEAM + i for s in range(3) for z in range(planes)], HEAD_DIM)
+    greet(swap.near)
+    swap.start()
+    gather.start()
+    swap.finish()
+    gather.finish()
+
+
+def opening(weight, small, planes, cid):
+    shape = (TEAM, weight.shape[0], weight.shape[1] // TEAM)
+    return pl.pallas_call(
+        functools.partial(open_kernel, planes),
+        out_shape=[jax.ShapeDtypeStruct(shape, BF16), jax.ShapeDtypeStruct((TEAM,) + small.shape, BF16)],
+        in_specs=[VMEM, ANY],
+        out_specs=[ANY, ANY],
+        scratch_shapes=[pltpu.VMEM(shape, BF16)] + Swap.sems * 2,
+        cost_estimate=lasting(15),
+        compiler_params=params(cid),
+    )(weight, small)
+
+
+def second_kernel(planes, gate_ref, up_ref, x_ref, _, pieces_ref, x_all_ref, made, *sems):
+    swap, gather = Swap(made, pieces_ref, sems[:3]), Gather(x_ref, x_all_ref, sems[3:])
+    greet(swap.near)
+    gather.start()
+    size = gate_ref.shape[1] // (planes * TEAM)
+    for i in range(TEAM):
+        units = [z * TEAM + i for z in range(planes)]
+        made[i] = jnp.concatenate([slices(gate_ref, units, size), slices(up_ref, units, size)], axis=1)
+    swap.start()
+    gather.middle()
+    gather.finish()
+    swap.finish()
+
+
+def second(gate, up, inputs, after, planes, cid):
+    shape = (TEAM, gate.shape[0], 2 * gate.shape[1] // TEAM)
+    return pl.pallas_call(
+        functools.partial(second_kernel, planes),
+        out_shape=[jax.ShapeDtypeStruct(shape, BF16), jax.ShapeDtypeStruct((TEAM,) + inputs.shape, BF16)],
+        in_specs=[VMEM, VMEM, ANY, ANY],
+        out_specs=[ANY, ANY],
+        scratch_shapes=[pltpu.VMEM(shape, BF16)] + Swap.sems + Gather.sems,
+        cost_estimate=lasting(55),
+        compiler_params=params(cid),
+    )(gate, up, inputs, after)
+
+
+def close_kernel(parts, planes, x_ref, _, *refs):
+    outs, held, sems = refs[:-4], refs[-4], refs[-3:]
+    swap = Swap(x_ref, held, sems)
+    greet(swap.near)
+    swap.start()
+    swap.finish()
+    size = held.shape[2] // (parts * planes)
+    for part in range(parts):
+        for z in range(planes):
+            at = part * planes + z
+            row = jnp.concatenate([held[i, :, at * size : (at + 1) * size] for i in range(TEAM)], axis=1)
+            out, first = (outs[part], z) if len(outs) > 1 else (outs[0], at)
+            out[:, first * TEAM * size : (first + 1) * TEAM * size] = row.astype(F32)
+
+
+def closing(blocks, after, parts, outs, planes, cid):
+    _, depth, width = blocks.shape
+    return pl.pallas_call(
+        functools.partial(close_kernel, parts, planes),
+        out_shape=[jax.ShapeDtypeStruct((depth, TEAM * width // outs), F32)] * outs,
+        in_specs=[ANY, ANY],
+        out_specs=[VMEM] * outs,
+        scratch_shapes=[pltpu.VMEM(blocks.shape, BF16)] + Swap.sems,
+        cost_estimate=lasting(18),
+        compiler_params=params(cid),
+    )(blocks, after)
+
+
+def vectors_kernel(planes, x_ref, _, o_ref, held, block, far, *sems):
+    own_sem, send, recv = sems[3:]
     mine, base, _, _ = place()
-    greet([base + lax.rem(mine + k, TEAM) for k in range(1, TEAM)])
-    copies = []
-    for k in range(1, TEAM):
-        other = lax.rem(mine + k, TEAM)
-        copy = remote(x_ref.at[other], o_ref.at[mine], send_sem.at[k], recv_sem.at[k], base + other)
+    plane = base // TEAM
+    swap = Swap(x_ref, held, sems[:3])
+    others = [lax.rem(plane + k, planes) for k in range(1, planes)]
+    greet(swap.near + [other * TEAM + mine for other in others])
+    swap.start()
+    swap.finish()
+    total = held[0]
+    for i in range(1, TEAM):
+        total = total + held[i]
+    block[...] = total
+    copies = [
+        remote(block.at[other], far.at[plane], send.at[k], recv.at[k], other * TEAM + mine)
+        for k, other in enumerate(others)
+    ]
+    copies.append(pltpu.make_async_copy(block.at[plane], far.at[plane], own_sem))
+    for copy in copies:
         copy.start()
-        copies.append(copy)
-    own = pltpu.make_async_copy(x_ref.at[mine], o_ref.at[mine], own_sem)
-    own.start()
     for copy in copies:
         copy.wait()
-    own.wait()
-
-
-def team_swap(blocks, cid):
+    total = far[0]
+    for i in range(1, planes):
+        total = total + far[i]
+    o_ref[...] = total
+
+
+def vector_sums(x, after, cid):
+    planes = x.shape[1]
+    many = pltpu.SemaphoreType.DMA((planes,))
     return pl.pallas_call(
-        swap_kernel,
-        out_shape=jax.ShapeDtypeStruct(blocks.shape, blocks.dtype),
-        in_specs=[ANY],
-        out_specs=ANY,
-        scratch_shapes=[pltpu.SemaphoreType.DMA] + [pltpu.SemaphoreType.DMA((TEAM,))] * 2,
+        functools.partial(vectors_kernel, planes),
+        out_shape=jax.ShapeDtypeStruct(x.shape[2:], F32),
+        in_specs=[VMEM, ANY],
+        out_specs=VMEM,
+        scratch_shapes=[pltpu.VMEM(x.shape, F32), pltpu.VMEM(x.shape[1:], F32), pltpu.VMEM(x.shape[1:], F32)]
+        + Swap.sems
+        + [pltpu.SemaphoreType.DMA, many, many],
+        cost_estimate=lasting(10),
         compiler_params=params(cid),
-    )(blocks)
-
-
-def gather_kernel(x_ref, o_ref, own_sem, send_sem, recv_sem, pass_sem, passed_sem):
-    mine, base, chip, core = place()
-    sibling = base + chip * 2 + 1 - core
-    peers = {k: chip_at(chip, k) * 2 + core for k in (3, 1, 2)}
-    greet([base + peer for peer in peers.values()] + [sibling])
-    copies = {}
-    for k, peer in peers.items():
-        copies[k] = remote(x_ref, o_ref.at[mine], send_sem.at[k], recv_sem.at[k], base + peer)
-        copies[k].start()
-    copies[0] = remote(x_ref, o_ref.at[mine], send_sem.at[0], recv_sem.at[0], sibling)
-    copies[0].start()
-    own = pltpu.make_async_copy(x_ref, o_ref.at[mine], own_sem)
-    own.start()
-    passed = []
-    for k in (1, 2, 3):
-        copies[k].wait_recv()
-        block = o_ref.at[peers[k]]
-        copy = remote(block, block, pass_sem.at[k], passed_sem.at[k], sibling)
-        copy.start()
-        passed.append(copy)
-    for k in (1, 2, 3):
-        copies[k].wait_send()
-    copies[0].wait()
-    own.wait()
-    for copy in passed:
-        copy.wait()
-
-
-def team_gather(block, cid):
+    )(x, after)
+
+
+class Gather:
+    sems = [pltpu.SemaphoreType.DMA((5,)), pltpu.SemaphoreType.DMA((5,)), pltpu.SemaphoreType.DMA((2,)),
+            pltpu.SemaphoreType.DMA((2,)), pltpu.SemaphoreType.DMA((6,)), pltpu.SemaphoreType.DMA((6,)),
+            pltpu.SemaphoreType.DMA]
+
+    def __init__(self, src, out, sems):
+        send, recv, hop_send, hop_recv, pass_send, pass_recv, own_sem = sems
+        mine, base, chip, core = place()
+        side, over, across = (chip_at(chip, k) * 2 + core for k in (1, 2, 3))
+        self.sibling = base + chip * 2 + 1 - core
+        self.near = [base + side, base + over, self.sibling]
+        half = src.shape[0] // 2
+        top, low = pl.ds(0, half), pl.ds(half, half)
+        self.first = [
+            remote(src.at[part], out.at[mine, part], send.at[i], recv.at[i], base + to)
+            for i, (part, to) in enumerate(((top, side), (low, over), (low, side), (top, over)))
+        ]
+        self.first.append(remote(src, out.at[mine], send.at[4], recv.at[4], self.sibling))
+        self.own = pltpu.make_async_copy(src, out.at[mine], own_sem)
+        self.hops = [
+            remote(out.at[at, part], out.at[at, part], hop_send.at[i], hop_recv.at[i], base + to)
+            for i, (at, part, to) in enumerate(((side, top, over), (over, low, side)))
+        ]
+        self.passed = [
+            remote(out.at[at, part], out.at[at, part], pass_send.at[i], pass_recv.at[i], self.sibling)
+            for i, (at, part) in enumerate(
+                ((side, top), (over, low), (side, low), (over, top), (across, top), (across, low))
+            )
+        ]
+
+    def start(self):
+        for copy in self.first:
+            copy.start()
+        self.own.start()
+
+    def middle(self):
+        for i in (0, 1):
+            self.first[i].wait_recv()
+            self.hops[i].start()
+            self.passed[i].start()
+
+    def finish(self):
+        for i in (2, 3):
+            self.first[i].wait_recv()
+            self.passed[i].start()
+        for i in (0, 1):
+            self.hops[i].wait_recv()
+            self.passed[4 + i].start()
+        for copy in self.first[:4] + self.hops:
+            copy.wait_send()
+        self.first[4].wait()
+        self.own.wait()
+        for copy in self.passed:
+            copy.wait()
+
+
+class Sum:
+    def scratch(rows, width):
+        return [pltpu.VMEM((4, rows, width), BF16), pltpu.VMEM((4, rows, width), BF16),
+                pltpu.VMEM((2, rows // 2, width), BF16), pltpu.VMEM((2, rows, width), BF16)]
+
+    sems = [pltpu.SemaphoreType.DMA((4,))] * 3 + [pltpu.SemaphoreType.DMA((2,))] * 2 + [pltpu.SemaphoreType.DMA((4,))] * 2
+
+    def __init__(self, blocks, scratch, sems, away=None):
+        self.own, self.beside, self.via, self.far = scratch
+        load_sem, near_send, near_recv, via_send, via_recv, far_send, far_recv = sems
+        _, base, chip, core = place()
+        chips = [chip_at(chip, k) for k in range(4)]
+        sibling = base + chip * 2 + 1 - core
+        side, over = (base + chips[k] * 2 + core for k in (1, 2))
+        self.near = [side, over, sibling]
+        self.half = self.own.shape[1] // 2
+        top, low = pl.ds(0, self.half), pl.ds(self.half, self.half)
+        self.loads = [
+            pltpu.make_async_copy(blocks.at[chips[k] * 2 + core], self.own.at[k], load_sem.at[k])
+            for k in range(4)
+            if away is None
+        ]
+
+        def near_copy(k):
+            src = blocks.at[chips[k] * 2 + 1 - core] if away is None else away.at[k]
+            return remote(src, self.beside.at[k], near_send.at[k], near_recv.at[k], sibling)
+
+        self.near_copy = near_copy
+        self.nears = [near_copy(k) for k in range(4)]
+        self.vias = [
+            remote(self.own.at[3, part], self.via.at[i], via_send.at[i], via_recv.at[i], to)
+            for i, (part, to) in enumerate(((top, side), (low, over)))
+        ]
+        self.fars = [
+            remote(self.own.at[k, part], self.far.at[k - 1, part], far_send.at[i], far_recv.at[i], to)
+            for i, (k, part, to) in enumerate(((2, low, over), (1, top, side), (2, top, over), (1, low, side)))
+        ]
+
+    def start(self):
+        for k in (3, 2, 1, 0):
+            self.loads[k].start()
+            self.nears[k].start()
+
+    def pair(self, k):
+        if self.loads:
+            self.loads[k].wait()
+        self.nears[k].wait_recv()
+
+        @pl.loop(0, self.own.shape[1] // 16)
+        def _(i):
+            part = pl.ds(pl.multiple_of(i * 16, 16), 16)
+            self.own[k, part, :] = (self.own[k, part, :].astype(F32) + self.beside[k, part, :].astype(F32)).astype(BF16)
+
+    def middle_a(self):
+        self.pair(3)
+        for copy in self.vias:
+            copy.start()
+
+    def middle_b(self):
+        self.pair(2)
+        self.fars[0].start()
+
+    def middle_c(self):
+        self.pair(1)
+        self.fars[1].start()
+
+    def middle(self):
+        self.middle_a()
+        self.middle_b()
+        self.middle_c()
+
+    def middle_two(self):
+        for i, k in ((0, 2), (1, 1)):
+            self.vias[i].wait_recv()
+
+            @pl.loop(0, self.half // 16)
+            def _(j, i=i, k=k):
+                part = pl.ds(pl.multiple_of(j * 16, 16), 16)
+                at = pl.ds(pl.multiple_of(j * 16 + i * self.half, 16), 16)
+                self.own[k, at, :] = (self.own[k, at, :].astype(F32) + self.via[i, part, :].astype(F32)).astype(BF16)
+
+            self.fars[2 + i].start()
+
+    def finish(self, use):
+        if self.loads:
+            self.loads[0].wait()
+        self.nears[0].wait_recv()
+        for copy in self.fars:
+            copy.wait_recv()
+
+        @pl.loop(0, self.own.shape[1] // 16)
+        def _(i):
+            part = pl.ds(pl.multiple_of(i * 16, 16), 16)
+            total = self.own[0, part, :].astype(F32) + self.beside[0, part, :].astype(F32)
+            use(part, total + self.far[0, part, :].astype(F32) + self.far[1, part, :].astype(F32))
+
+        for copy in self.nears + self.vias + self.fars:
+            copy.wait_send()
+
+
+def fold(x):
+    return x[:8] + x[8:]
+
+
+def mid_kernel(part_ref, x_ref, gain_ref, bias_ref, resid_ref, o_ref, block, *scratch):
+    total = Sum(part_ref, scratch[:4], scratch[4:11])
+    gather = Gather(block, o_ref, scratch[11:])
+    greet(total.near)
+    total.start()
+    total.middle()
+    total.middle_two()
+
+    def use(rows, value):
+        resid = x_ref[rows, :].astype(F32) + value
+        resid_ref[rows, :] = resid
+        normed, _ = normalize(resid)
+        block[rows, :] = (normed * gain_ref[...] + bias_ref[...]).astype(BF16)
+
+    total.finish(use)
+    gather.start()
+    gather.middle()
+    gather.finish()
+
+
+def mid(part, inputs, gain, bias, cid):
+    rows, width = inputs.shape
     return pl.pallas_call(
-        gather_kernel,
-        out_shape=jax.ShapeDtypeStruct((TEAM,) + block.shape, block.dtype),
-        in_specs=[ANY],
-        out_specs=ANY,
-        scratch_shapes=[pltpu.SemaphoreType.DMA] + [pltpu.SemaphoreType.DMA((4,))] * 4,
+        mid_kernel,
+        out_shape=[jax.ShapeDtypeStruct((rows, width), F32), jax.ShapeDtypeStruct((TEAM, rows, width), BF16)],
+        in_specs=[ANY, VMEM, VMEM, VMEM],
+        out_specs=[VMEM, ANY],
+        scratch_shapes=[pltpu.VMEM((rows, width), BF16)] + Sum.scratch(rows, width) + Sum.sems + Gather.sems,
+        cost_estimate=lasting(85),
         compiler_params=params(cid),
-    )(block)
-
-
-def sum_kernel(x_ref, o_ref, own, near, far, own_sem, near_send, near_recv, far_send, far_recv):
-    mine, base, chip, core = place()
-    sibling = base + chip * 2 + 1 - core
-    chips = {k: chip_at(chip, k) for k in (3, 1, 2, 0)}
-    rows = own.shape[1]
-    loads = {}
-    for k, at in chips.items():
-        loads[k] = pltpu.make_async_copy(x_ref.at[at * 2 + core], own.at[k], own_sem.at[k])
-        loads[k].start()
-    greet([base + chips[k] * 2 + core for k in (3, 1, 2)] + [sibling])
-    nears = {}
-    for k, at in chips.items():
-        nears[k] = remote(x_ref.at[at * 2 + 1 - core], near.at[k], near_send.at[k], near_recv.at[k], sibling)
-        nears[k].start()
-    fars = {}
-    for k in (3, 1, 2):
-        loads[k].wait()
-        nears[k].wait_recv()
-
-        @pl.loop(0, rows // 16)
-        def _(i, k=k):
-            part = pl.ds(pl.multiple_of(i * 16, 16), 16)
-            own[k, part, :] = (own[k, part, :].astype(F32) + near[k, part, :].astype(F32)).astype(BF16)
-
-        fars[k] = remote(own.at[k], far.at[k - 1], far_send.at[k - 1], far_recv.at[k - 1], base + chips[k] * 2 + core)
-        fars[k].start()
-    loads[0].wait()
-    nears[0].wait_recv()
-    for k in (1, 2, 3):
-        fars[k].wait_recv()
-
-    @pl.loop(0, rows // 16)
+    )(part, inputs, gain, bias)
+
+
+def mid_back_kernel(grads_ref, w_ref, resid_ref, g_ref, gain_ref, _, __, out_ref, sums_ref, o_ref, block, away, *scratch):
+    total = Sum(None, scratch[:4], scratch[4:11], away)
+    gather = Gather(block, o_ref, scratch[11:])
+    greet(total.near)
+    _, _, chip, core = place()
+    tile = 512
+
+    @pl.loop(0, 8)
     def _(i):
-        part = pl.ds(pl.multiple_of(i * 16, 16), 16)
-        total = own[0, part, :].astype(F32) + near[0, part, :].astype(F32)
-        for k in range(3):
-            total = total + far[k, part, :].astype(F32)
-        o_ref[part, :] = total
-
-    for k in (3, 1, 2, 0):
-        nears[k].wait_send()
-    for k in (3, 1, 2):
-        fars[k].wait_send()
-
-
-def team_sum(blocks, cid):
-    _, rows, width = blocks.shape
+        k = 3 - i // 2
+        at = lax.rem(chip // 2 + k // 2, 2) * 2 + lax.rem(chip + k, 2)
+
+        def make(to, at):
+            @pl.loop(0, w_ref.shape[0] // tile)
+            def _(j):
+                columns = pl.ds(pl.multiple_of(j * tile, tile), tile)
+                to[k, :, columns] = dot(grads_ref[at], w_ref[columns, :], NT).astype(BF16)
+
+        @pl.when(lax.rem(i, 2) == 0)
+        def _():
+            make(away, at * 2 + 1 - core)
+            total.near_copy(k).start()
+
+        @pl.when(lax.rem(i, 2) == 1)
+        def _():
+            make(total.own, at * 2 + core)
+
+        for step, advance in ((3, total.middle_a), (5, total.middle_b), (7, total.middle_c)):
+            pl.when(i == step)(advance)
+
+    total.middle_two()
+    sums_ref[...] = jnp.zeros_like(sums_ref)
+
+    def use(rows, value):
+        normed, inverse = normalize(resid_ref[rows, :])
+        sums_ref[:8, :] += fold(value * normed)
+        sums_ref[8:, :] += fold(value)
+        grad = g_ref[rows, :].astype(F32) + norm_back(value * gain_ref[...], normed, inverse)
+        out_ref[rows, :] = grad
+        block[rows, :] = grad.astype(BF16)
+
+    total.finish(use)
+    gather.start()
+    gather.middle()
+    gather.finish()
+
+
+def mid_back(grads, w_both, resid, out_grad, gain, after, then, cid):
+    rows, width = resid.shape
     return pl.pallas_call(
-        sum_kernel,
-        out_shape=jax.ShapeDtypeStruct((rows, width), F32),
-        in_specs=[ANY],
-        out_specs=VMEM,
-        scratch_shapes=[
-            pltpu.VMEM((4, rows, width), BF16),
-            pltpu.VMEM((4, rows, width), BF16),
-            pltpu.VMEM((3, rows, width), BF16),
-            pltpu.SemaphoreType.DMA((4,)),
-            pltpu.SemaphoreType.DMA((4,)),
-            pltpu.SemaphoreType.DMA((4,)),
-            pltpu.SemaphoreType.DMA((3,)),
-            pltpu.SemaphoreType.DMA((3,)),
+        mid_back_kernel,
+        out_shape=[
+            jax.ShapeDtypeStruct((rows, width), F32),
+            jax.ShapeDtypeStruct((16, width), F32),
+            jax.ShapeDtypeStruct((TEAM, rows, width), BF16),
         ],
+        in_specs=[VMEM, VMEM, VMEM, VMEM, VMEM, ANY, ANY],
+        out_specs=[VMEM, VMEM, ANY],
+        scratch_shapes=[pltpu.VMEM((rows, width), BF16), pltpu.VMEM((4, rows, width), BF16)] + Sum.scratch(rows, width) + Sum.sems + Gather.sems,
+        cost_estimate=lasting(87),
         compiler_params=params(cid),
-    )(blocks)
+    )(grads, w_both, resid, out_grad, gain, after, then)
+
+
+def last_kernel(part_ref, x_ref, grad_ref, gain_ref, _, out_ref, sums_ref, *scratch):
+    total = Sum(part_ref, scratch[:4], scratch[4:])
+    greet(total.near)
+    total.start()
+    total.middle()
+    total.middle_two()
+    sums_ref[...] = jnp.zeros_like(sums_ref)
+
+    def use(rows, value):
+        normed, inverse = normalize(x_ref[rows, :].astype(F32))
+        sums_ref[:8, :] += fold(value * normed)
+        sums_ref[8:, :] += fold(value)
+        out_ref[rows, :] = grad_ref[rows, :] + norm_back(value * gain_ref[...], normed, inverse)
+
+    total.finish(use)
+
+
+def last(part, inputs, grad_resid, gain, after, cid):
+    rows, width = inputs.shape
+    return pl.pallas_call(
+        last_kernel,
+        out_shape=[jax.ShapeDtypeStruct((rows, width), F32), jax.ShapeDtypeStruct((16, width), F32)],
+        in_specs=[ANY, VMEM, VMEM, VMEM, ANY],
+        out_specs=[VMEM, VMEM],
+        scratch_shapes=Sum.scratch(rows, width) + Sum.sems,
+        cost_estimate=lasting(47),
+        compiler_params=params(cid),
+    )(part, inputs, grad_resid, gain, after)
 
 
 def dot(a, b, dims=((1,), (0,))):
@@ -210,16 +519,23 @@
     )
 
 
-def turn(heads, cosine, front, back, sign):
+def turn(heads, cosine, sine):
     half, width = ROT // 2, heads.shape[-1]
-    moved = pltpu.roll(heads, width - half, 1) * front + pltpu.roll(heads, half, 1) * back
-    return heads * cosine + sign * moved
+    lanes = lax.broadcasted_iota(jnp.int32, heads.shape, 1) % HEAD_DIM
+    moved = jnp.where(lanes < half, -pltpu.roll(heads, width - half, 1), pltpu.roll(heads, half, 1))
+    return heads * cosine + moved * sine
+
+
+def wide(table):
+    return jnp.concatenate([table] * (LOCAL * HEAD_DIM // 128), axis=1)
 
 
 def visible(start):
-    rows = lax.broadcasted_iota(jnp.int32, (start.shape[0],) * 2, 0)
-    columns = lax.broadcasted_iota(jnp.int32, (start.shape[0],) * 2, 1)
-    return (columns <= rows) & (columns >= start)
+    size = start.shape[0]
+    rows = lax.broadcasted_iota(jnp.int32, (size, size), 0)
+    columns = lax.broadcasted_iota(jnp.int32, (size, size), 1)
+    start = jnp.concatenate([start] * (size // start.shape[1]), axis=1)
+    return (columns <= rows) & (columns.astype(F32) >= start)
 
 
 def head_of(x, h):
@@ -234,21 +550,32 @@
     return exponent / jnp.sum(exponent, axis=-1, keepdims=True)
 
 
-def attend_kernel(x_ref, gain_ref, bias_ref, w_ref, b_ref, wo_ref, tab_ref, start_ref, h_ref, qkv_ref, attn_ref, part_ref):
+def attend_kernel(
+    x_ref, gain_ref, bias_ref, w_ref, b_ref, wo_ref, tab_ref, g_ref, h_ref, qkv_ref, attn_ref, part_ref, g_all_ref, *sems
+):
+    gather = Gather(g_ref, g_all_ref, sems)
+    step = pl.program_id(0)
+
+    @pl.when(step == 0)
+    def _():
+        greet(gather.near)
+        gather.start()
+
+    pl.when(step == TEAM // 2)(gather.middle)
     stream = x_ref[0].astype(F32)
     normed, _ = normalize(stream)
     h_one = (normed * gain_ref[...] + bias_ref[...]).astype(BF16)
     h_ref[0] = h_one
     qkv = dot(h_one, w_ref[...]) + b_ref[...]
     width = LOCAL * HEAD_DIM
-    cosine, front, back = (jnp.concatenate([tab_ref[0, i]] * (width // 128), axis=1) for i in range(3))
-    query = turn(qkv[:, :width], cosine, front, back, 1.0).astype(BF16)
-    key = turn(qkv[:, width : 2 * width], cosine, front, back, 1.0).astype(BF16)
+    cosine, sine = wide(tab_ref[0, 0]), wide(tab_ref[0, 1])
+    query = turn(qkv[:, :width], cosine, sine).astype(BF16)
+    key = turn(qkv[:, width : 2 * width], cosine, sine).astype(BF16)
     value = qkv[:, 2 * width :].astype(BF16)
     qkv_ref[0, :, :width] = query
     qkv_ref[0, :, width : 2 * width] = key
     qkv_ref[0, :, 2 * width :] = value
-    allowed = visible(start_ref[0])
+    allowed = visible(tab_ref[0, 2])
     mixed = jnp.zeros((query.shape[0], width), F32)
     for h in range(LOCAL):
         probs = soft(head_of(query, h), key, allowed).astype(BF16)
@@ -256,6 +583,7 @@
     attn_low = mixed.astype(BF16)
     attn_ref[0] = attn_low
     part_ref[0] = dot(attn_low, wo_ref[...]).astype(BF16)
+    pl.when(step == TEAM - 1)(gather.finish)
 
 
 def per_seq(*shape):
@@ -266,7 +594,7 @@
     return pl.BlockSpec(shape, lambda s: (0,) * len(shape))
 
 
-def attend(x_all, gain, bias, w_qkv, b_qkv, w_out, tables, start):
+def attend(x_all, gain, bias, w_qkv, b_qkv, w_out, tables, out_grad, cid):
     seqs, rows, _ = x_all.shape
     width = LOCAL * HEAD_DIM
     return pl.pallas_call(
@@ -280,24 +608,39 @@
             whole(1, 3 * width),
             whole(width, D),
             per_seq(3, rows, 128),
-            per_seq(rows, 1),
+            ANY,
         ],
-        out_specs=[per_seq(rows, D), per_seq(rows, 3 * width), per_seq(rows, width), per_seq(rows, D)],
+        out_specs=[per_seq(rows, D), per_seq(rows, 3 * width), per_seq(rows, width), per_seq(rows, D), ANY],
         out_shape=[
             jax.ShapeDtypeStruct((seqs, rows, D), BF16),
             jax.ShapeDtypeStruct((seqs, rows, 3 * width), BF16),
             jax.ShapeDtypeStruct((seqs, rows, width), BF16),
             jax.ShapeDtypeStruct((seqs, rows, D), BF16),
+            jax.ShapeDtypeStruct((seqs, rows, D), BF16),
         ],
-        compiler_params=params(),
-    )(x_all, gain, bias, w_qkv, b_qkv, w_out, tables, start)
-
-
-def attend_back_kernel(g_ref, wo_ref, w_ref, qkv_ref, tab_ref, start_ref, gqkv_ref, part_ref, gb_ref):
+        scratch_shapes=Gather.sems,
+        cost_estimate=lasting(44),
+        compiler_params=params(cid),
+    )(x_all, gain, bias, w_qkv, b_qkv, w_out, tables, out_grad)
+
+
+def attend_back_kernel(
+    g_ref, wo_ref, w_ref, qkv_ref, tab_ref, block_ref, resid_ref, _, gqkv_ref, part_ref, gb_ref, out_ref, *scratch
+):
+    total = Sum(block_ref, scratch[:4], scratch[4:])
+    step = pl.program_id(0)
+
+    @pl.when(step == 0)
+    def _():
+        greet(total.near)
+        total.start()
+
+    pl.when(step == 1)(total.middle)
+    pl.when(step == TEAM - 3)(total.middle_two)
     width = LOCAL * HEAD_DIM
     grad_att = dot(g_ref[0], wo_ref[...], NT).astype(BF16)
     query, key, value = (qkv_ref[0, :, i * width : (i + 1) * width] for i in range(3))
-    allowed = visible(start_ref[0])
+    allowed = visible(tab_ref[0, 2])
     zero = jnp.zeros((query.shape[0], width), F32)
     grad_query, grad_key, grad_value = zero, zero, zero
     for h in range(LOCAL):
@@ -310,16 +653,23 @@
         grad_value = grad_value + dot(low, grad_h, TN)
         grad_query = grad_query + dot(grad_scores, key_h)
         grad_key = grad_key + dot(grad_scores, query_h, TN)
-    cosine, front, back = (jnp.concatenate([tab_ref[0, i]] * (width // 128), axis=1) for i in range(3))
-    grad_query = turn(grad_query * 0.125, cosine, front, back, -1.0)
-    grad_key = turn(grad_key * 0.125, cosine, front, back, -1.0)
+    cosine, sine = wide(tab_ref[0, 0]), -wide(tab_ref[0, 1])
+    grad_query = turn(grad_query * 0.125, cosine, sine)
+    grad_key = turn(grad_key * 0.125, cosine, sine)
     grad_qkv = jnp.concatenate([grad_query, grad_key, grad_value], axis=1).astype(BF16)
     gqkv_ref[0] = grad_qkv
     gb_ref[0] = jnp.sum(grad_qkv.astype(F32), axis=0, keepdims=True)
     part_ref[0] = dot(grad_qkv, w_ref[...], NT).astype(BF16)
 
-
-def attend_back(g_all, w_out, w_qkv, qkv, tables, start):
+    def use(rows, value):
+        out_ref[rows, :] = (resid_ref[rows, :] + value).astype(BF16)
+
+    @pl.when(step == TEAM - 1)
+    def _():
+        total.finish(use)
+
+
+def attend_back(g_all, w_out, w_qkv, qkv, tables, blocks, resid, after, cid):
     seqs, rows, _ = g_all.shape
     width = LOCAL * HEAD_DIM
     return pl.pallas_call(
@@ -331,16 +681,21 @@
             whole(D, 3 * width),
             per_seq(rows, 3 * width),
             per_seq(3, rows, 128),
-            per_seq(rows, 1),
+            ANY,
+            whole(rows, D),
+            ANY,
         ],
-        out_specs=[per_seq(rows, 3 * width), per_seq(rows, D), per_seq(1, 3 * width)],
+        out_specs=[per_seq(rows, 3 * width), per_seq(rows, D), per_seq(1, 3 * width), whole(rows, D)],
         out_shape=[
             jax.ShapeDtypeStruct((seqs, rows, 3 * width), BF16),
             jax.ShapeDtypeStruct((seqs, rows, D), BF16),
             jax.ShapeDtypeStruct((seqs, 1, 3 * width), F32),
+            jax.ShapeDtypeStruct((rows, D), BF16),
         ],
-        compiler_params=params(),
-    )(g_all, w_out, w_qkv, qkv, tables, start)
+        scratch_shapes=Sum.scratch(rows, D) + Sum.sems,
+        cost_estimate=lasting(47),
+        compiler_params=params(cid),
+    )(g_all, w_out, w_qkv, qkv, tables, blocks, resid, after)
 
 
 def team_shards(
@@ -364,88 +719,74 @@
         return lax.psum_scatter(x, "fsdp", scatter_dimension=0, tiled=True, axis_index_groups=lines)
 
     w_out = line_gather(out_weight)
-    vectors = jnp.concatenate([norm1_gain, norm1_bias, norm2_gain, norm2_bias, qkv_bias])
-    extra = jnp.zeros((16, 3 * width), BF16)
-    extra = extra.at[0, : vectors.shape[0]].set(vectors).at[1, :rows].set(positions.astype(BF16))
-    pieces = qkv_weight.reshape(depth, 3, planes, TEAM, HEAD_DIM).transpose(3, 0, 1, 2, 4).reshape(TEAM, depth, 3 * width)
-    pieces = jnp.concatenate([pieces, jnp.broadcast_to(extra, (TEAM,) + extra.shape)], axis=1)
-    pieces = team_swap(pieces, 0)
-    places = pieces[:, depth + 1, :rows].astype(F32)
-    gathered = line_gather(pieces).reshape(n, depth + 16, 3 * width)
-    w_qkv = gathered[:, :depth].reshape(D, 3 * width)
-    vectors = gathered[:, depth, : vectors.shape[0]].astype(F32)
+    small = jnp.concatenate([norm1_gain, norm1_bias, norm2_gain, norm2_bias, qkv_bias])
+    small = jnp.zeros((16, 2 * rows), BF16).at[0, : small.shape[0]].set(small).at[1, :rows].set(positions.astype(BF16))
+    pieces, small = opening(qkv_weight, small, planes, 0)
+    places = small[:, 1, :rows].astype(F32)
+    vectors = jnp.zeros((16 * 3 * width,), BF16).at[: TEAM * 2 * rows].set(small[:, 0].reshape(-1))
+    pieces = jnp.concatenate([pieces.reshape(TEAM * depth, 3 * width), vectors.reshape(16, 3 * width)])
+    gathered = line_gather(pieces).reshape(planes, TEAM * depth + 16, 3 * width)
+    w_qkv = gathered[:, : TEAM * depth].reshape(D, 3 * width)
+    vectors = gathered[:, TEAM * depth :].reshape(planes, -1)[:, : TEAM * 2 * rows].reshape(n, 2 * rows).astype(F32)
     gain_one, bias_one, gain_two, bias_two = (vectors[:, i * depth : (i + 1) * depth].reshape(1, D) for i in range(4))
-    b_qkv = vectors[:, 4 * depth :].reshape(3, planes, TEAM, HEAD_DIM)
+    b_qkv = vectors[:, 4 * depth : 4 * depth + qkv_bias.shape[0]].reshape(3, planes, TEAM, HEAD_DIM)
     b_qkv = lax.dynamic_index_in_dim(b_qkv, mine, 2, keepdims=False).reshape(1, 3 * width)
 
-    both = jnp.stack([w.reshape(depth, planes, TEAM, ff) for w in (gate_weight, up_weight)], axis=1)
-    both = both.transpose(3, 0, 1, 2, 4).reshape(TEAM, depth, 2 * planes * ff)
-    both = team_swap(both, 1)
+    both, x_all = second(gate_weight, up_weight, inputs, w_out, planes, 1)
     w_both = line_gather(both.reshape(TEAM * depth, 2 * planes * ff))
     w_down = line_gather(down_weight)
-    x_all = team_gather(inputs, 2)
-    g_all = team_gather(out_grad, 3)
 
     half = ROT // 2
     frequency = 10000.0 ** (-jnp.arange(half, dtype=F32) / half)
+    frequency = jnp.concatenate([frequency, frequency, jnp.zeros((HEAD_DIM - ROT,), F32)] * (128 // HEAD_DIM))
     angles = places[:, :, None] * frequency
-    cosine, sine = jnp.cos(angles), jnp.sin(angles)
-    ones, zeros = (jnp.full(angles.shape[:2] + (HEAD_DIM - ROT,), v, F32) for v in (1.0, 0.0))
-    none = jnp.zeros_like(sine)
-    tables = jnp.stack(
-        [
-            jnp.concatenate([a, b, c] * (128 // HEAD_DIM), axis=-1)
-            for a, b, c in ((cosine, cosine, ones), (-sine, none, zeros), (none, sine, zeros))
-        ],
-        axis=1,
-    )
-    start = (jnp.arange(rows, dtype=jnp.int32)[None] - places.astype(jnp.int32))[:, :, None]
-
-    h_one, qkv, attn_low, part = attend(x_all, gain_one, bias_one, w_qkv, b_qkv, w_out, tables, start)
-    stream = inputs.astype(F32)
-    resid = stream + team_sum(part, 4)
-    normed_two, inverse_two = normalize(resid)
-    h_two = team_gather((normed_two * gain_two + bias_two).astype(BF16), 5).reshape(tokens, D)
+    start = jnp.arange(rows, dtype=F32)[None] - places
+    tables = jnp.stack([jnp.cos(angles), jnp.sin(angles), jnp.broadcast_to(start[:, :, None], angles.shape)], axis=1)
+
+    h_one, qkv, attn_low, part, g_all = attend(x_all, gain_one, bias_one, w_qkv, b_qkv, w_out, tables, out_grad, 3)
+    resid, h_two = mid(part, inputs, gain_two, bias_two, 4)
+    h_two = h_two.reshape(tokens, D)
     g_rows = g_all.reshape(tokens, D)
     pre = dot(h_two, w_both)
     gate_pre, up_pre = pre[:, : planes * ff], pre[:, planes * ff :]
     sigmoid = jax.nn.sigmoid(gate_pre)
     silu = gate_pre * sigmoid
     hidden = (silu * up_pre).astype(BF16)
-    grad_down = line_sum(dot(hidden, g_rows, TN).astype(BF16))
+    grad_down = dot(hidden, g_rows, TN).astype(BF16)
+    g_rows, grad_down = lax.optimization_barrier((g_rows, grad_down))
+    grad_down = line_sum(grad_down)
     grad_hidden = dot(g_rows, w_down, NT)
     grad_gate = (grad_hidden * up_pre * sigmoid * (1.0 + gate_pre * (1.0 - sigmoid))).astype(BF16)
     grad_up = (grad_hidden * silu).astype(BF16)
     grad_both = jnp.concatenate([grad_gate, grad_up], axis=1)
-    grad_w_both = line_sum(dot(h_two, grad_both, TN).astype(BF16))
-    part = dot(grad_both, w_both, NT).astype(BF16).reshape(TEAM, rows, D)
-    grad_htwo = team_sum(part, 6)
-    grad_resid = out_grad.astype(F32) + norm_back(grad_htwo * gain_two, normed_two, inverse_two)
-    branch = team_gather(grad_resid.astype(BF16), 7)
-    grad_qkv, part, grad_bias = attend_back(branch, w_out, w_qkv, qkv, tables, start)
+    grad_w_both = dot(h_two, grad_both, TN).astype(BF16)
+    grads = grad_both.reshape(TEAM, rows, 2 * planes * ff)
+    grad_resid, sums_two, branch = mid_back(grads, w_both, resid, out_grad, gain_two, grad_w_both, grad_down, 5)
+    grad_w_both = line_sum(grad_w_both)
+    grad_out = dot(attn_low.reshape(tokens, width), branch.reshape(tokens, D), TN).astype(BF16)
+    part = dot(hidden, w_down).astype(BF16).reshape(TEAM, rows, D)
+    grad_qkv, part, grad_bias, block_out = attend_back(branch, w_out, w_qkv, qkv, tables, part, resid, grad_out, 6)
+    grad_out = line_sum(grad_out).astype(F32)
     grad_qkv = grad_qkv.reshape(tokens, 3 * width)
-    grad_w_qkv = line_sum(dot(h_one.reshape(tokens, D), grad_qkv, TN).astype(BF16))
-    grad_out = line_sum(dot(attn_low.reshape(tokens, width), branch.reshape(tokens, D), TN).astype(BF16))
-    grad_hone = team_sum(part, 8)
-    normed_one, inverse_one = normalize(stream)
-    input_grad = grad_resid + norm_back(grad_hone * gain_one, normed_one, inverse_one)
-
-    hidden, _ = lax.optimization_barrier((hidden, grad_hone))
-    part = dot(hidden, w_down).astype(BF16).reshape(TEAM, rows, D)
-    block_out = (resid + team_sum(part, 9)).astype(BF16)
+    grad_qkv, grad_w_both = lax.optimization_barrier((grad_qkv, grad_w_both))
+    grad_w_qkv = dot(h_one.reshape(tokens, D), grad_qkv, TN).astype(BF16)
+    input_grad, sums_one = last(part, inputs, grad_resid, gain_one, grad_w_qkv, 7)
+    grad_w_qkv = line_sum(grad_w_qkv)
 
     bias = jnp.zeros((3, planes, TEAM, HEAD_DIM), F32)
     bias = lax.dynamic_update_slice(
         bias, jnp.sum(grad_bias, axis=0).reshape(3, planes, 1, HEAD_DIM), (0, 0, mine, 0)
     ).reshape(n, -1)
-    sums = [jnp.sum(v, axis=0).reshape(n, depth) for v in (grad_hone * normed_one, grad_hone, grad_htwo * normed_two, grad_htwo)]
-    sums = lax.psum_scatter(jnp.concatenate(sums + [bias], axis=1), "fsdp", scatter_dimension=0, tiled=True)[0]
-    sums = [sums[i * depth : (i + 1) * depth] for i in range(4)] + [sums[4 * depth :]]
-
-    grad_w_both = team_swap(grad_w_both.reshape(TEAM, depth, 2 * planes * ff), 10)
-    grad_w_both = grad_w_both.reshape(TEAM, depth, 2, planes, ff).transpose(2, 1, 3, 0, 4).reshape(2, depth, -1).astype(F32)
-    grad_w_qkv = team_swap(grad_w_qkv.reshape(TEAM, depth, 3 * width), 11)
-    grad_w_qkv = grad_w_qkv.reshape(TEAM, depth, 3, planes, HEAD_DIM).transpose(1, 2, 3, 0, 4).reshape(depth, -1).astype(F32)
+    sums = [jnp.sum(v[i : i + 8], axis=0).reshape(n, depth) for v in (sums_one, sums_two) for i in (0, 8)]
+    sums = jnp.pad(jnp.concatenate(sums + [bias], axis=1), ((0, 0), (0, 1024 - 4 * depth - bias.shape[1])))
+    sums = sums.reshape(planes, TEAM, 8, 128).transpose(1, 0, 2, 3)
+    sums = vector_sums(sums, input_grad, 8).reshape(-1)
+    sums = [sums[i * depth : (i + 1) * depth] for i in range(4)] + [sums[4 * depth : 4 * depth + bias.shape[1]]]
+
+    blocks = grad_w_both.reshape(TEAM, depth, 2 * planes * ff)
+    grad_gate_w, grad_up_w = closing(blocks, sums[0], 2, 2, planes, 9)
+    blocks = grad_w_qkv.reshape(TEAM, depth, 3 * width)
+    (grad_w_qkv,) = closing(blocks, grad_up_w, 3, 1, planes, 10)
     return (
         block_out,
         input_grad,
@@ -453,11 +794,11 @@
         sums[1],
         grad_w_qkv,
         sums[4],
-        grad_out.astype(F32),
+        grad_out,
         sums[2],
         sums[3],
-        grad_w_both[0],
-        grad_w_both[1],
+        grad_gate_w,
+        grad_up_w,
         grad_down.astype(F32),
     )
 

time: 855 us -> 626 us (0.73)
  Pallas kernels: 566 us -> 441 us
  blocking collectives: 45.4 us -> 0 us
  local copies, waits for them, and re-layouts: 64.8 us -> 35.8 us
  matrix products: 114 us -> 88.2 us
  waiting for transfers between devices: 1.35 us -> 14 us
  other arithmetic: 36.6 us -> 24.9 us
    pallas_call x12 -> x8, Pallas kernels: 501 us -> 349 us  [the longest x1 97.3 us: mid_back(): pl.pallas_call(mid_back_kernel, out_shape=[jax.ShapeDtypeStruct((rows, wi...]
    unnamed x1 -> x0, blocking collectives: 45.4 us -> none
    dot_general x8 -> x7, matrix products: 114 us -> 88.2 us  [dot(): return lax.dot_general(a, b, (dims, ((), ())), preferred_element_type=F32)]
    convert_element_type x4 -> x1, local copies, waits for them, and re-layouts: 17.9 us -> 0.05 us  [team_shards(): gathered[:, TEAM * depth:].reshape(planes, -1)[:, :TEAM * 2 * rows]]
    pallas_call x1, Pallas kernels: 31 us -> 45 us  [attend(): pl.pallas_call(attend_kernel, grid=(seqs,), in_specs=[per_seq(rows, D), w...]
    pallas_call x1, Pallas kernels: 34.6 us -> 46.8 us  [attend_back(): pl.pallas_call(attend_back_kernel, grid=(seqs,), in_specs=[per_seq(rows,...]
    unnamed x48 -> x36, local copies, waits for them, and re-layouts: 0.81 us -> 11 us
    all_gather x4, waiting for transfers between devices: 0.03 us -> 8.78 us  [line_gather(): lax.all_gather(x, 'fsdp', axis=0, tiled=True, axis_index_groups=lines)]
  transfers between devices with their start and end apart: 8 -> 8, of which waited for: 0 -> 3; matrix products, arithmetic and copies ran while one was open for 17% -> 22% of each run, Pallas kernels for 50% -> 69%
where the time goes in v2:
time: 626 us; the launch traced here: 619 us
  Pallas kernels  441 us (70%)
  matrix products  88.2 us (14%)
  local copies, waits for them, and re-layouts  35.8 us (6%)
  other arithmetic  24.9 us (4%)
  between operations  14.7 us (2%)
  waiting for transfers between devices  14 us (2%)
    pallas_call x1, Pallas kernels, mid_back(): pl.pallas_call(mid_back_kernel, out_shape=[jax.ShapeDtypeStruct((rows, wi...  97.3 us
    dot_general x7, matrix products, dot(): return lax.dot_general(a, b, (dims, ((), ())), preferred_element_type=F32)  88.2 us
    pallas_call x1, Pallas kernels, mid(): pl.pallas_call(mid_kernel, out_shape=[jax.ShapeDtypeStruct((rows, width),...  84.8 us
    pallas_call x1, Pallas kernels, second(): pl.pallas_call(functools.partial(second_kernel, planes), out_shape=[jax.S...  57.8 us
    pallas_call x1, Pallas kernels, last(): pl.pallas_call(last_kernel, out_shape=[jax.ShapeDtypeStruct((rows, width)...  47.4 us
    pallas_call x1, Pallas kernels, attend_back(): pl.pallas_call(attend_back_kernel, grid=(seqs,), in_specs=[per_seq(rows,...  46.8 us
    pallas_call x1, Pallas kernels, attend(): pl.pallas_call(attend_kernel, grid=(seqs,), in_specs=[per_seq(rows, D), w...  45 us
    pallas_call x2, Pallas kernels, closing(): pl.pallas_call(functools.partial(close_kernel, parts, planes), out_shape=...  33.8 us
  transfers between devices with their start and end apart: 8, of which 3 were waited for; matrix products, arithmetic and copies ran while one was open for 22% of the time, Pallas kernels for 69%

profile of v2, /device:TPU:0, one launch (start us, length us, event | category | flops | bytes accessed | tf_op | source)
XLA Modules:
  0.0 618.8 jit_solution(6714151188127787938)
XLA Ops:
  7.2 0.7 all-gather.5.cloned.1.call-update
  8.0 3.4 concatenate.21
  11.4 0.7 convert_element_type.51
  12.9 17.0 %shard_map.221 = (bf16[8,64,768]{2,1,0:T(8,128)(2,1)}, bf16[8,16,512]{2,1,0:T(8,128)(2,1)}) custom-call(bf16[64,6144]{1,0:T(8,128)(2,1)} %w_ref.1, bf16[16,512]{1,0:T(8,128)(2,1)} %copy-done.10), custom_call_target="tpu_custom_call" | custom-call | bytes 54000000 | tf_op jit(solution)/shard_map/pallas_call | solution.py:101
  29.9 0.9 slice_reduce_fusion.4
  30.9 2.1 pad_maximum_fusion.2
  33.0 7.2 %all-gather.5.cloned.1.call-done._.wo_ref = bf16[256,2048]{1,0:T(8,128)(2,1)} async-done(((bf16[64,2048]{1,0:T(8,128)(2,1)}), bf16[256,2048]{1,0:T(8,128)(2,1)}) %all-gather.5.cloned.1.call-update) | async-done | bytes 1048592 | tf_op jit(solution)/shard_map/all_gather | solution.py:716
  40.2 57.8 %shard_map.220 = (bf16[8,64,1408]{2,1,0:T(8,128)(2,1)}, bf16[8,256,2048]{2,1,0:T(8,128)(2,1)}) custom-call(bf16[64,5632]{1,0:T(8,128)(2,1)} %gate_ref.1, bf16[64,5632]{1,0:T(8,128)(2,1)} %up_ref.1, bf16[256,2048]{1,0:T(8,128)(2,1)} %x_ref.5, bf16[256,2048]{1,0:T(8,128)(2,1)} %all-gather.5.cloned.1.call-done._.wo_ref), custom_call_target="tpu_custom_call" | custom-call | bytes 198000000 | tf_op jit(solution)/shard_map/pallas_call | solution.py:128
  98.7 0.8 slice_convert_fusion.1
  99.6 3.7 multiply_cosine_fusion
  103.6 1.9 pad_maximum_fusion.1.tab_ref
  105.5 1.5 all-gather.7.cloned.1.call-done
  107.0 0.9 slice_bitcast_fusion
  108.2 3.8 slice.134
  113.4 0.7 reshape.222.bias_ref
  115.4 45.0 %shard_map.222 = (bf16[8,256,2048]{2,1,0:T(8,128)(2,1)}, bf16[8,256,768]{2,1,0:T(8,128)(2,1)}, bf16[8,256,256]{2,1,0:T(8,128)(2,1)}, bf16[8,256,2048]{2,1,0:T(8,128)(2,1)}, bf16[8,256,2048]{2,1,0:T(8,128)(2,1)}) custom-call(bf16[8,256,2048]{2,1,0:T(8,128)(2,1)} %get-tuple-element.74.x_ref, f32[1,2048]{1,0:T(1,128)} %reshape.221.gain_ref, ...), custom_call_target="tpu_custom_call" | custom-call | bytes 158400000 | tf_op jit(solution)/shard_map/pallas_call | solution.py:600
  160.4 84.8 %shard_map.223 = (f32[256,2048]{1,0:T(8,128)}, bf16[8,256,2048]{2,1,0:T(8,128)(2,1)}) custom-call(bf16[8,256,2048]{2,1,0:T(8,128)(2,1)} %get-tuple-element.78.part_ref, bf16[256,2048]{1,0:T(8,128)(2,1)} %x_ref.5, f32[1,2048]{1,0:T(1,128)} %reshape.227.gain_ref, f32[1,2048]{1,0:T(1,128)} %reshape.228.bias_ref), custom_call_target="tpu_custom_call" | custom-call | bytes 306000000 | tf_op jit(solution)/shard_map/pallas_call | solution.py:393
  245.3 18.8 %fusion.4 = f32[2048,1408]{0,1:T(8,128)} fusion(bf16[2048,2048]{1,0:T(8,128)(2,1)} %bitcast.73, bf16[2048,1408]{1,0:T(8,128)(2,1)} %all-gather.9.cloned.1.call-done.w_ref), kind=kOutput, calls=%fused_computation.33 | convolution fusion | flops 11811160064 | bytes 25690112 | tf_op jit(solution)/shard_map/dot_general | solution.py:499
  264.1 5.4 multiply_convert_fusion.2
  269.5 1.3 copy-done.12
  270.8 7.4 %convolution_convert_fusion.3 = bf16[704,2048]{1,0:T(8,128)(2,1)} fusion(bf16[2048,704]{0,1:T(8,128)(2,1)S(1)} %multiply_convert_fusion.2, bf16[2048,2048]{1,0:T(8,128)(2,1)S(1)} %bitcast.72), kind=kOutput, calls=%fused_computation.9 | convolution fusion | flops 5907021824 | bytes 14155776 | tf_op jit(solution)/shard_map/dot_general | solution.py:499
  278.4 15.7 %multiply_convert_fusion.1 = (bf16[2048,704]{0,1:T(8,128)(2,1)S(1)}, bf16[2048,704]{0,1:T(8,128)(2,1)S(1)}) fusion(f32[2048,1408]{0,1:T(8,128)} %fusion.4, bf16[2048,2048]{1,0:T(8,128)(2,1)} %bitcast.71, bf16[704,2048]{1,0:T(8,128)(2,1)} %all-gather.11.cloned.1.call-done), kind=kOutput, calls=%fused_computation.4 | convolution fusion | flops 5924323328 | bytes 28573696 | tf_op jit(solution)/shard_map/dot_general | solution.py:499
  294.0 1.6 copy-done.4
  295.6 0.8 copy-done.5
  296.5 17.4 %convolution_convert_fusion.1._ = bf16[2048,1408]{1,0:T(8,128)(2,1)} fusion(bf16[2048,2048]{1,0:T(8,128)(2,1)} %bitcast.74, bf16[2048,704]{0,1:T(8,128)(2,1)S(1)} %get-tuple-element.105, bf16[2048,704]{0,1:T(8,128)(2,1)S(1)} %get-tuple-element.104), kind=kOutput, calls=%fused_computation.1 | convolution fusion | flops 11825577984 | bytes 19922944 | tf_op jit(solution)/shard_map/dot_general | solution.py:499
  313.9 6.2 %pad_maximum_fusion = bf16[2048,1408]{0,1:T(8,128)(2,1)} fusion(bf16[2048,704]{0,1:T(8,128)(2,1)} %copy-done.5, bf16[2048,704]{0,1:T(8,128)(2,1)} %copy-done.4), kind=kLoop, calls=%fused_computation.2 | loop fusion | flops 11534336 | bytes 11534336 | tf_op jit(solution)/shard_map/concatenate | solution.py:761
  320.1 8.5 %copy.29 = bf16[2048,1408]{1,0:T(8,128)(2,1)} copy(bf16[2048,1408]{0,1:T(8,128)(2,1)} %pad_maximum_fusion) | data formatting | bytes 11534336 | tf_op jit(solution)/shard_map/concatenate | solution.py:761
  328.6 3.9 reduce-scatter.5.cloned.1.call-done.__
  332.5 97.3 %shard_map.224 = (f32[256,2048]{1,0:T(8,128)}, f32[16,2048]{1,0:T(8,128)}, bf16[8,256,2048]{2,1,0:T(8,128)(2,1)}) custom-call(bf16[8,256,1408]{2,1,0:T(8,128)(2,1)} %bitcast.55, bf16[2048,1408]{1,0:T(8,128)(2,1)} %all-gather.9.cloned.1.call-done.w_ref, f32[256,2048]{1,0:T(8,128)} %get-tuple-element.82.resid_ref, bf16[256,2048]{1,0:T(8,128)(2,1)} %g_ref.3, ...), custom_call_target="tpu_custom_call" | custom-call | bytes 313200000 | tf_op jit(solution)/shard_map/pallas_call | solution.py:453
  429.8 6.7 %fusion.1._ = bf16[256,2048]{1,0:T(8,128)(2,1)} fusion(bf16[8,256,256]{2,1,0:T(8,128)(2,1)S(1)} %copy-done.7, bf16[8,256,2048]{2,1,0:T(8,128)(2,1)} %get-tuple-element.84.g_ref), kind=kOutput, calls=%fused_computation.12 | convolution fusion | flops 2148007936 | bytes 10485760 | tf_op jit(solution)/shard_map/dot_general | solution.py:499
  436.6 10.8 %convolution_convert_fusion = bf16[2048,2048]{1,0:T(8,128)(2,1)} fusion(bf16[2048,704]{0,1:T(8,128)(2,1)S(1)} %multiply_convert_fusion.2, bf16[704,2048]{1,0:T(8,128)(2,1)} %all-gather.11.cloned.1.call-done), kind=kOutput, calls=%fused_computation | convolution fusion | flops 5909774336 | bytes 14155776 | tf_op jit(solution)/shard_map/dot_general | solution.py:499
  447.4 46.8 %shard_map.225 = (bf16[8,256,768]{2,1,0:T(8,128)(2,1)}, bf16[8,256,2048]{2,1,0:T(8,128)(2,1)}, f32[8,1,768]{2,1,0:T(1,128)}, bf16[256,2048]{1,0:T(8,128)(2,1)}) custom-call(bf16[8,256,2048]{2,1,0:T(8,128)(2,1)} %get-tuple-element.84.g_ref, bf16[256,2048]{1,0:T(8,128)(2,1)} %all-gather.5.cloned.1.call-done._.wo_ref, bf16[2048,768]{1,0:T(8,128)(2,1)} %bitcast.54, ...), custom_call_target="tpu_custom_call" | custom-call | bytes 169200000 | tf_op jit(solution)/shard_map/pallas_call | solution.py:675
  494.2 11.4 %convolution_convert_fusion.2._ = bf16[2048,768]{1,0:T(8,128)(2,1)} fusion(bf16[2048,2048]{1,0:T(8,128)(2,1)} %bitcast.70, bf16[2048,768]{1,0:T(8,128)(2,1)} %bitcast.75), kind=kOutput, calls=%fused_computation.8 | convolution fusion | flops 6444023808 | bytes 14680064 | tf_op jit(solution)/shard_map/dot_general | solution.py:499
  506.1 1.3 convert_element_type.65
  507.3 1.8 convert_element_type.64
  509.1 47.4 %shard_map.226 = (f32[256,2048]{1,0:T(8,128)}, f32[16,2048]{1,0:T(8,128)}) custom-call(bf16[8,256,2048]{2,1,0:T(8,128)(2,1)} %get-tuple-element.88.part_ref, bf16[256,2048]{1,0:T(8,128)(2,1)} %x_ref.5, f32[256,2048]{1,0:T(8,128)} %get-tuple-element.89.grad_ref, f32[1,2048]{1,0:T(1,128)} %reshape.221.gain_ref, bf16[2048,768]{1,0:T(8,128)(2,1)} %convolution_convert_fusion.2._), custom_call_target="tpu_custom_call" | custom-call | bytes 169200000 | tf_op jit(solution)/shard_map/pallas_call | solution.py:487
  556.5 1.1 slice_reduce_fusion.2
  557.8 0.7 copy_bitcast_fusion.1.x_ref
  558.5 11.1 %shard_map.227 = f32[8,128]{1,0:T(8,128)} custom-call(f32[8,4,8,128]{3,2,1,0:T(8,128)} %copy_bitcast_fusion.1.x_ref, f32[256,2048]{1,0:T(8,128)} %get-tuple-element.129._), custom_call_target="tpu_custom_call" | custom-call | bytes 36000000 | tf_op jit(solution)/shard_map/pallas_call | solution.py:198
  569.6 1.2 slice.127
  570.8 1.4 fusion.3
  572.3 20.2 %shard_map.228 = (f32[64,5632]{1,0:T(8,128)}, f32[64,5632]{1,0:T(8,128)}) custom-call(bf16[8,64,1408]{2,1,0:T(8,128)(2,1)} %bitcast.59, f32[64]{0:T(128)} %get-tuple-element.130._), custom_call_target="tpu_custom_call" | custom-call | bytes 64800000 | tf_op jit(solution)/shard_map/pallas_call | solution.py:156
  592.5 13.6 %shard_map.229 = f32[64,6144]{1,0:T(8,128)} custom-call(bf16[8,64,768]{2,1,0:T(8,128)(2,1)} %bitcast.62, f32[64,5632]{1,0:T(8,128)} %get-tuple-element.138._), custom_call_target="tpu_custom_call" | custom-call | bytes 64800000 | tf_op jit(solution)/shard_map/pallas_call | solution.py:156
  606.2 1.0 copy.52
  607.1 1.3 copy.53
  608.5 1.1 copy.54
  609.6 1.1 copy.55
  610.7 1.1 copy.56
  (79 shorter events, 6.0 us)
Async XLA Ops:
  7.2 33.1 %all-gather.5.cloned.1.call-start = ((), (), s32[]{:S(2)}) async-start(), calls=%async_computation.4 | async-start | bytes 1310720 | tf_op jit(solution)/shard_map/all_gather | solution.py:716
  7.9 99.1 %all-gather.7.cloned.1.call-start = ((), (), s32[]{:S(2)}) async-start(), calls=%async_computation.5 | async-start | bytes 4055040 | tf_op jit(solution)/shard_map/all_gather | solution.py:716
  12.3 0.6 copy-start.10
  33.0 212.3 %all-gather.9.cloned.1.call-start = ((), (), s32[]{:S(2)}) async-start(), calls=%async_computation.6 | async-start | bytes 7208960 | tf_op jit(solution)/shard_map/all_gather | solution.py:716
  98.1 180.3 %all-gather.11.cloned.1.call-start = ((), (), s32[]{:S(2)}) async-start(), calls=%async_computation.7 | async-start | bytes 3604480 | tf_op jit(solution)/shard_map/all_gather | solution.py:716
  98.6 233.9 %reduce-scatter.5.cloned.1.call-start = ((), (), s32[]{:S(2)}) async-start(), calls=%async_computation.8 | async-start | bytes 3604480 | tf_op jit(solution)/shard_map/reduce_scatter | solution.py:719
  264.1 6.7 %copy-start.12 = (bf16[8,256,2048]{2,1,0:T(8,128)(2,1)S(1)}, bf16[8,256,2048]{2,1,0:T(8,128)(2,1)}, u32[]{:S(2)}) copy-start(bf16[8,256,2048]{2,1,0:T(8,128)(2,1)} %get-tuple-element.77) | copy-start | bytes 25165828
  278.3 215.9 %reduce-scatter.7.cloned.1.call-start = ((), (), s32[]{:S(2)}) async-start(), calls=%async_computation.9 | async-start | bytes 7208960 | tf_op jit(solution)/shard_map/reduce_scatter | solution.py:719
  294.0 1.6 copy-start.4
  294.0 2.4 copy-start.5
  313.9 193.5 %reduce-scatter.11.cloned.1.call-start = ((), (), s32[]{:S(2)}) async-start(), calls=%async_computation.11 | async-start | bytes 1310720 | tf_op jit(solution)/shard_map/reduce_scatter | solution.py:719
  332.5 97.3 %copy-start.7 = (bf16[8,256,256]{2,1,0:T(8,128)(2,1)S(1)}, bf16[8,256,256]{2,1,0:T(8,128)(2,1)}, u32[]{:S(2)}) copy-start(bf16[8,256,256]{2,1,0:T(8,128)(2,1)} %get-tuple-element.86) | copy-start | bytes 3145732
  436.5 156.0 %reduce-scatter.9.cloned.1.call-start = ((), (), s32[]{:S(2)}) async-start(), calls=%async_computation.10 | async-start | bytes 3932160 | tf_op jit(solution)/shard_map/reduce_scatter | solution.py:719
  494.2 11.5 %copy-start.11 = (f32[8,1,768]{2,1,0:T(1,128)S(1)}, f32[8,1,768]{2,1,0:T(1,128)}, u32[]{:S(2)}) copy-start(f32[8,1,768]{2,1,0:T(1,128)} %get-tuple-element.96) | copy-start | bytes 73732
  494.2 11.7 %copy-start.9 = (f32[16,2048]{1,0:T(8,128)S(1)}, f32[16,2048]{1,0:T(8,128)}, u32[]{:S(2)}) copy-start(f32[16,2048]{1,0:T(8,128)} %get-tuple-element.95) | copy-start | bytes 393220
  494.2 11.9 %copy-start.3 = (bf16[176,2048]{1,0:T(8,128)(2,1)S(1)}, bf16[176,2048]{1,0:T(8,128)(2,1)}, u32[]{:S(2)}) copy-start(bf16[176,2048]{1,0:T(8,128)(2,1)} %reduce-scatter.5.cloned.1.call-done.__) | copy-start | bytes 2162692
  556.5 49.6 %copy-start.8 = (bf16[256,2048]{1,0:T(8,128)(2,1)S(1)}, bf16[256,2048]{1,0:T(8,128)(2,1)}, u32[]{:S(2)}) copy-start(bf16[256,2048]{1,0:T(8,128)(2,1)} %get-tuple-element.128) | copy-start | bytes 3145732
  556.5 50.6 %copy-start = (f32[256,2048]{1,0:T(8,128)S(1)}, f32[256,2048]{1,0:T(8,128)}, u32[]{:S(2)}) copy-start(f32[256,2048]{1,0:T(8,128)} %get-tuple-element.129._) | copy-start | bytes 6291460
  592.5 17.1 %copy-start.6 = (f32[64,5632]{1,0:T(8,128)S(1)}, f32[64,5632]{1,0:T(8,128)}, u32[]{:S(2)}) copy-start(f32[64,5632]{1,0:T(8,128)} %get-tuple-element.137) | copy-start | bytes 4325380
  606.1 2.3 copy-start.1
  606.2 4.6 copy-start.2
Sparse Core Ops, SparseCore 0:
  9.6 30.6 all-gather.4
  42.4 64.6 all-gather.6
  108.6 105.3 all-gather.8
  215.5 57.4 all-gather.10
  278.4 54.0 reduce-scatter.4
  334.7 102.0 reduce-scatter.6
  439.7 27.6 reduce-scatter.10
  505.8 59.3 reduce-scatter.8

commit v3 on v2

--- a/solution.py
+++ b/solution.py
@@ -45,6 +45,10 @@
     return along_y * 2 + along_x
 
 
+def relation(chip, core, r):
+    return chip_at(chip, r // 2) * 2 + lax.rem(core + r, 2)
+
+
 def greet(devices):
     barrier = pltpu.get_barrier_semaphore()
     for device in devices:
@@ -61,16 +65,19 @@
 class Swap:
     sems = [pltpu.SemaphoreType.DMA, pltpu.SemaphoreType.DMA((TEAM,)), pltpu.SemaphoreType.DMA((TEAM,))]
 
-    def __init__(self, src, out, sems, same=False):
+    def __init__(self, src, out, sems, same=False, near_first=False):
         own_sem, send, recv = sems
-        mine, base, _, _ = place()
-        others = [lax.rem(mine + k, TEAM) for k in range(1, TEAM)]
+        mine, base, chip, core = place()
+        others = [relation(chip, core, r) for r in range(1, TEAM)]
         self.near = [base + other for other in others]
         self.copies = [
-            remote(src if same else src.at[other], out.at[mine], send.at[k], recv.at[k], base + other)
-            for k, other in enumerate(others)
+            remote(
+                src if same else src.at[other], out.at[r if near_first else mine], send.at[r], recv.at[r], base + other
+            )
+            for r, other in enumerate(others, 1)
         ]
-        self.copies.append(pltpu.make_async_copy(src if same else src.at[mine], out.at[mine], own_sem))
+        own = src if same else src.at[mine]
+        self.copies.append(pltpu.make_async_copy(own, out.at[0 if near_first else mine], own_sem))
 
     def start(self):
         for copy in self.copies:
@@ -81,131 +88,175 @@
             copy.wait()
 
 
+class Line:
+    def sems(planes):
+        return [pltpu.SemaphoreType.DMA, pltpu.SemaphoreType.DMA((planes,)), pltpu.SemaphoreType.DMA((planes,))]
+
+    def __init__(self, planes, src, out, sems, same=False, within=False):
+        own_sem, send, recv = sems
+        mine, base, _, _ = place()
+        plane = base // TEAM
+        others = [lax.rem(plane + k, planes) for k in range(1, planes)]
+        self.near = [other * TEAM + mine for other in others]
+        self.copies = [
+            remote(src if same else src.at[other], out.at[plane], send.at[k], recv.at[k], other * TEAM + mine)
+            for k, other in enumerate(others)
+        ]
+        own = src if same else src.at[plane]
+        self.own = None if within else pltpu.make_async_copy(own, out.at[plane], own_sem)
+
+    def start(self):
+        for copy in self.copies:
+            copy.start()
+        if self.own is not None:
+            self.own.start()
+
+    def finish(self):
+        for copy in self.copies:
+            copy.wait()
+        if self.own is not None:
+            self.own.wait()
+
+
 def slices(ref, pieces, size):
     return jnp.concatenate([ref[:, i * size : (i + 1) * size] for i in pieces], axis=1)
 
 
-def open_kernel(planes, w_ref, small_ref, pieces_ref, all_ref, made, *sems):
-    swap, gather = Swap(made, pieces_ref, sems[:3]), Swap(small_ref, all_ref, sems[3:], same=True)
+def open_kernel(planes, w_ref, out_weight_ref, pieces_ref, w_out_ref, made, *sems):
+    swap, line = Swap(made, pieces_ref, sems[:3]), Line(planes, out_weight_ref, w_out_ref, sems[3:], same=True)
+    greet(swap.near + line.near)
+    line.start()
     for i in range(TEAM):
         made[i] = slices(w_ref, [s * HEADS + z * TEAM + i for s in range(3) for z in range(planes)], HEAD_DIM)
-    greet(swap.near)
     swap.start()
-    gather.start()
     swap.finish()
-    gather.finish()
-
-
-def opening(weight, small, planes, cid):
+    line.finish()
+
+
+def opening(weight, out_weight, planes, cid):
     shape = (TEAM, weight.shape[0], weight.shape[1] // TEAM)
     return pl.pallas_call(
         functools.partial(open_kernel, planes),
-        out_shape=[jax.ShapeDtypeStruct(shape, BF16), jax.ShapeDtypeStruct((TEAM,) + small.shape, BF16)],
+        out_shape=[
+            jax.ShapeDtypeStruct(shape, BF16),
+            jax.ShapeDtypeStruct((planes,) + out_weight.shape, BF16),
+        ],
         in_specs=[VMEM, ANY],
         out_specs=[ANY, ANY],
-        scratch_shapes=[pltpu.VMEM(shape, BF16)] + Swap.sems * 2,
-        cost_estimate=lasting(15),
+        scratch_shapes=[pltpu.VMEM(shape, BF16)] + Swap.sems + Line.sems(planes),
+        cost_estimate=lasting(22),
         compiler_params=params(cid),
-    )(weight, small)
-
-
-def second_kernel(planes, gate_ref, up_ref, x_ref, _, pieces_ref, x_all_ref, made, *sems):
-    swap, gather = Swap(made, pieces_ref, sems[:3]), Gather(x_ref, x_all_ref, sems[3:])
-    greet(swap.near)
+    )(weight, out_weight)
+
+
+def second_kernel(
+    planes, gate_ref, up_ref, x_ref, small_ref, place_ref, _, pieces_ref, x_all_ref, all_ref, places_ref, made, *sems
+):
+    plane = place()[1] // TEAM
+    swap, gather = Swap(made, pieces_ref, sems[:3]), Gather(x_ref, x_all_ref, sems[3:10])
+    vectors = Swap(small_ref, all_ref.at[plane], sems[10:13], same=True)
+    places = Swap(place_ref, places_ref, sems[13:16], same=True, near_first=True)
+    line = Line(planes, all_ref.at[plane], all_ref, sems[16:], same=True, within=True)
+    greet(swap.near + line.near)
+    vectors.start()
+    places.start()
     gather.start()
     size = gate_ref.shape[1] // (planes * TEAM)
     for i in range(TEAM):
         units = [z * TEAM + i for z in range(planes)]
         made[i] = jnp.concatenate([slices(gate_ref, units, size), slices(up_ref, units, size)], axis=1)
     swap.start()
+    vectors.finish()
+    line.start()
     gather.middle()
     gather.finish()
     swap.finish()
-
-
-def second(gate, up, inputs, after, planes, cid):
+    places.finish()
+    line.finish()
+
+
+def second(gate, up, inputs, small, positions, after, planes, cid):
     shape = (TEAM, gate.shape[0], 2 * gate.shape[1] // TEAM)
     return pl.pallas_call(
         functools.partial(second_kernel, planes),
-        out_shape=[jax.ShapeDtypeStruct(shape, BF16), jax.ShapeDtypeStruct((TEAM,) + inputs.shape, BF16)],
-        in_specs=[VMEM, VMEM, ANY, ANY],
-        out_specs=[ANY, ANY],
-        scratch_shapes=[pltpu.VMEM(shape, BF16)] + Swap.sems + Gather.sems,
-        cost_estimate=lasting(55),
+        out_shape=[
+            jax.ShapeDtypeStruct(shape, BF16),
+            jax.ShapeDtypeStruct((TEAM,) + inputs.shape, BF16),
+            jax.ShapeDtypeStruct((planes, TEAM) + small.shape, BF16),
+            jax.ShapeDtypeStruct((TEAM,) + positions.shape, BF16),
+        ],
+        in_specs=[VMEM, VMEM] + [ANY] * 4,
+        out_specs=[ANY] * 4,
+        scratch_shapes=[pltpu.VMEM(shape, BF16)]
+        + Swap.sems
+        + Gather.sems
+        + Swap.sems * 2
+        + Line.sems(planes),
+        cost_estimate=lasting(60),
         compiler_params=params(cid),
-    )(gate, up, inputs, after)
-
-
-def close_kernel(parts, planes, x_ref, _, *refs):
-    outs, held, sems = refs[:-4], refs[-4], refs[-3:]
-    swap = Swap(x_ref, held, sems)
+    )(gate, up, inputs, small, positions, after)
+
+
+def unslice(held, parts, planes, outs):
+    size = held.shape[2] // (parts * planes)
+    for at in range(parts * planes):
+        row = jnp.concatenate([held[i, :, at * size : (at + 1) * size] for i in range(TEAM)], axis=1)
+        out, first = (outs[at // planes], at % planes) if len(outs) > 1 else (outs[0], at)
+        out[:, first * TEAM * size : (first + 1) * TEAM * size] = row.astype(F32)
+
+
+def added(ref):
+    total = ref[0].astype(F32)
+    for i in range(1, ref.shape[0]):
+        total = total + ref[i].astype(F32)
+    return total
+
+
+def vectors_kernel(planes, x_ref, o_ref, held, block, far, *sems):
+    swap, line = Swap(x_ref, held, sems[:3]), Line(planes, block, far, sems[3:])
+    greet(swap.near + line.near)
+    swap.start()
+    swap.finish()
+    block[...] = added(held)
+    line.start()
+    line.finish()
+    o_ref[...] = added(far)
+
+
+def vector_sums(x, cid):
+    planes = x.shape[1]
+    return pl.pallas_call(
+        functools.partial(vectors_kernel, planes),
+        out_shape=jax.ShapeDtypeStruct(x.shape[2:], F32),
+        in_specs=[VMEM],
+        out_specs=VMEM,
+        scratch_shapes=[pltpu.VMEM(x.shape, F32), pltpu.VMEM(x.shape[1:], F32), pltpu.VMEM(x.shape[1:], F32)]
+        + Swap.sems
+        + Line.sems(planes),
+        cost_estimate=lasting(10),
+        compiler_params=params(cid),
+    )(x)
+
+
+def close_kernel(planes, w_ref, _, out_ref, pieces, *sems):
+    swap = Swap(w_ref, pieces, sems)
     greet(swap.near)
     swap.start()
     swap.finish()
-    size = held.shape[2] // (parts * planes)
-    for part in range(parts):
-        for z in range(planes):
-            at = part * planes + z
-            row = jnp.concatenate([held[i, :, at * size : (at + 1) * size] for i in range(TEAM)], axis=1)
-            out, first = (outs[part], z) if len(outs) > 1 else (outs[0], at)
-            out[:, first * TEAM * size : (first + 1) * TEAM * size] = row.astype(F32)
-
-
-def closing(blocks, after, parts, outs, planes, cid):
+    unslice(pieces, 3, planes, [out_ref])
+
+
+def closing(blocks, after, planes, cid):
     _, depth, width = blocks.shape
     return pl.pallas_call(
-        functools.partial(close_kernel, parts, planes),
-        out_shape=[jax.ShapeDtypeStruct((depth, TEAM * width // outs), F32)] * outs,
+        functools.partial(close_kernel, planes),
+        out_shape=jax.ShapeDtypeStruct((depth, TEAM * width), F32),
         in_specs=[ANY, ANY],
-        out_specs=[VMEM] * outs,
+        out_specs=VMEM,
         scratch_shapes=[pltpu.VMEM(blocks.shape, BF16)] + Swap.sems,
-        cost_estimate=lasting(18),
+        cost_estimate=lasting(14),
         compiler_params=params(cid),
     )(blocks, after)
-
-
-def vectors_kernel(planes, x_ref, _, o_ref, held, block, far, *sems):
-    own_sem, send, recv = sems[3:]
-    mine, base, _, _ = place()
-    plane = base // TEAM
-    swap = Swap(x_ref, held, sems[:3])
-    others = [lax.rem(plane + k, planes) for k in range(1, planes)]
-    greet(swap.near + [other * TEAM + mine for other in others])
-    swap.start()
-    swap.finish()
-    total = held[0]
-    for i in range(1, TEAM):
-        total = total + held[i]
-    block[...] = total
-    copies = [
-        remote(block.at[other], far.at[plane], send.at[k], recv.at[k], other * TEAM + mine)
-        for k, other in enumerate(others)
-    ]
-    copies.append(pltpu.make_async_copy(block.at[plane], far.at[plane], own_sem))
-    for copy in copies:
-        copy.start()
-    for copy in copies:
-        copy.wait()
-    total = far[0]
-    for i in range(1, planes):
-        total = total + far[i]
-    o_ref[...] = total
-
-
-def vector_sums(x, after, cid):
-    planes = x.shape[1]
-    many = pltpu.SemaphoreType.DMA((planes,))
-    return pl.pallas_call(
-        functools.partial(vectors_kernel, planes),
-        out_shape=jax.ShapeDtypeStruct(x.shape[2:], F32),
-        in_specs=[VMEM, ANY],
-        out_specs=VMEM,
-        scratch_shapes=[pltpu.VMEM(x.shape, F32), pltpu.VMEM(x.shape[1:], F32), pltpu.VMEM(x.shape[1:], F32)]
-        + Swap.sems
-        + [pltpu.SemaphoreType.DMA, many, many],
-        cost_estimate=lasting(10),
-        compiler_params=params(cid),
-    )(x, after)
 
 
 class Gather:
@@ -215,27 +266,25 @@
 
     def __init__(self, src, out, sems):
         send, recv, hop_send, hop_recv, pass_send, pass_recv, own_sem = sems
-        mine, base, chip, core = place()
-        side, over, across = (chip_at(chip, k) * 2 + core for k in (1, 2, 3))
+        _, base, chip, core = place()
+        side, over = (chip_at(chip, k) * 2 + core for k in (1, 2))
         self.sibling = base + chip * 2 + 1 - core
         self.near = [base + side, base + over, self.sibling]
         half = src.shape[0] // 2
         top, low = pl.ds(0, half), pl.ds(half, half)
         self.first = [
-            remote(src.at[part], out.at[mine, part], send.at[i], recv.at[i], base + to)
-            for i, (part, to) in enumerate(((top, side), (low, over), (low, side), (top, over)))
+            remote(src.at[part], out.at[at, part], send.at[i], recv.at[i], base + to)
+            for i, (part, at, to) in enumerate(((top, 2, side), (low, 4, over), (low, 2, side), (top, 4, over)))
         ]
-        self.first.append(remote(src, out.at[mine], send.at[4], recv.at[4], self.sibling))
-        self.own = pltpu.make_async_copy(src, out.at[mine], own_sem)
+        self.first.append(remote(src, out.at[1], send.at[4], recv.at[4], self.sibling))
+        self.own = pltpu.make_async_copy(src, out.at[0], own_sem)
         self.hops = [
-            remote(out.at[at, part], out.at[at, part], hop_send.at[i], hop_recv.at[i], base + to)
-            for i, (at, part, to) in enumerate(((side, top, over), (over, low, side)))
+            remote(out.at[at, part], out.at[6, part], hop_send.at[i], hop_recv.at[i], base + to)
+            for i, (at, part, to) in enumerate(((2, top, over), (4, low, side)))
         ]
         self.passed = [
-            remote(out.at[at, part], out.at[at, part], pass_send.at[i], pass_recv.at[i], self.sibling)
-            for i, (at, part) in enumerate(
-                ((side, top), (over, low), (side, low), (over, top), (across, top), (across, low))
-            )
+            remote(out.at[at, part], out.at[at + 1, part], pass_send.at[i], pass_recv.at[i], self.sibling)
+            for i, (at, part) in enumerate(((2, top), (4, low), (2, low), (4, top), (6, top), (6, low)))
         ]
 
     def start(self):
@@ -250,18 +299,31 @@
             self.passed[i].start()
 
     def finish(self):
-        for i in (2, 3):
-            self.first[i].wait_recv()
-            self.passed[i].start()
-        for i in (0, 1):
-            self.hops[i].wait_recv()
-            self.passed[4 + i].start()
-        for copy in self.first[:4] + self.hops:
+        for i in range(2, TEAM):
+            self.ready(i)
+        self.first[4].wait_recv()
+        self.own.wait()
+        self.sent()
+
+    def ready(self, i):
+        if i == 0:
+            self.own.wait()
+        elif i == 1:
+            self.first[4].wait_recv()
+        elif i == 6:
+            for j in (0, 1):
+                self.hops[j].wait_recv()
+                self.passed[4 + j].start()
+        elif i % 2 == 0:
+            self.first[1 + i // 2].wait_recv()
+            self.passed[1 + i // 2].start()
+        else:
+            for j in {3: (0, 2), 5: (1, 3), 7: (4, 5)}[i]:
+                self.passed[j].wait_recv()
+
+    def sent(self):
+        for copy in self.first + self.hops + self.passed:
             copy.wait_send()
-        self.first[4].wait()
-        self.own.wait()
-        for copy in self.passed:
-            copy.wait()
 
 
 class Sum:
@@ -275,20 +337,19 @@
         self.own, self.beside, self.via, self.far = scratch
         load_sem, near_send, near_recv, via_send, via_recv, far_send, far_recv = sems
         _, base, chip, core = place()
-        chips = [chip_at(chip, k) for k in range(4)]
         sibling = base + chip * 2 + 1 - core
-        side, over = (base + chips[k] * 2 + core for k in (1, 2))
+        side, over = (base + chip_at(chip, k) * 2 + core for k in (1, 2))
         self.near = [side, over, sibling]
         self.half = self.own.shape[1] // 2
         top, low = pl.ds(0, self.half), pl.ds(self.half, self.half)
         self.loads = [
-            pltpu.make_async_copy(blocks.at[chips[k] * 2 + core], self.own.at[k], load_sem.at[k])
+            pltpu.make_async_copy(blocks.at[2 * k], self.own.at[k], load_sem.at[k])
             for k in range(4)
             if away is None
         ]
 
         def near_copy(k):
-            src = blocks.at[chips[k] * 2 + 1 - core] if away is None else away.at[k]
+            src = blocks.at[2 * k + 1] if away is None else away.at[k]
             return remote(src, self.beside.at[k], near_send.at[k], near_recv.at[k], sibling)
 
         self.near_copy = near_copy
@@ -401,75 +462,189 @@
     )(part, inputs, gain, bias)
 
 
-def mid_back_kernel(grads_ref, w_ref, resid_ref, g_ref, gain_ref, _, __, out_ref, sums_ref, o_ref, block, away, *scratch):
+def expand_kernel(h_ref, w_ref, pre_ref, hidden_ref):
+    pre = dot(h_ref[0], w_ref[...])
+    pre_ref[0] = pre
+    ff = hidden_ref.shape[2]
+    gate_pre, up_pre = pre[:, :ff], pre[:, ff:]
+    hidden_ref[0] = (gate_pre * jax.nn.sigmoid(gate_pre) * up_pre).astype(BF16)
+
+
+def expand(h_two, w_both):
+    seqs, rows, _ = h_two.shape
+    width = w_both.shape[1]
+    return pl.pallas_call(
+        expand_kernel,
+        grid=(seqs,),
+        in_specs=[per_seq(rows, D), whole(D, width)],
+        out_specs=[per_seq(rows, width), per_seq(rows, width // 2)],
+        out_shape=[
+            jax.ShapeDtypeStruct((seqs, rows, width), F32),
+            jax.ShapeDtypeStruct((seqs, rows, width // 2), BF16),
+        ],
+        cost_estimate=lasting(18),
+        compiler_params=params(),
+    )(h_two, w_both)
+
+
+def mlp_back_kernel(
+    pre_ref, g_all_ref, h_ref, wd_ref, w_ref, resid_ref, g_ref, gain_ref, _,
+    out_ref, sums_ref, block_ref, grad_w_ref,
+    pre, g_all, turned, made, grads, away, w, resid, own_grad, *scratch,
+):
+    pre_sem, g_sem, turned_sem, made_sem, late_sem = scratch[11:]
     total = Sum(None, scratch[:4], scratch[4:11], away)
-    gather = Gather(block, o_ref, scratch[11:])
+    rows, ff = pre_ref.shape[1], wd_ref.shape[0]
+    chunk = turned.shape[2]
+
+    def loads(i):
+        slot, at = lax.rem(i, 2), TEAM - 1 - i
+        return (
+            pltpu.make_async_copy(pre_ref.at[at], pre.at[slot], pre_sem.at[slot]),
+            pltpu.make_async_copy(g_all_ref.at[at], g_all.at[slot], g_sem.at[slot]),
+        )
+
+    def load_chunk(i):
+        slot = lax.rem(i, 2)
+        columns = pl.ds(pl.multiple_of(i * chunk, chunk), chunk)
+        return pltpu.make_async_copy(h_ref.at[:, columns], turned.at[slot], turned_sem.at[slot])
+
+    def store_chunk(i):
+        slot = lax.rem(i, 2)
+        part = pl.ds(pl.multiple_of(i * chunk, chunk), chunk)
+        return pltpu.make_async_copy(made.at[slot], grad_w_ref.at[part, :], made_sem.at[slot])
+
+    for copy in loads(0):
+        copy.start()
+    late = [
+        pltpu.make_async_copy(src, dst, late_sem.at[i])
+        for i, (src, dst) in enumerate(((w_ref, w), (resid_ref, resid), (g_ref, own_grad)))
+    ]
+    for copy in late:
+        copy.start()
     greet(total.near)
-    _, _, chip, core = place()
-    tile = 512
-
-    @pl.loop(0, 8)
+
+    @pl.loop(0, TEAM)
     def _(i):
-        k = 3 - i // 2
-        at = lax.rem(chip // 2 + k // 2, 2) * 2 + lax.rem(chip + k, 2)
-
-        def make(to, at):
-            @pl.loop(0, w_ref.shape[0] // tile)
-            def _(j):
-                columns = pl.ds(pl.multiple_of(j * tile, tile), tile)
-                to[k, :, columns] = dot(grads_ref[at], w_ref[columns, :], NT).astype(BF16)
+        slot = lax.rem(i, 2)
+        k, at = 3 - i // 2, TEAM - 1 - i
+
+        @pl.when(i < TEAM - 1)
+        def _():
+            for copy in loads(i + 1):
+                copy.start()
+
+        for copy in loads(i):
+            copy.wait()
+        grad_hidden = dot(g_all[slot], wd_ref[...], NT)
+        gate_pre, up_pre = pre[slot, :, :ff], pre[slot, :, ff:]
+        sigmoid = jax.nn.sigmoid(gate_pre)
+        grad_gate = grad_hidden * up_pre * sigmoid * (1.0 + gate_pre * (1.0 - sigmoid))
+        grad_up = grad_hidden * (gate_pre * sigmoid)
+        part = pl.ds(pl.multiple_of(at * rows, rows), rows)
+        grads[part, :] = jnp.concatenate([grad_gate, grad_up], axis=1).astype(BF16)
+
+        def make(to):
+            to[k] = dot(grads[part, :], w[...], NT).astype(BF16)
+
+        pl.when(i == 0)(late[0].wait)
 
         @pl.when(lax.rem(i, 2) == 0)
         def _():
-            make(away, at * 2 + 1 - core)
+            make(away)
             total.near_copy(k).start()
 
         @pl.when(lax.rem(i, 2) == 1)
         def _():
-            make(total.own, at * 2 + core)
-
-        for step, advance in ((3, total.middle_a), (5, total.middle_b), (7, total.middle_c)):
+            make(total.own)
+
+        for step, advance in ((1, total.middle_a), (3, total.middle_b), (5, total.middle_c)):
             pl.when(i == step)(advance)
 
+    load_chunk(0).start()
     total.middle_two()
+    chunks = h_ref.shape[1] // chunk
+
+    @pl.loop(0, chunks)
+    def _(i):
+        slot = lax.rem(i, 2)
+
+        @pl.when(i < chunks - 1)
+        def _():
+            load_chunk(i + 1).start()
+
+        load_chunk(i).wait()
+
+        @pl.when(i >= 2)
+        def _():
+            store_chunk(i - 2).wait()
+
+        made[slot] = dot(turned[slot], grads[...], TN).astype(BF16)
+        store_chunk(i).start()
+
     sums_ref[...] = jnp.zeros_like(sums_ref)
+    for copy in late[1:]:
+        copy.wait()
 
     def use(rows, value):
-        normed, inverse = normalize(resid_ref[rows, :])
+        normed, inverse = normalize(resid[rows, :])
         sums_ref[:8, :] += fold(value * normed)
         sums_ref[8:, :] += fold(value)
-        grad = g_ref[rows, :].astype(F32) + norm_back(value * gain_ref[...], normed, inverse)
+        grad = own_grad[rows, :].astype(F32) + norm_back(value * gain_ref[...], normed, inverse)
         out_ref[rows, :] = grad
-        block[rows, :] = grad.astype(BF16)
+        block_ref[rows, :] = grad.astype(BF16)
 
     total.finish(use)
-    gather.start()
-    gather.middle()
-    gather.finish()
-
-
-def mid_back(grads, w_both, resid, out_grad, gain, after, then, cid):
-    rows, width = resid.shape
+    store_chunk(chunks - 2).wait()
+    store_chunk(chunks - 1).wait()
+
+
+def mlp_back(pre, g_all, h_two, w_down, w_both, resid, out_grad, gain, after, cid):
+    seqs, rows, both = pre.shape
+    width = resid.shape[1]
+    chunk = 256
+    two = pltpu.SemaphoreType.DMA((2,))
     return pl.pallas_call(
-        mid_back_kernel,
+        mlp_back_kernel,
         out_shape=[
             jax.ShapeDtypeStruct((rows, width), F32),
             jax.ShapeDtypeStruct((16, width), F32),
-            jax.ShapeDtypeStruct((TEAM, rows, width), BF16),
+            jax.ShapeDtypeStruct((rows, width), BF16),
+            jax.ShapeDtypeStruct((width, both), BF16),
         ],
-        in_specs=[VMEM, VMEM, VMEM, VMEM, VMEM, ANY, ANY],
-        out_specs=[VMEM, VMEM, ANY],
-        scratch_shapes=[pltpu.VMEM((rows, width), BF16), pltpu.VMEM((4, rows, width), BF16)] + Sum.scratch(rows, width) + Sum.sems + Gather.sems,
-        cost_estimate=lasting(87),
+        in_specs=[ANY, ANY, ANY, VMEM, ANY, ANY, ANY, VMEM, ANY],
+        out_specs=[VMEM, VMEM, VMEM, ANY],
+        scratch_shapes=[
+            pltpu.VMEM((2, rows, both), F32),
+            pltpu.VMEM((2, rows, width), BF16),
+            pltpu.VMEM((2, seqs * rows, chunk), BF16),
+            pltpu.VMEM((2, chunk, both), BF16),
+            pltpu.VMEM((seqs * rows, both), BF16),
+            pltpu.VMEM((4, rows, width), BF16),
+            pltpu.VMEM((width, both), BF16),
+            pltpu.VMEM((rows, width), F32),
+            pltpu.VMEM((rows, width), BF16),
+        ]
+        + Sum.scratch(rows, width)
+        + Sum.sems
+        + [two] * 4
+        + [pltpu.SemaphoreType.DMA((3,))],
+        cost_estimate=lasting(60),
         compiler_params=params(cid),
-    )(grads, w_both, resid, out_grad, gain, after, then)
-
-
-def last_kernel(part_ref, x_ref, grad_ref, gain_ref, _, out_ref, sums_ref, *scratch):
-    total = Sum(part_ref, scratch[:4], scratch[4:])
-    greet(total.near)
+    )(pre, g_all, h_two, w_down, w_both, resid, out_grad, gain, after)
+
+
+def last_kernel(
+    planes, part_ref, x_ref, grad_ref, gain_ref, both_ref, branch_ref,
+    out_ref, sums_ref, gate_ref, up_ref, wo_ref, held, far, *scratch,
+):
+    total = Sum(part_ref, scratch[:4], scratch[4:11])
+    swap, line = Swap(both_ref, held, scratch[11:14]), Line(planes, branch_ref, far, scratch[14:])
+    greet(swap.near + line.near)
     total.start()
+    line.start()
     total.middle()
+    swap.start()
     total.middle_two()
     sums_ref[...] = jnp.zeros_like(sums_ref)
 
@@ -480,19 +655,33 @@
         out_ref[rows, :] = grad_ref[rows, :] + norm_back(value * gain_ref[...], normed, inverse)
 
     total.finish(use)
-
-
-def last(part, inputs, grad_resid, gain, after, cid):
+    line.finish()
+    wo_ref[...] = added(far)
+    swap.finish()
+    unslice(held, 2, planes, [gate_ref, up_ref])
+
+
+def last(part, inputs, grad_resid, gain, both, branch, cid):
     rows, width = inputs.shape
+    planes, depth, _ = branch.shape
     return pl.pallas_call(
-        last_kernel,
-        out_shape=[jax.ShapeDtypeStruct((rows, width), F32), jax.ShapeDtypeStruct((16, width), F32)],
-        in_specs=[ANY, VMEM, VMEM, VMEM, ANY],
-        out_specs=[VMEM, VMEM],
-        scratch_shapes=Sum.scratch(rows, width) + Sum.sems,
-        cost_estimate=lasting(47),
+        functools.partial(last_kernel, planes),
+        out_shape=[
+            jax.ShapeDtypeStruct((rows, width), F32),
+            jax.ShapeDtypeStruct((16, width), F32),
+        ]
+        + [jax.ShapeDtypeStruct((depth, both.shape[2] * TEAM // 2), F32)] * 2
+        + [jax.ShapeDtypeStruct((depth, width), F32)],
+        in_specs=[ANY, VMEM, VMEM, VMEM, ANY, ANY],
+        out_specs=[VMEM] * 5,
+        scratch_shapes=[pltpu.VMEM(both.shape, BF16), pltpu.VMEM(branch.shape, BF16)]
+        + Sum.scratch(rows, width)
+        + Sum.sems
+        + Swap.sems
+        + Line.sems(planes),
+        cost_estimate=lasting(60),
         compiler_params=params(cid),
-    )(part, inputs, grad_resid, gain, after)
+    )(part, inputs, grad_resid, gain, both, branch)
 
 
 def dot(a, b, dims=((1,), (0,))):
@@ -625,20 +814,25 @@
 
 
 def attend_back_kernel(
-    g_ref, wo_ref, w_ref, qkv_ref, tab_ref, block_ref, resid_ref, _, gqkv_ref, part_ref, gb_ref, out_ref, *scratch
+    block_ref, wo_ref, w_ref, qkv_ref, tab_ref, attn_ref, down_ref, resid_ref, _,
+    gqkv_ref, part_ref, gb_ref, wo_grad_ref, out_ref, held, wo_grad, *scratch,
 ):
-    total = Sum(block_ref, scratch[:4], scratch[4:])
+    gather, block = Gather(block_ref, held, scratch[:7]), Sum(down_ref, scratch[7:11], scratch[11:])
     step = pl.program_id(0)
 
     @pl.when(step == 0)
     def _():
-        greet(total.near)
-        total.start()
-
-    pl.when(step == 1)(total.middle)
-    pl.when(step == TEAM - 3)(total.middle_two)
+        greet(gather.near)
+        gather.start()
+        block.start()
+        wo_grad[...] = jnp.zeros_like(wo_grad)
+
+    for i in range(TEAM):
+        pl.when(step == i)(functools.partial(gather.ready, i))
+    grad = held[step]
     width = LOCAL * HEAD_DIM
-    grad_att = dot(g_ref[0], wo_ref[...], NT).astype(BF16)
+    wo_grad[...] += dot(attn_ref[0], grad, TN)
+    grad_att = dot(grad, wo_ref[...], NT).astype(BF16)
     query, key, value = (qkv_ref[0, :, i * width : (i + 1) * width] for i in range(3))
     allowed = visible(tab_ref[0, 2])
     zero = jnp.zeros((query.shape[0], width), F32)
@@ -664,38 +858,49 @@
     def use(rows, value):
         out_ref[rows, :] = (resid_ref[rows, :] + value).astype(BF16)
 
+    pl.when(step == 1)(gather.middle)
+    pl.when(step == 3)(block.middle)
+    pl.when(step == 6)(block.middle_two)
+
     @pl.when(step == TEAM - 1)
     def _():
-        total.finish(use)
-
-
-def attend_back(g_all, w_out, w_qkv, qkv, tables, blocks, resid, after, cid):
-    seqs, rows, _ = g_all.shape
+        wo_grad_ref[...] = wo_grad[...].astype(BF16)
+        block.finish(use)
+        gather.sent()
+
+
+def attend_back(block, w_out, w_qkv, qkv, tables, attn, down, resid, after, cid):
+    seqs, rows, _ = qkv.shape
     width = LOCAL * HEAD_DIM
     return pl.pallas_call(
         attend_back_kernel,
         grid=(seqs,),
         in_specs=[
-            per_seq(rows, D),
+            ANY,
             whole(width, D),
             whole(D, 3 * width),
             per_seq(rows, 3 * width),
             per_seq(3, rows, 128),
+            per_seq(rows, width),
             ANY,
             whole(rows, D),
             ANY,
         ],
-        out_specs=[per_seq(rows, 3 * width), per_seq(rows, D), per_seq(1, 3 * width), whole(rows, D)],
+        out_specs=[per_seq(rows, 3 * width), per_seq(rows, D), per_seq(1, 3 * width), whole(width, D), whole(rows, D)],
         out_shape=[
             jax.ShapeDtypeStruct((seqs, rows, 3 * width), BF16),
             jax.ShapeDtypeStruct((seqs, rows, D), BF16),
             jax.ShapeDtypeStruct((seqs, 1, 3 * width), F32),
+            jax.ShapeDtypeStruct((width, D), BF16),
             jax.ShapeDtypeStruct((rows, D), BF16),
         ],
-        scratch_shapes=Sum.scratch(rows, D) + Sum.sems,
-        cost_estimate=lasting(47),
+        scratch_shapes=[pltpu.VMEM((seqs, rows, D), BF16), pltpu.VMEM((width, D), F32)]
+        + Gather.sems
+        + Sum.scratch(rows, D)
+        + Sum.sems,
+        cost_estimate=lasting(65),
         compiler_params=params(cid),
-    )(g_all, w_out, w_qkv, qkv, tables, blocks, resid, after)
+    )(block, w_out, w_qkv, qkv, tables, attn, down, resid, after)
 
 
 def team_shards(
@@ -718,23 +923,21 @@
     def line_sum(x):
         return lax.psum_scatter(x, "fsdp", scatter_dimension=0, tiled=True, axis_index_groups=lines)
 
-    w_out = line_gather(out_weight)
-    small = jnp.concatenate([norm1_gain, norm1_bias, norm2_gain, norm2_bias, qkv_bias])
-    small = jnp.zeros((16, 2 * rows), BF16).at[0, : small.shape[0]].set(small).at[1, :rows].set(positions.astype(BF16))
-    pieces, small = opening(qkv_weight, small, planes, 0)
-    places = small[:, 1, :rows].astype(F32)
-    vectors = jnp.zeros((16 * 3 * width,), BF16).at[: TEAM * 2 * rows].set(small[:, 0].reshape(-1))
-    pieces = jnp.concatenate([pieces.reshape(TEAM * depth, 3 * width), vectors.reshape(16, 3 * width)])
-    gathered = line_gather(pieces).reshape(planes, TEAM * depth + 16, 3 * width)
-    w_qkv = gathered[:, : TEAM * depth].reshape(D, 3 * width)
-    vectors = gathered[:, TEAM * depth :].reshape(planes, -1)[:, : TEAM * 2 * rows].reshape(n, 2 * rows).astype(F32)
-    gain_one, bias_one, gain_two, bias_two = (vectors[:, i * depth : (i + 1) * depth].reshape(1, D) for i in range(4))
-    b_qkv = vectors[:, 4 * depth : 4 * depth + qkv_bias.shape[0]].reshape(3, planes, TEAM, HEAD_DIM)
-    b_qkv = lax.dynamic_index_in_dim(b_qkv, mine, 2, keepdims=False).reshape(1, 3 * width)
-
-    both, x_all = second(gate_weight, up_weight, inputs, w_out, planes, 1)
+    pieces, w_out = opening(qkv_weight, out_weight, planes, 0)
+    w_out = w_out.reshape(width, D)
+    w_qkv = line_gather(pieces.reshape(TEAM * depth, 3 * width))
+    small = jnp.stack([norm1_gain, norm1_bias, norm2_gain, norm2_bias])
+    small = jnp.concatenate([small, qkv_bias.reshape(-1, depth)])
+    small = jnp.pad(small, ((0, 16 - small.shape[0]), (0, 128 - depth)))
+    places = jnp.pad(positions.reshape(-1, 128).astype(BF16), ((0, 16 - rows // 128), (0, 0)))
+    both, x_all, small, places = second(gate_weight, up_weight, inputs, small, places, pieces, planes, 1)
     w_both = line_gather(both.reshape(TEAM * depth, 2 * planes * ff))
     w_down = line_gather(down_weight)
+    vectors = small.reshape(n, 16, 128)[:, :, :depth].astype(F32)
+    gain_one, bias_one, gain_two, bias_two = (vectors[:, i].reshape(1, D) for i in range(4))
+    b_qkv = vectors[:, 4 : 4 + 3 * planes * TEAM * HEAD_DIM // (n * depth)].reshape(3, planes, TEAM, HEAD_DIM)
+    b_qkv = lax.dynamic_index_in_dim(b_qkv, mine, 2, keepdims=False).reshape(1, 3 * width)
+    places = places.reshape(TEAM, -1)[:, :rows].astype(F32)
 
     half = ROT // 2
     frequency = 10000.0 ** (-jnp.arange(half, dtype=F32) / half)
@@ -745,32 +948,25 @@
 
     h_one, qkv, attn_low, part, g_all = attend(x_all, gain_one, bias_one, w_qkv, b_qkv, w_out, tables, out_grad, 3)
     resid, h_two = mid(part, inputs, gain_two, bias_two, 4)
-    h_two = h_two.reshape(tokens, D)
-    g_rows = g_all.reshape(tokens, D)
-    pre = dot(h_two, w_both)
-    gate_pre, up_pre = pre[:, : planes * ff], pre[:, planes * ff :]
-    sigmoid = jax.nn.sigmoid(gate_pre)
-    silu = gate_pre * sigmoid
-    hidden = (silu * up_pre).astype(BF16)
-    grad_down = dot(hidden, g_rows, TN).astype(BF16)
-    g_rows, grad_down = lax.optimization_barrier((g_rows, grad_down))
+    pre, hidden = expand(h_two, w_both)
+    hidden = hidden.reshape(tokens, planes * ff)
+    grad_down = dot(hidden, g_all.reshape(tokens, D), TN).astype(BF16)
+    grad_resid, sums_two, block, grad_w_both = mlp_back(
+        pre, g_all, h_two.reshape(tokens, D), w_down, w_both, resid, out_grad, gain_two, grad_down, 5
+    )
     grad_down = line_sum(grad_down)
-    grad_hidden = dot(g_rows, w_down, NT)
-    grad_gate = (grad_hidden * up_pre * sigmoid * (1.0 + gate_pre * (1.0 - sigmoid))).astype(BF16)
-    grad_up = (grad_hidden * silu).astype(BF16)
-    grad_both = jnp.concatenate([grad_gate, grad_up], axis=1)
-    grad_w_both = dot(h_two, grad_both, TN).astype(BF16)
-    grads = grad_both.reshape(TEAM, rows, 2 * planes * ff)
-    grad_resid, sums_two, branch = mid_back(grads, w_both, resid, out_grad, gain_two, grad_w_both, grad_down, 5)
     grad_w_both = line_sum(grad_w_both)
-    grad_out = dot(attn_low.reshape(tokens, width), branch.reshape(tokens, D), TN).astype(BF16)
-    part = dot(hidden, w_down).astype(BF16).reshape(TEAM, rows, D)
-    grad_qkv, part, grad_bias, block_out = attend_back(branch, w_out, w_qkv, qkv, tables, part, resid, grad_out, 6)
-    grad_out = line_sum(grad_out).astype(F32)
+    down = dot(hidden, w_down).astype(BF16).reshape(TEAM, rows, D)
+    grad_qkv, part, grad_bias, grad_out, block_out = attend_back(
+        block, w_out, w_qkv, qkv, tables, attn_low, down, resid, grad_down, 6
+    )
     grad_qkv = grad_qkv.reshape(tokens, 3 * width)
-    grad_qkv, grad_w_both = lax.optimization_barrier((grad_qkv, grad_w_both))
     grad_w_qkv = dot(h_one.reshape(tokens, D), grad_qkv, TN).astype(BF16)
-    input_grad, sums_one = last(part, inputs, grad_resid, gain_one, grad_w_qkv, 7)
+    part, grad_w_qkv, grad_w_both = lax.optimization_barrier((part, grad_w_qkv, grad_w_both))
+    input_grad, sums_one, grad_gate_w, grad_up_w, grad_out = last(
+        part, inputs, grad_resid, gain_one,
+        grad_w_both.reshape(TEAM, depth, 2 * planes * ff), grad_out.reshape(planes, depth, D), 7,
+    )
     grad_w_qkv = line_sum(grad_w_qkv)
 
     bias = jnp.zeros((3, planes, TEAM, HEAD_DIM), F32)
@@ -780,13 +976,10 @@
     sums = [jnp.sum(v[i : i + 8], axis=0).reshape(n, depth) for v in (sums_one, sums_two) for i in (0, 8)]
     sums = jnp.pad(jnp.concatenate(sums + [bias], axis=1), ((0, 0), (0, 1024 - 4 * depth - bias.shape[1])))
     sums = sums.reshape(planes, TEAM, 8, 128).transpose(1, 0, 2, 3)
-    sums = vector_sums(sums, input_grad, 8).reshape(-1)
+    sums = vector_sums(sums, 8)
+    grad_w_qkv = closing(grad_w_qkv.reshape(TEAM, depth, 3 * width), sums, planes, 9)
+    sums = sums.reshape(-1)
     sums = [sums[i * depth : (i + 1) * depth] for i in range(4)] + [sums[4 * depth : 4 * depth + bias.shape[1]]]
-
-    blocks = grad_w_both.reshape(TEAM, depth, 2 * planes * ff)
-    grad_gate_w, grad_up_w = closing(blocks, sums[0], 2, 2, planes, 9)
-    blocks = grad_w_qkv.reshape(TEAM, depth, 3 * width)
-    (grad_w_qkv,) = closing(blocks, grad_up_w, 3, 1, planes, 10)
     return (
         block_out,
         input_grad,

time: 626 us -> 544 us (0.87); the launches traced: 619 us -> 544 us
  matrix products: 88.2 us -> 32.9 us
  Pallas kernels: 441 us -> 464 us
  local copies, waits for them, and re-layouts: 35.8 us -> 19.6 us
  other arithmetic: 24.9 us -> 9.54 us
  waiting for transfers between devices: 14 us -> 3.55 us
    dot_general x7 -> x3, matrix products: 88.2 us -> 32.9 us  [dot(): return lax.dot_general(a, b, (dims, ((), ())), preferred_element_type=F32)]
    concatenate x2 -> x1, local copies, waits for them, and re-layouts: 11.9 us -> 0.73 us  [team_shards(): small = jnp.concatenate([small, qkv_bias.reshape(-1, depth)])]
    pallas_call x1, Pallas kernels: 17 us -> 26.6 us  [opening(): pl.pallas_call(functools.partial(open_kernel, planes), out_shape=[jax.Sha...]
    pallas_call x5, Pallas kernels: 225 us -> 234 us  [the longest x1 76.8 us: attend_back(): pl.pallas_call(attend_back_kernel, grid=(seqs,), in_specs=[ANY, whole(wid...]
    all_gather x4 -> x3, waiting for transfers between devices: 8.78 us -> 0.04 us  [line_gather(): lax.all_gather(x, 'fsdp', axis=0, tiled=True, axis_index_groups=lines)]
    concatenate x2 -> x0, other arithmetic: 8.27 us -> none  [the longest x1 6.2 us: team_shards(): grad_both = jnp.concatenate([grad_gate, grad_up], axis=1)]
    convert_element_type x5 -> x3, other arithmetic: 8.62 us -> 1.61 us  [the longest x1 0.92 us: team_shards(): vectors = small.reshape(n, 16, 128)[:, :, :depth].astype(F32)]
  transfers between devices with their start and end apart: 8 -> 6, of which waited for: 3 -> 1; matrix products, arithmetic and copies ran while one was open for 22% -> 10% of each run, Pallas kernels for 69% -> 78%
where the time goes in v3:
time: 544 us
  Pallas kernels  464 us (85%)
  matrix products  32.9 us (6%)
  local copies, waits for them, and re-layouts  19.6 us (4%)
  between operations  14.4 us (3%)
  other arithmetic  9.54 us (2%)
    pallas_call x1, Pallas kernels, mid(): pl.pallas_call(mid_kernel, out_shape=[jax.ShapeDtypeStruct((rows, width),...  85.2 us
    pallas_call x1, Pallas kernels, attend_back(): pl.pallas_call(attend_back_kernel, grid=(seqs,), in_specs=[ANY, whole(wid...  76.8 us
    pallas_call x1, Pallas kernels, last(): pl.pallas_call(functools.partial(last_kernel, planes), out_shape=[jax.Sha...  67.1 us
    pallas_call x1, Pallas kernels, second(): pl.pallas_call(functools.partial(second_kernel, planes), out_shape=[jax.S...  62 us
    pallas_call x1, Pallas kernels, mlp_back(): pl.pallas_call(mlp_back_kernel, out_shape=[jax.ShapeDtypeStruct((rows, wi...  56.7 us
    pallas_call x1, Pallas kernels, attend(): pl.pallas_call(attend_kernel, grid=(seqs,), in_specs=[per_seq(rows, D), w...  44.9 us
    dot_general x3, matrix products, dot(): return lax.dot_general(a, b, (dims, ((), ())), preferred_element_type=F32)  32.9 us
    pallas_call x1, Pallas kernels, opening(): pl.pallas_call(functools.partial(open_kernel, planes), out_shape=[jax.Sha...  26.6 us
  transfers between devices with their start and end apart: 6, of which 1 were waited for; matrix products, arithmetic and copies ran while one was open for 10% of the time, Pallas kernels for 78%

profile of v3, /device:TPU:0, one launch (start us, length us, event | category | flops | bytes accessed | tf_op | source)
XLA Modules:
  0.0 543.8 jit_solution(12809567380550536236)
XLA Ops:
  7.2 26.6 %shard_map.220 = (bf16[8,64,768]{2,1,0:T(8,128)(2,1)}, bf16[4,64,2048]{2,1,0:T(8,128)(2,1)}) custom-call(bf16[64,6144]{1,0:T(8,128)(2,1)} %w_ref.1, bf16[64,2048]{1,0:T(8,128)(2,1)} %out_weight_ref.1), custom_call_target="tpu_custom_call" | custom-call | bytes 79200000 | tf_op jit(solution)/shard_map/pallas_call | solution.py:138
  33.9 0.7 reshape.109
  34.6 0.7 concatenate.9
  35.4 0.6 pad.12.small_ref
  36.0 0.7 convert_bitcast_fusion
  36.6 0.6 pad.13.place_ref
  37.2 62.0 %shard_map.221 = (bf16[8,64,1408]{2,1,0:T(8,128)(2,1)}, bf16[8,256,2048]{2,1,0:T(8,128)(2,1)}, bf16[4,8,16,128]{3,2,1,0:T(8,128)(2,1)}, bf16[8,16,128]{2,1,0:T(8,128)(2,1)}) custom-call(bf16[64,5632]{1,0:T(8,128)(2,1)} %gate_ref.1, bf16[64,5632]{1,0:T(8,128)(2,1)} %up_ref.1, bf16[256,2048]{1,0:T(8,128)(2,1)} %x_ref.5, bf16[16,128]{1,0:T(8,128)(2,1)} %pad.12.small_ref, ...), custom_call_target="tpu_custom_call" | custom-call | bytes 216000000 | tf_op jit(solution)/shard_map/pallas_call | solution.py:180
  99.4 0.7 all-gather.8.cloned.1.call-update
  100.1 0.9 slice_convert_fusion
  101.1 0.7 reshape.113.b_ref
  101.8 0.8 copy.39
  102.6 0.2 slice_reduce_fusion.4
  102.8 0.7 reshape_squeeze.12.gain_ref
  103.4 0.7 reshape_squeeze.13.bias_ref
  104.1 0.7 reshape_squeeze.14.gain_ref
  104.8 0.7 reshape_squeeze.15.bias_ref
  105.5 0.1 concatenate.10
  105.6 3.7 multiply_cosine_fusion
  109.3 0.3 stack_broadcast_in_dim.2
  109.6 1.8 pad_maximum_fusion.tab_ref
  111.5 44.9 %shard_map.222 = (bf16[8,256,2048]{2,1,0:T(8,128)(2,1)}, bf16[8,256,768]{2,1,0:T(8,128)(2,1)}, bf16[8,256,256]{2,1,0:T(8,128)(2,1)}, bf16[8,256,2048]{2,1,0:T(8,128)(2,1)}, bf16[8,256,2048]{2,1,0:T(8,128)(2,1)}) custom-call(bf16[8,256,2048]{2,1,0:T(8,128)(2,1)} %get-tuple-element.45.x_ref, f32[1,2048]{1,0:T(1,128)} %reshape_squeeze.12.gain_ref, ...), custom_call_target="tpu_custom_call" | custom-call | bytes 158400000 | tf_op jit(solution)/shard_map/pallas_call | solution.py:789
  156.4 85.2 %shard_map.223 = (f32[256,2048]{1,0:T(8,128)}, bf16[8,256,2048]{2,1,0:T(8,128)(2,1)}) custom-call(bf16[8,256,2048]{2,1,0:T(8,128)(2,1)} %get-tuple-element.49.part_ref, bf16[256,2048]{1,0:T(8,128)(2,1)} %x_ref.5, f32[1,2048]{1,0:T(1,128)} %reshape_squeeze.14.gain_ref, f32[1,2048]{1,0:T(1,128)} %reshape_squeeze.15.bias_ref), custom_call_target="tpu_custom_call" | custom-call | bytes 306000000 | tf_op jit(solution)/shard_map/pallas_call | solution.py:454
  241.6 19.7 %shard_map.224 = (f32[8,256,1408]{2,1,0:T(8,128)}, bf16[8,256,704]{2,1,0:T(8,128)(2,1)}) custom-call(bf16[8,256,2048]{2,1,0:T(8,128)(2,1)} %get-tuple-element.50.h_ref, bf16[2048,1408]{1,0:T(8,128)(2,1)} %all-gather.6.cloned.1.call-done.w_ref), custom_call_target="tpu_custom_call" | custom-call | bytes 64800000 | tf_op jit(solution)/shard_map/pallas_call | solution.py:476
  261.3 10.7 %bitcast_convert_fusion.1._ = bf16[704,2048]{1,0:T(8,128)(2,1)} fusion(bf16[8,256,704]{2,1,0:T(8,128)(2,1)} %get-tuple-element.55, bf16[8,256,2048]{2,1,0:T(8,128)(2,1)} %get-tuple-element.53.g_all_ref), kind=kOutput, calls=%fused_computation.2 | convolution fusion | flops 5907021824 | bytes 14155776 | tf_op jit(solution)/shard_map/dot_general | solution.py:688
  272.1 56.7 %shard_map.225 = (f32[256,2048]{1,0:T(8,128)}, f32[16,2048]{1,0:T(8,128)}, bf16[256,2048]{1,0:T(8,128)(2,1)}, bf16[2048,1408]{1,0:T(8,128)(2,1)}) custom-call(f32[8,256,1408]{2,1,0:T(8,128)} %get-tuple-element.52.pre_ref, bf16[8,256,2048]{2,1,0:T(8,128)(2,1)} %get-tuple-element.53.g_all_ref, bf16[2048,2048]{1,0:T(8,128)(2,1)} %bitcast.41, ...), custom_call_target="tpu_custom_call" | custom-call | bytes 216000000 | tf_op jit(solution)/shard_map/pallas_call | solution.py:607
  328.9 1.7 copy-done.2
  330.6 10.8 %convolution_convert_fusion = bf16[2048,2048]{1,0:T(8,128)(2,1)} fusion(bf16[2048,704]{1,0:T(8,128)(2,1)} %bitcast.60, bf16[704,2048]{1,0:T(8,128)(2,1)S(1)} %copy-done.2), kind=kOutput, calls=%fused_computation | convolution fusion | flops 5909774336 | bytes 14155776 | tf_op jit(solution)/shard_map/dot_general | solution.py:688
  341.4 76.8 %shard_map.226 = (bf16[8,256,768]{2,1,0:T(8,128)(2,1)}, bf16[8,256,2048]{2,1,0:T(8,128)(2,1)}, f32[8,1,768]{2,1,0:T(1,128)}, bf16[256,2048]{1,0:T(8,128)(2,1)}, bf16[256,2048]{1,0:T(8,128)(2,1)}) custom-call(bf16[256,2048]{1,0:T(8,128)(2,1)} %get-tuple-element.56.block_ref, bf16[256,2048]{1,0:T(8,128)(2,1)} %bitcast.44, ...), custom_call_target="tpu_custom_call" | custom-call | bytes 234000000 | tf_op jit(solution)/shard_map/pallas_call | solution.py:875
  418.2 11.4 %bitcast_convert_fusion = bf16[2048,768]{1,0:T(8,128)(2,1)} fusion(bf16[8,256,2048]{2,1,0:T(8,128)(2,1)} %get-tuple-element.61, bf16[8,256,768]{2,1,0:T(8,128)(2,1)} %get-tuple-element.62), kind=kOutput, calls=%fused_computation.1 | convolution fusion | flops 6444023808 | bytes 14680064 | tf_op jit(solution)/shard_map/dot_general | solution.py:688
  429.6 2.7 reduce-scatter.6.cloned.1.call-done
  432.4 0.1 reshape.124
  432.6 0.1 reshape.126
  432.7 0.1 reshape.127
  432.8 1.3 convert_element_type.37
  434.0 67.1 %shard_map.227 = (f32[256,2048]{1,0:T(8,128)}, f32[16,2048]{1,0:T(8,128)}, f32[64,5632]{1,0:T(8,128)}, f32[64,5632]{1,0:T(8,128)}, f32[64,2048]{1,0:T(8,128)}) custom-call(bf16[8,256,2048]{2,1,0:T(8,128)(2,1)} %get-tuple-element.64.part_ref, bf16[256,2048]{1,0:T(8,128)(2,1)} %x_ref.5, f32[256,2048]{1,0:T(8,128)} %get-tuple-element.65.grad_ref, ...), custom_call_target="tpu_custom_call" | custom-call | bytes 216000000 | tf_op jit(solution)/shard_map/pallas_call | solution.py:667
  501.2 1.1 slice_reduce_fusion.2
  502.4 0.1 concatenate.11
  502.5 0.7 copy_bitcast_fusion.1.x_ref
  503.2 10.9 %shard_map.228._ = f32[8,128]{1,0:T(8,128)} custom-call(f32[8,4,8,128]{3,2,1,0:T(8,128)} %copy_bitcast_fusion.1.x_ref), custom_call_target="tpu_custom_call" | custom-call | bytes 36000000 | tf_op jit(solution)/shard_map/pallas_call | solution.py:228
  514.1 1.2 slice.61
  515.3 1.4 fusion
  516.7 13.7 %shard_map.229 = f32[64,6144]{1,0:T(8,128)} custom-call(bf16[8,64,768]{2,1,0:T(8,128)(2,1)} %bitcast.49, f32[8,128]{1,0:T(8,128)} %shard_map.228._), custom_call_target="tpu_custom_call" | custom-call | bytes 50400000 | tf_op jit(solution)/shard_map/pallas_call | solution.py:251
  530.4 1.0 copy.47
  531.4 1.3 copy.48
  532.7 1.1 copy.49
  533.9 0.8 copy.50
  534.7 1.1 copy.51
  535.8 1.1 copy.52
  (50 shorter events, 0.9 us)
Async XLA Ops:
  7.2 104.3 %all-gather.4.cloned.1.call-start = ((), (), s32[]{:S(2)}) async-start(), calls=%async_computation.3 | async-start | bytes 3932160 | tf_op jit(solution)/shard_map/all_gather | solution.py:921
  33.8 207.7 %all-gather.6.cloned.1.call-start = ((), (), s32[]{:S(2)}) async-start(), calls=%async_computation.4 | async-start | bytes 7208960 | tf_op jit(solution)/shard_map/all_gather | solution.py:921
  99.3 172.7 %all-gather.8.cloned.1.call-start = ((), (), s32[]{:S(2)}) async-start(), calls=%async_computation.5 | async-start | bytes 3604480 | tf_op jit(solution)/shard_map/all_gather | solution.py:921
  100.1 241.4 %reduce-scatter.4.cloned.1.call-start = ((), (), s32[]{:S(2)}) async-start(), calls=%async_computation.6 | async-start | bytes 3604480 | tf_op jit(solution)/shard_map/reduce_scatter | solution.py:924
  272.0 160.3 %reduce-scatter.6.cloned.1.call-start = ((), (), s32[]{:S(2)}) async-start(), calls=%async_computation.7 | async-start | bytes 7208960 | tf_op jit(solution)/shard_map/reduce_scatter | solution.py:924
  328.8 1.8 copy-start.2
  328.8 187.9 %reduce-scatter.8.cloned.1.call-start = ((), (), s32[]{:S(2)}) async-start(), calls=%async_computation.8 | async-start | bytes 3932160 | tf_op jit(solution)/shard_map/reduce_scatter | solution.py:924
  429.6 2.8 copy-start.8
  429.6 3.0 copy-start.9
  429.6 3.2 copy-start.1
  501.2 29.3 %copy-start.6 = (bf16[256,2048]{1,0:T(8,128)(2,1)S(1)}, bf16[256,2048]{1,0:T(8,128)(2,1)}, u32[]{:S(2)}) copy-start(bf16[256,2048]{1,0:T(8,128)(2,1)} %get-tuple-element.102) | copy-start | bytes 3145732
  501.2 30.2 %copy-start.3 = (f32[256,2048]{1,0:T(8,128)S(1)}, f32[256,2048]{1,0:T(8,128)}, u32[]{:S(2)}) copy-start(f32[256,2048]{1,0:T(8,128)} %get-tuple-element.103) | copy-start | bytes 6291460
  530.4 2.3 copy-start
  531.4 2.5 copy-start.7
  532.7 2.0 copy-start.5
  532.7 3.1 copy-start.4
Sparse Core Ops, SparseCore 0:
  34.0 69.8 all-gather.3
  105.4 105.2 all-gather.5
  212.3 57.4 all-gather.7
  272.1 55.8 reduce-scatter.3
  330.2 102.1 reduce-scatter.5
  434.5 76.9 reduce-scatter.7

commit v4 on v3

--- a/solution.py
+++ b/solution.py
@@ -2,6 +2,7 @@
 
 import jax
 import jax.numpy as jnp
+import numpy as np
 from jax import lax
 from jax.experimental import pallas as pl
 from jax.experimental.pallas import tpu as pltpu
@@ -118,46 +119,93 @@
             self.own.wait()
 
 
+class LineGather:
+    def sems(planes):
+        return [pltpu.SemaphoreType.DMA, pltpu.SemaphoreType.DMA((2, planes)), pltpu.SemaphoreType.DMA((2, planes))]
+
+    def __init__(self, planes, src, out, sems):
+        own_sem, self.send, self.recv = sems
+        mine, base, _, _ = place()
+        self.plane, self.planes, self.src, self.out = base // TEAM, planes, src, out
+        self.me = base + mine
+        self.near = [lax.rem(self.plane + k, planes) * TEAM + mine for k in (1, planes - 1)]
+        self.own = pltpu.make_async_copy(src, out.at[self.plane], own_sem)
+
+    def copy(self, way, stage):
+        step = 1 - 2 * way
+        block, to = self.plane - step * (stage - 1), self.plane + step
+        is_there = (block >= 0) & (block < self.planes) & (to >= 0) & (to < self.planes)
+        src = self.src if stage == 1 else self.out.at[block]
+        sems = self.send.at[way, stage], self.recv.at[way, stage]
+        return is_there, remote(src, self.out.at[block], *sems, self.me + step * TEAM)
+
+    def arrived(self, way, stage):
+        block = self.plane - (1 - 2 * way) * stage
+
+        @pl.when((block >= 0) & (block < self.planes))
+        def _():
+            dst = self.out.at[block]
+            remote(dst, dst, self.send.at[way, stage], self.recv.at[way, stage], self.me).wait_recv()
+
+    def start(self):
+        self.own.start()
+        self.stage(1)
+
+    def stage(self, stage):
+        for way in (0, 1):
+            if stage > 1:
+                self.arrived(way, stage - 1)
+            is_there, copy = self.copy(way, stage)
+            pl.when(is_there)(copy.start)
+
+    def finish(self):
+        self.own.wait()
+        for way in (0, 1):
+            self.arrived(way, self.planes - 1)
+            for stage in range(1, self.planes):
+                is_there, copy = self.copy(way, stage)
+                pl.when(is_there)(copy.wait_send)
+
+
 def slices(ref, pieces, size):
     return jnp.concatenate([ref[:, i * size : (i + 1) * size] for i in pieces], axis=1)
 
 
-def open_kernel(planes, w_ref, out_weight_ref, pieces_ref, w_out_ref, made, *sems):
-    swap, line = Swap(made, pieces_ref, sems[:3]), Line(planes, out_weight_ref, w_out_ref, sems[3:], same=True)
-    greet(swap.near + line.near)
-    line.start()
+def open_kernel(planes, w_ref, pieces_ref, made, *sems):
+    swap = Swap(made, pieces_ref, sems)
     for i in range(TEAM):
         made[i] = slices(w_ref, [s * HEADS + z * TEAM + i for s in range(3) for z in range(planes)], HEAD_DIM)
+    greet(swap.near)
     swap.start()
     swap.finish()
-    line.finish()
-
-
-def opening(weight, out_weight, planes, cid):
+
+
+def opening(weight, planes, cid):
     shape = (TEAM, weight.shape[0], weight.shape[1] // TEAM)
     return pl.pallas_call(
         functools.partial(open_kernel, planes),
-        out_shape=[
-            jax.ShapeDtypeStruct(shape, BF16),
-            jax.ShapeDtypeStruct((planes,) + out_weight.shape, BF16),
-        ],
-        in_specs=[VMEM, ANY],
-        out_specs=[ANY, ANY],
-        scratch_shapes=[pltpu.VMEM(shape, BF16)] + Swap.sems + Line.sems(planes),
-        cost_estimate=lasting(22),
+        out_shape=jax.ShapeDtypeStruct(shape, BF16),
+        in_specs=[VMEM],
+        out_specs=ANY,
+        scratch_shapes=[pltpu.VMEM(shape, BF16)] + Swap.sems,
+        cost_estimate=lasting(17),
         compiler_params=params(cid),
-    )(weight, out_weight)
+    )(weight)
 
 
 def second_kernel(
-    planes, gate_ref, up_ref, x_ref, small_ref, place_ref, _, pieces_ref, x_all_ref, all_ref, places_ref, made, *sems
+    planes, gate_ref, up_ref, x_ref, small_ref, place_ref, qkv_ref, rate_ref,
+    pieces_ref, x_all_ref, w_qkv_ref, tab_ref, norm_ref, b_ref, made, all_ref, places_ref, tables, *sems,
 ):
-    plane = place()[1] // TEAM
+    mine, base, _, _ = place()
+    plane = base // TEAM
     swap, gather = Swap(made, pieces_ref, sems[:3]), Gather(x_ref, x_all_ref, sems[3:10])
     vectors = Swap(small_ref, all_ref.at[plane], sems[10:13], same=True)
     places = Swap(place_ref, places_ref, sems[13:16], same=True, near_first=True)
-    line = Line(planes, all_ref.at[plane], all_ref, sems[16:], same=True, within=True)
+    line = Line(planes, all_ref.at[plane], all_ref, sems[16:19], same=True, within=True)
+    rows = LineGather(planes, qkv_ref, w_qkv_ref, sems[19:22])
     greet(swap.near + line.near)
+    rows.start()
     vectors.start()
     places.start()
     gather.start()
@@ -168,33 +216,77 @@
     swap.start()
     vectors.finish()
     line.start()
+    rows.stage(2)
+    places.finish()
+    square = (128, 128)
+
+    @pl.loop(0, TEAM)
+    def _(i):
+        known = places_ref[i].astype(F32)
+        for part in range(tables.shape[2] // 128):
+            at = jnp.transpose(jnp.broadcast_to(known[part : part + 1, :], square))
+            here = pl.ds(part * 128, 128)
+            angle = at * rate_ref[...]
+            tables[i, 0, here, :] = jnp.cos(angle)
+            tables[i, 1, here, :] = jnp.sin(angle)
+            token = lax.broadcasted_iota(jnp.int32, square, 0) + part * 128
+            tables[i, 2, here, :] = token.astype(F32) - at
+
+    store = pltpu.make_async_copy(tables, tab_ref, sems[22])
+    store.start()
     gather.middle()
+    for stage in range(3, planes):
+        rows.stage(stage)
+    line.finish()
+    depth = gate_ref.shape[0]
+    each = [all_ref[z, i].astype(F32) for z in range(planes) for i in range(TEAM)]
+    for i in range(4):
+        norm_ref[i : i + 1, :] = jnp.concatenate([known[i : i + 1, :depth] for known in each], axis=1)
+    per = qkv_ref.shape[1] * TEAM // (planes * TEAM * depth)
+    bias = []
+    for part in range(3):
+        for z in range(planes):
+            head = part * HEADS + z * TEAM + mine
+            known = all_ref[head // per // TEAM, lax.rem(head // per, TEAM)].astype(F32)
+            row = lax.broadcasted_iota(jnp.int32, known.shape, 0) == 4 + lax.rem(head, per)
+            bias.append(jnp.sum(jnp.where(row, known, 0.0), axis=0, keepdims=True)[:, :depth])
+    b_ref[...] = jnp.concatenate(bias, axis=1)
     gather.finish()
     swap.finish()
-    places.finish()
-    line.finish()
-
-
-def second(gate, up, inputs, small, positions, after, planes, cid):
+    rows.finish()
+    store.wait()
+
+
+def second(gate, up, inputs, small, positions, qkv, rate, planes, cid):
     shape = (TEAM, gate.shape[0], 2 * gate.shape[1] // TEAM)
+    tables = (TEAM, 3, inputs.shape[0], 128)
     return pl.pallas_call(
         functools.partial(second_kernel, planes),
         out_shape=[
             jax.ShapeDtypeStruct(shape, BF16),
             jax.ShapeDtypeStruct((TEAM,) + inputs.shape, BF16),
-            jax.ShapeDtypeStruct((planes, TEAM) + small.shape, BF16),
-            jax.ShapeDtypeStruct((TEAM,) + positions.shape, BF16),
+            jax.ShapeDtypeStruct((planes,) + qkv.shape, BF16),
+            jax.ShapeDtypeStruct(tables, F32),
+            jax.ShapeDtypeStruct((4, inputs.shape[1]), F32),
+            jax.ShapeDtypeStruct((1, qkv.shape[1]), F32),
         ],
-        in_specs=[VMEM, VMEM] + [ANY] * 4,
-        out_specs=[ANY] * 4,
-        scratch_shapes=[pltpu.VMEM(shape, BF16)]
+        in_specs=[VMEM] * 7,
+        out_specs=[ANY] * 4 + [VMEM] * 2,
+        scratch_shapes=[
+            pltpu.VMEM(shape, BF16),
+            pltpu.VMEM((planes, TEAM) + small.shape, BF16),
+            pltpu.VMEM((TEAM,) + positions.shape, BF16),
+            pltpu.VMEM(tables, F32),
+        ]
         + Swap.sems
         + Gather.sems
         + Swap.sems * 2
-        + Line.sems(planes),
-        cost_estimate=lasting(60),
+        + Line.sems(planes)
+        + LineGather.sems(planes)
+        + [pltpu.SemaphoreType.DMA],
+        cost_estimate=lasting(65),
         compiler_params=params(cid),
-    )(gate, up, inputs, small, positions, after)
+    )(gate, up, inputs, small, positions, qkv, rate)
 
 
 def unslice(held, parts, planes, outs):
@@ -205,6 +297,42 @@
         out[:, first * TEAM * size : (first + 1) * TEAM * size] = row.astype(F32)
 
 
+def both_kernel(planes, held_ref, gate_ref, up_ref):
+    unslice(held_ref, 2, planes, [gate_ref, up_ref])
+
+
+def both_grads(held, planes):
+    _, depth, width = held.shape
+    return pl.pallas_call(
+        functools.partial(both_kernel, planes),
+        out_shape=[jax.ShapeDtypeStruct((depth, width * TEAM // 2), F32)] * 2,
+        in_specs=[VMEM],
+        out_specs=[VMEM] * 2,
+        cost_estimate=lasting(4),
+        compiler_params=params(),
+    )(held)
+
+
+def rest_kernel(planes, held_ref, far_ref, w_ref, wo_ref):
+    unslice(held_ref, 3, planes, [w_ref])
+    wo_ref[...] = added(far_ref)
+
+
+def rest_grads(held, far):
+    _, depth, width = held.shape
+    return pl.pallas_call(
+        functools.partial(rest_kernel, far.shape[0]),
+        out_shape=[
+            jax.ShapeDtypeStruct((depth, width * TEAM), F32),
+            jax.ShapeDtypeStruct(far.shape[1:], F32),
+        ],
+        in_specs=[VMEM] * 2,
+        out_specs=[VMEM] * 2,
+        cost_estimate=lasting(4),
+        compiler_params=params(),
+    )(held, far)
+
+
 def added(ref):
     total = ref[0].astype(F32)
     for i in range(1, ref.shape[0]):
@@ -212,51 +340,30 @@
     return total
 
 
-def vectors_kernel(planes, x_ref, o_ref, held, block, far, *sems):
-    swap, line = Swap(x_ref, held, sems[:3]), Line(planes, block, far, sems[3:])
-    greet(swap.near + line.near)
+def close_kernel(planes, w_ref, block_ref, _, __, held_ref, vector_ref, beyond, *sems):
+    swap, outer = Swap(w_ref, held_ref, sems[:3]), Line(planes, block_ref, beyond, sems[3:])
+    greet(swap.near + outer.near)
+    outer.start()
     swap.start()
+    outer.finish()
     swap.finish()
-    block[...] = added(held)
-    line.start()
-    line.finish()
-    o_ref[...] = added(far)
-
-
-def vector_sums(x, cid):
-    planes = x.shape[1]
-    return pl.pallas_call(
-        functools.partial(vectors_kernel, planes),
-        out_shape=jax.ShapeDtypeStruct(x.shape[2:], F32),
-        in_specs=[VMEM],
-        out_specs=VMEM,
-        scratch_shapes=[pltpu.VMEM(x.shape, F32), pltpu.VMEM(x.shape[1:], F32), pltpu.VMEM(x.shape[1:], F32)]
-        + Swap.sems
-        + Line.sems(planes),
-        cost_estimate=lasting(10),
-        compiler_params=params(cid),
-    )(x)
-
-
-def close_kernel(planes, w_ref, _, out_ref, pieces, *sems):
-    swap = Swap(w_ref, pieces, sems)
-    greet(swap.near)
-    swap.start()
-    swap.finish()
-    unslice(pieces, 3, planes, [out_ref])
-
-
-def closing(blocks, after, planes, cid):
-    _, depth, width = blocks.shape
+    vector_ref[...] = added(beyond)
+
+
+def closing(blocks, sums, after, cid):
+    planes = sums.shape[0]
     return pl.pallas_call(
         functools.partial(close_kernel, planes),
-        out_shape=jax.ShapeDtypeStruct((depth, TEAM * width), F32),
-        in_specs=[ANY, ANY],
-        out_specs=VMEM,
-        scratch_shapes=[pltpu.VMEM(blocks.shape, BF16)] + Swap.sems,
-        cost_estimate=lasting(14),
+        out_shape=[
+            jax.ShapeDtypeStruct(blocks.shape, BF16),
+            jax.ShapeDtypeStruct(sums.shape[1:], F32),
+        ],
+        in_specs=[VMEM, VMEM, ANY, ANY],
+        out_specs=[ANY, VMEM],
+        scratch_shapes=[pltpu.VMEM(sums.shape, F32)] + Swap.sems + Line.sems(planes),
+        cost_estimate=lasting(16),
         compiler_params=params(cid),
-    )(blocks, after)
+    )(blocks, sums, *after)
 
 
 class Gather:
@@ -429,62 +536,80 @@
     return x[:8] + x[8:]
 
 
-def mid_kernel(part_ref, x_ref, gain_ref, bias_ref, resid_ref, o_ref, block, *scratch):
-    total = Sum(part_ref, scratch[:4], scratch[4:11])
-    gather = Gather(block, o_ref, scratch[11:])
-    greet(total.near)
-    total.start()
-    total.middle()
-    total.middle_two()
-
-    def use(rows, value):
-        resid = x_ref[rows, :].astype(F32) + value
-        resid_ref[rows, :] = resid
-        normed, _ = normalize(resid)
-        block[rows, :] = (normed * gain_ref[...] + bias_ref[...]).astype(BF16)
-
-    total.finish(use)
-    gather.start()
-    gather.middle()
-    gather.finish()
-
-
-def mid(part, inputs, gain, bias, cid):
-    rows, width = inputs.shape
-    return pl.pallas_call(
-        mid_kernel,
-        out_shape=[jax.ShapeDtypeStruct((rows, width), F32), jax.ShapeDtypeStruct((TEAM, rows, width), BF16)],
-        in_specs=[ANY, VMEM, VMEM, VMEM],
-        out_specs=[VMEM, ANY],
-        scratch_shapes=[pltpu.VMEM((rows, width), BF16)] + Sum.scratch(rows, width) + Sum.sems + Gather.sems,
-        cost_estimate=lasting(85),
-        compiler_params=params(cid),
-    )(part, inputs, gain, bias)
-
-
-def expand_kernel(h_ref, w_ref, pre_ref, hidden_ref):
-    pre = dot(h_ref[0], w_ref[...])
+def expand_kernel(
+    planes, h_ref, w_ref, g_ref, down_ref, pre_ref, hidden_ref, grad_ref, g_all_ref, wd_ref, held, g, total, w, *sems
+):
+    gather, line = Gather(g_ref, g_all_ref, sems[:7]), LineGather(planes, down_ref, wd_ref, sems[7:10])
+    step = pl.program_id(0)
+
+    @pl.when(step == 0)
+    def _():
+        greet(gather.near + line.near)
+        line.start()
+        gather.start()
+        weights = pltpu.make_async_copy(w_ref, w, sems[11])
+        weights.start()
+        weights.wait()
+
+    pre = dot(h_ref[0], w[...])
     pre_ref[0] = pre
     ff = hidden_ref.shape[2]
     gate_pre, up_pre = pre[:, :ff], pre[:, ff:]
-    hidden_ref[0] = (gate_pre * jax.nn.sigmoid(gate_pre) * up_pre).astype(BF16)
-
-
-def expand(h_two, w_both):
+    hidden = (gate_pre * jax.nn.sigmoid(gate_pre) * up_pre).astype(BF16)
+    hidden_ref[0] = hidden
+    held[step] = hidden
+    pl.when(step == TEAM - 2)(functools.partial(line.stage, 2))
+
+    @pl.when(step == TEAM - 1)
+    def _():
+        def load(i):
+            return pltpu.make_async_copy(g_all_ref.at[i], g.at[i % 2], sems[10].at[i % 2])
+
+        gather.middle()
+        gather.ready(0)
+        load(0).start()
+        for i in range(TEAM):
+            if i < TEAM - 1:
+                gather.ready(i + 1)
+                load(i + 1).start()
+            load(i).wait()
+            product = dot(held[i], g[i % 2], TN)
+            total[...] = product if i == 0 else total[...] + product
+            if i == 4:
+                for stage in range(3, planes):
+                    line.stage(stage)
+        grad_ref[...] = total[...].astype(BF16)
+        gather.sent()
+        line.finish()
+
+
+def expand(h_two, w_both, out_grad, down, planes, cid):
     seqs, rows, _ = h_two.shape
     width = w_both.shape[1]
     return pl.pallas_call(
-        expand_kernel,
+        functools.partial(expand_kernel, planes),
         grid=(seqs,),
-        in_specs=[per_seq(rows, D), whole(D, width)],
-        out_specs=[per_seq(rows, width), per_seq(rows, width // 2)],
+        in_specs=[per_seq(rows, D), ANY, VMEM, VMEM],
+        out_specs=[per_seq(rows, width), per_seq(rows, width // 2), whole(width // 2, D), ANY, ANY],
         out_shape=[
             jax.ShapeDtypeStruct((seqs, rows, width), F32),
             jax.ShapeDtypeStruct((seqs, rows, width // 2), BF16),
+            jax.ShapeDtypeStruct((width // 2, D), BF16),
+            jax.ShapeDtypeStruct((seqs, rows, D), BF16),
+            jax.ShapeDtypeStruct((planes,) + down.shape, BF16),
         ],
-        cost_estimate=lasting(18),
-        compiler_params=params(),
-    )(h_two, w_both)
+        scratch_shapes=[
+            pltpu.VMEM((seqs, rows, width // 2), BF16),
+            pltpu.VMEM((2, rows, D), BF16),
+            pltpu.VMEM((width // 2, D), F32),
+            pltpu.VMEM((D, width), BF16),
+        ]
+        + Gather.sems
+        + LineGather.sems(planes)
+        + [pltpu.SemaphoreType.DMA((2,)), pltpu.SemaphoreType.DMA],
+        cost_estimate=lasting(55),
+        compiler_params=params(cid),
+    )(h_two, w_both, out_grad, down)
 
 
 def mlp_back_kernel(
@@ -630,58 +755,82 @@
         + [two] * 4
         + [pltpu.SemaphoreType.DMA((3,))],
         cost_estimate=lasting(60),
-        compiler_params=params(cid),
+        compiler_params=params(cid, 50),
     )(pre, g_all, h_two, w_down, w_both, resid, out_grad, gain, after)
 
 
+def share(x, sums, bias, planes, per, depth):
+    mine = place()[0]
+    x[...] = jnp.zeros_like(x)
+    sums = [jnp.sum(v, axis=0, keepdims=True) for v in sums]
+    for z in range(planes):
+        for i in range(TEAM):
+            at = (z * TEAM + i) * depth
+            for row, v in enumerate(sums):
+                x[i, z, row : row + 1, :depth] = v[:, at : at + depth]
+    for part in range(3):
+        for z in range(planes):
+            head = part * HEADS + z * TEAM + mine
+            owner = head // per
+            at = (part * planes + z) * HEAD_DIM
+            x[lax.rem(owner, TEAM), owner // TEAM, pl.ds(4 + lax.rem(head, per), 1), :depth] = bias[:, at : at + HEAD_DIM]
+
+
 def last_kernel(
-    planes, part_ref, x_ref, grad_ref, gain_ref, both_ref, branch_ref,
-    out_ref, sums_ref, gate_ref, up_ref, wo_ref, held, far, *scratch,
+    planes, part_ref, x_ref, gain_ref, both_ref, branch_ref, sums_two_ref, bias_ref, _,
+    out_ref, held_ref, far_ref, vector_ref, sums, shared, got, *scratch,
 ):
-    total = Sum(part_ref, scratch[:4], scratch[4:11])
-    swap, line = Swap(both_ref, held, scratch[11:14]), Line(planes, branch_ref, far, scratch[14:])
+    total, swap = Sum(part_ref, scratch[:4], scratch[4:11]), Swap(both_ref, held_ref, scratch[11:14])
+    line, inner = Line(planes, branch_ref, far_ref, scratch[14:17]), Swap(shared, got, scratch[17:])
     greet(swap.near + line.near)
     total.start()
     line.start()
     total.middle()
     swap.start()
     total.middle_two()
-    sums_ref[...] = jnp.zeros_like(sums_ref)
+    sums[...] = jnp.zeros_like(sums)
 
     def use(rows, value):
         normed, inverse = normalize(x_ref[rows, :].astype(F32))
-        sums_ref[:8, :] += fold(value * normed)
-        sums_ref[8:, :] += fold(value)
-        out_ref[rows, :] = grad_ref[rows, :] + norm_back(value * gain_ref[...], normed, inverse)
+        sums[:8, :] += fold(value * normed)
+        sums[8:, :] += fold(value)
+        out_ref[rows, :] = norm_back(value * gain_ref[...], normed, inverse)
 
     total.finish(use)
+    vectors = [sums[:8, :], sums[8:, :], sums_two_ref[:8, :], sums_two_ref[8:, :]]
+    depth = part_ref.shape[2] // (planes * TEAM)
+    share(shared, vectors, added(bias_ref), planes, bias_ref.shape[2] // (planes * depth), depth)
+    inner.start()
+    inner.finish()
+    vector_ref[...] = added(got)
+    swap.finish()
     line.finish()
-    wo_ref[...] = added(far)
-    swap.finish()
-    unslice(held, 2, planes, [gate_ref, up_ref])
-
-
-def last(part, inputs, grad_resid, gain, both, branch, cid):
+
+
+def last(part, inputs, gain, both, branch, sums_two, bias, after, cid):
     rows, width = inputs.shape
-    planes, depth, _ = branch.shape
+    planes = branch.shape[0]
+    vectors = (TEAM, planes, 8, 128)
     return pl.pallas_call(
         functools.partial(last_kernel, planes),
         out_shape=[
             jax.ShapeDtypeStruct((rows, width), F32),
-            jax.ShapeDtypeStruct((16, width), F32),
-        ]
-        + [jax.ShapeDtypeStruct((depth, both.shape[2] * TEAM // 2), F32)] * 2
-        + [jax.ShapeDtypeStruct((depth, width), F32)],
-        in_specs=[ANY, VMEM, VMEM, VMEM, ANY, ANY],
-        out_specs=[VMEM] * 5,
-        scratch_shapes=[pltpu.VMEM(both.shape, BF16), pltpu.VMEM(branch.shape, BF16)]
+            jax.ShapeDtypeStruct(both.shape, BF16),
+            jax.ShapeDtypeStruct(branch.shape, BF16),
+            jax.ShapeDtypeStruct(vectors[1:], F32),
+        ],
+        in_specs=[ANY, VMEM, VMEM, VMEM, VMEM, VMEM, VMEM, ANY],
+        out_specs=[VMEM, ANY, ANY, VMEM],
+        scratch_shapes=[pltpu.VMEM((16, width), F32)]
+        + [pltpu.VMEM(vectors, F32)] * 2
         + Sum.scratch(rows, width)
         + Sum.sems
         + Swap.sems
-        + Line.sems(planes),
-        cost_estimate=lasting(60),
+        + Line.sems(planes)
+        + Swap.sems,
+        cost_estimate=lasting(58),
         compiler_params=params(cid),
-    )(part, inputs, grad_resid, gain, both, branch)
+    )(part, inputs, gain, both, branch, sums_two, bias, after)
 
 
 def dot(a, b, dims=((1,), (0,))):
@@ -740,17 +889,19 @@
 
 
 def attend_kernel(
-    x_ref, gain_ref, bias_ref, w_ref, b_ref, wo_ref, tab_ref, g_ref, h_ref, qkv_ref, attn_ref, part_ref, g_all_ref, *sems
+    planes, x_ref, gain_ref, bias_ref, w_ref, b_ref, wo_ref, tab_ref, gain_two_ref, bias_two_ref, both_ref,
+    h_ref, qkv_ref, attn_ref, resid_ref, h_two_ref, w_both_ref, block, away, *scratch,
 ):
-    gather = Gather(g_ref, g_all_ref, sems)
+    total, gather = Sum(None, scratch[:4], scratch[4:11], away), Gather(block, h_two_ref, scratch[11:18])
+    line = LineGather(planes, both_ref, w_both_ref, scratch[18:])
     step = pl.program_id(0)
 
     @pl.when(step == 0)
     def _():
-        greet(gather.near)
-        gather.start()
-
-    pl.when(step == TEAM // 2)(gather.middle)
+        greet(total.near + line.near)
+        line.start()
+
+    pl.when(step == TEAM - 2)(functools.partial(line.stage, 2))
     stream = x_ref[0].astype(F32)
     normed, _ = normalize(stream)
     h_one = (normed * gain_ref[...] + bias_ref[...]).astype(BF16)
@@ -771,8 +922,36 @@
         mixed = mixed + dot(probs, head_of(value, h))
     attn_low = mixed.astype(BF16)
     attn_ref[0] = attn_low
-    part_ref[0] = dot(attn_low, wo_ref[...]).astype(BF16)
-    pl.when(step == TEAM - 1)(gather.finish)
+    part = dot(attn_low, wo_ref[...]).astype(BF16)
+    k = 3 - step // 2
+
+    @pl.when(lax.rem(step, 2) == 0)
+    def _():
+        away[k] = part
+        total.near_copy(k).start()
+
+    @pl.when(lax.rem(step, 2) == 1)
+    def _():
+        total.own[k] = part
+
+    for at, advance in ((1, total.middle_a), (3, total.middle_b), (5, total.middle_c), (6, total.middle_two)):
+        pl.when(step == at)(advance)
+
+    def use(rows, value):
+        resid = x_ref[0, rows, :].astype(F32) + value
+        resid_ref[rows, :] = resid
+        normed, _ = normalize(resid)
+        block[rows, :] = (normed * gain_two_ref[...] + bias_two_ref[...]).astype(BF16)
+
+    @pl.when(step == TEAM - 1)
+    def _():
+        total.finish(use)
+        gather.start()
+        for stage in range(3, planes):
+            line.stage(stage)
+        gather.middle()
+        gather.finish()
+        line.finish()
 
 
 def per_seq(*shape):
@@ -783,34 +962,45 @@
     return pl.BlockSpec(shape, lambda s: (0,) * len(shape))
 
 
-def attend(x_all, gain, bias, w_qkv, b_qkv, w_out, tables, out_grad, cid):
+def attend(x_all, gain, bias, w_qkv, b_qkv, w_out, tables, gain_two, bias_two, both, planes, cid):
     seqs, rows, _ = x_all.shape
     width = LOCAL * HEAD_DIM
+
+    def far_first(*shape):
+        return pl.BlockSpec((1,) + shape, lambda s: (seqs - 1 - s,) + (0,) * len(shape))
+
     return pl.pallas_call(
-        attend_kernel,
+        functools.partial(attend_kernel, planes),
         grid=(seqs,),
         in_specs=[
-            per_seq(rows, D),
+            far_first(rows, D),
             whole(1, D),
             whole(1, D),
             whole(D, 3 * width),
             whole(1, 3 * width),
             whole(width, D),
-            per_seq(3, rows, 128),
-            ANY,
+            far_first(3, rows, 128),
+            whole(1, D),
+            whole(1, D),
+            VMEM,
         ],
-        out_specs=[per_seq(rows, D), per_seq(rows, 3 * width), per_seq(rows, width), per_seq(rows, D), ANY],
+        out_specs=[far_first(rows, D), far_first(rows, 3 * width), far_first(rows, width), whole(rows, D), ANY, ANY],
         out_shape=[
             jax.ShapeDtypeStruct((seqs, rows, D), BF16),
             jax.ShapeDtypeStruct((seqs, rows, 3 * width), BF16),
             jax.ShapeDtypeStruct((seqs, rows, width), BF16),
+            jax.ShapeDtypeStruct((rows, D), F32),
             jax.ShapeDtypeStruct((seqs, rows, D), BF16),
-            jax.ShapeDtypeStruct((seqs, rows, D), BF16),
+            jax.ShapeDtypeStruct((planes,) + both.shape, BF16),
         ],
-        scratch_shapes=Gather.sems,
-        cost_estimate=lasting(44),
+        scratch_shapes=[pltpu.VMEM((rows, D), BF16), pltpu.VMEM((4, rows, D), BF16)]
+        + Sum.scratch(rows, D)
+        + Sum.sems
+        + Gather.sems
+        + LineGather.sems(planes),
+        cost_estimate=lasting(100),
         compiler_params=params(cid),
-    )(x_all, gain, bias, w_qkv, b_qkv, w_out, tables, out_grad)
+    )(x_all, gain, bias, w_qkv, b_qkv, w_out, tables, gain_two, bias_two, both)
 
 
 def attend_back_kernel(
@@ -856,7 +1046,7 @@
     part_ref[0] = dot(grad_qkv, w_ref[...], NT).astype(BF16)
 
     def use(rows, value):
-        out_ref[rows, :] = (resid_ref[rows, :] + value).astype(BF16)
+        out_ref[rows, :] = resid_ref[rows, :] + value
 
     pl.when(step == 1)(gather.middle)
     pl.when(step == 3)(block.middle)
@@ -892,7 +1082,7 @@
             jax.ShapeDtypeStruct((seqs, rows, D), BF16),
             jax.ShapeDtypeStruct((seqs, 1, 3 * width), F32),
             jax.ShapeDtypeStruct((width, D), BF16),
-            jax.ShapeDtypeStruct((rows, D), BF16),
+            jax.ShapeDtypeStruct((rows, D), F32),
         ],
         scratch_shapes=[pltpu.VMEM((seqs, rows, D), BF16), pltpu.VMEM((width, D), F32)]
         + Gather.sems
@@ -917,40 +1107,31 @@
     lines = [[z * TEAM + i for z in range(planes)] for i in range(TEAM)]
     mine = lax.rem(lax.axis_index("fsdp"), TEAM)
 
-    def line_gather(x):
-        return lax.all_gather(x, "fsdp", axis=0, tiled=True, axis_index_groups=lines)
-
     def line_sum(x):
         return lax.psum_scatter(x, "fsdp", scatter_dimension=0, tiled=True, axis_index_groups=lines)
 
-    pieces, w_out = opening(qkv_weight, out_weight, planes, 0)
-    w_out = w_out.reshape(width, D)
-    w_qkv = line_gather(pieces.reshape(TEAM * depth, 3 * width))
+    w_out = lax.all_gather(out_weight, "fsdp", axis=0, tiled=True, axis_index_groups=lines)
+    pieces = opening(qkv_weight, planes, 0)
+    pieces = pieces.reshape(TEAM * depth, 3 * width)
     small = jnp.stack([norm1_gain, norm1_bias, norm2_gain, norm2_bias])
     small = jnp.concatenate([small, qkv_bias.reshape(-1, depth)])
     small = jnp.pad(small, ((0, 16 - small.shape[0]), (0, 128 - depth)))
     places = jnp.pad(positions.reshape(-1, 128).astype(BF16), ((0, 16 - rows // 128), (0, 0)))
-    both, x_all, small, places = second(gate_weight, up_weight, inputs, small, places, pieces, planes, 1)
-    w_both = line_gather(both.reshape(TEAM * depth, 2 * planes * ff))
-    w_down = line_gather(down_weight)
-    vectors = small.reshape(n, 16, 128)[:, :, :depth].astype(F32)
-    gain_one, bias_one, gain_two, bias_two = (vectors[:, i].reshape(1, D) for i in range(4))
-    b_qkv = vectors[:, 4 : 4 + 3 * planes * TEAM * HEAD_DIM // (n * depth)].reshape(3, planes, TEAM, HEAD_DIM)
-    b_qkv = lax.dynamic_index_in_dim(b_qkv, mine, 2, keepdims=False).reshape(1, 3 * width)
-    places = places.reshape(TEAM, -1)[:, :rows].astype(F32)
-
     half = ROT // 2
-    frequency = 10000.0 ** (-jnp.arange(half, dtype=F32) / half)
-    frequency = jnp.concatenate([frequency, frequency, jnp.zeros((HEAD_DIM - ROT,), F32)] * (128 // HEAD_DIM))
-    angles = places[:, :, None] * frequency
-    start = jnp.arange(rows, dtype=F32)[None] - places
-    tables = jnp.stack([jnp.cos(angles), jnp.sin(angles), jnp.broadcast_to(start[:, :, None], angles.shape)], axis=1)
-
-    h_one, qkv, attn_low, part, g_all = attend(x_all, gain_one, bias_one, w_qkv, b_qkv, w_out, tables, out_grad, 3)
-    resid, h_two = mid(part, inputs, gain_two, bias_two, 4)
-    pre, hidden = expand(h_two, w_both)
-    hidden = hidden.reshape(tokens, planes * ff)
-    grad_down = dot(hidden, g_all.reshape(tokens, D), TN).astype(BF16)
+    rate = 10000.0 ** (-np.arange(half) / half)
+    rate = np.tile(np.concatenate([rate, rate, np.zeros(HEAD_DIM - ROT)]), 128 // HEAD_DIM)[None].astype(np.float32)
+    both, x_all, w_qkv, tables, norms, b_qkv = second(
+        gate_weight, up_weight, inputs, small, places, pieces, jnp.asarray(rate), planes, 1
+    )
+    w_qkv = w_qkv.reshape(D, 3 * width)
+    gain_one, bias_one, gain_two, bias_two = (norms[i : i + 1] for i in range(4))
+    both = both.reshape(TEAM * depth, 2 * planes * ff)
+    h_one, qkv, attn_low, resid, h_two, w_both = attend(
+        x_all, gain_one, bias_one, w_qkv, b_qkv, w_out, tables, gain_two, bias_two, both, planes, 2
+    )
+    w_both = w_both.reshape(D, 2 * planes * ff)
+    pre, hidden, grad_down, g_all, w_down = expand(h_two, w_both, out_grad, down_weight, planes, 3)
+    hidden, w_down = hidden.reshape(tokens, planes * ff), w_down.reshape(planes * ff, D)
     grad_resid, sums_two, block, grad_w_both = mlp_back(
         pre, g_all, h_two.reshape(tokens, D), w_down, w_both, resid, out_grad, gain_two, grad_down, 5
     )
@@ -963,33 +1144,28 @@
     grad_qkv = grad_qkv.reshape(tokens, 3 * width)
     grad_w_qkv = dot(h_one.reshape(tokens, D), grad_qkv, TN).astype(BF16)
     part, grad_w_qkv, grad_w_both = lax.optimization_barrier((part, grad_w_qkv, grad_w_both))
-    input_grad, sums_one, grad_gate_w, grad_up_w, grad_out = last(
-        part, inputs, grad_resid, gain_one,
-        grad_w_both.reshape(TEAM, depth, 2 * planes * ff), grad_out.reshape(planes, depth, D), 7,
+    blocks = grad_w_both.reshape(TEAM, depth, 2 * planes * ff)
+    branch = grad_out.reshape(planes, depth, D)
+    norm_part, blocks, branch, shared = last(
+        part, inputs, gain_one, blocks, branch, sums_two, grad_bias, grad_w_qkv, 7
     )
     grad_w_qkv = line_sum(grad_w_qkv)
-
-    bias = jnp.zeros((3, planes, TEAM, HEAD_DIM), F32)
-    bias = lax.dynamic_update_slice(
-        bias, jnp.sum(grad_bias, axis=0).reshape(3, planes, 1, HEAD_DIM), (0, 0, mine, 0)
-    ).reshape(n, -1)
-    sums = [jnp.sum(v[i : i + 8], axis=0).reshape(n, depth) for v in (sums_one, sums_two) for i in (0, 8)]
-    sums = jnp.pad(jnp.concatenate(sums + [bias], axis=1), ((0, 0), (0, 1024 - 4 * depth - bias.shape[1])))
-    sums = sums.reshape(planes, TEAM, 8, 128).transpose(1, 0, 2, 3)
-    sums = vector_sums(sums, 8)
-    grad_w_qkv = closing(grad_w_qkv.reshape(TEAM, depth, 3 * width), sums, planes, 9)
-    sums = sums.reshape(-1)
-    sums = [sums[i * depth : (i + 1) * depth] for i in range(4)] + [sums[4 * depth : 4 * depth + bias.shape[1]]]
+    block_out, input_grad = block_out.astype(BF16), grad_resid + norm_part
+    grad_gate_w, grad_up_w = both_grads(blocks, planes)
+    blocks = grad_w_qkv.reshape(TEAM, depth, 3 * width)
+    blocks, sums = closing(blocks, shared, (input_grad, grad_up_w), 8)
+    grad_w_qkv, grad_out = rest_grads(blocks, branch)
+
     return (
         block_out,
         input_grad,
-        sums[0],
-        sums[1],
+        sums[0, :depth],
+        sums[1, :depth],
         grad_w_qkv,
-        sums[4],
+        sums[4 : 4 + qkv_bias.shape[0] // depth, :depth].reshape(-1),
         grad_out,
-        sums[2],
-        sums[3],
+        sums[2, :depth],
+        sums[3, :depth],
         grad_gate_w,
         grad_up_w,
         grad_down.astype(F32),

time: 544 us -> 525 us (0.965)
  matrix products: 32.9 us -> 22.1 us
  local copies, waits for them, and re-layouts: 19.6 us -> 12.5 us
    dot_general x3 -> x2, matrix products: 32.9 us -> 22.1 us  [dot(): return lax.dot_general(a, b, (dims, ((), ())), preferred_element_type=F32)]
    pallas_call x1, Pallas kernels: 62 us -> 70.3 us  [second(): pl.pallas_call(functools.partial(second_kernel, planes), out_shape=[jax.S...]
    pallas_call x6, Pallas kernels: 201 us -> 195 us  [the longest x1 102 us: attend(): pl.pallas_call(functools.partial(attend_kernel, planes), grid=(seqs,), in...]
  transfers between devices with their start and end apart: 6 -> 4, of which waited for: 1 -> 2; matrix products, arithmetic and copies ran while one was open for 10% -> 6% of each run, Pallas kernels for 78% -> 56%
where the time goes in v4:
time: 525 us; the launch traced here: 524 us
  Pallas kernels  468 us (89%)
  matrix products  22.1 us (4%)
  between operations  13.9 us (3%)
  local copies, waits for them, and re-layouts  12.5 us (2%)
  other arithmetic  6.3 us (1%)
    pallas_call x1, Pallas kernels, attend(): pl.pallas_call(functools.partial(attend_kernel, planes), grid=(seqs,), in...  102 us
    pallas_call x1, Pallas kernels, attend_back(): pl.pallas_call(attend_back_kernel, grid=(seqs,), in_specs=[ANY, whole(wid...  77.1 us
    pallas_call x1, Pallas kernels, second(): pl.pallas_call(functools.partial(second_kernel, planes), out_shape=[jax.S...  70.3 us
    pallas_call x1, Pallas kernels, last(): pl.pallas_call(functools.partial(last_kernel, planes), out_shape=[jax.Sha...  69.7 us
    pallas_call x1, Pallas kernels, mlp_back(): pl.pallas_call(mlp_back_kernel, out_shape=[jax.ShapeDtypeStruct((rows, wi...  55.7 us
    pallas_call x1, Pallas kernels, expand(): pl.pallas_call(functools.partial(expand_kernel, planes), grid=(seqs,), in...  54.4 us
    dot_general x2, matrix products, dot(): return lax.dot_general(a, b, (dims, ((), ())), preferred_element_type=F32)  22.1 us
    pallas_call x1, Pallas kernels, closing(): pl.pallas_call(functools.partial(close_kernel, planes), out_shape=[jax.Sh...  17.1 us
  transfers between devices with their start and end apart: 4, of which 2 were waited for; matrix products, arithmetic and copies ran while one was open for 6% of the time, Pallas kernels for 56%

profile of v4, /device:TPU:0, one launch (start us, length us, event | category | flops | bytes accessed | tf_op | source)
XLA Modules:
  0.0 524.4 jit_solution(8889185416024964514)
XLA Ops:
  7.2 0.0 all-gather.2.cloned.1.call-start
  7.2 0.7 all-gather.2.cloned.1.call-update
  7.9 0.0 reduce-scatter.4.cloned.1.call-start
  8.0 0.7 reshape.67
  8.7 0.7 concatenate.3
  9.4 0.6 pad.8.small_ref
  10.0 0.7 convert_bitcast_fusion
  10.7 0.6 pad.9.place_ref
  11.3 15.1 %shard_map.229 = bf16[8,64,768]{2,1,0:T(8,128)(2,1)} custom-call(bf16[64,6144]{1,0:T(8,128)(2,1)} %w_ref.1), custom_call_target="tpu_custom_call" | custom-call | bytes 61200000 | tf_op jit(solution)/shard_map/pallas_call | solution.py:185
  26.4 70.3 %shard_map.230 = (bf16[8,64,1408]{2,1,0:T(8,128)(2,1)}, bf16[8,256,2048]{2,1,0:T(8,128)(2,1)}, bf16[4,512,768]{2,1,0:T(8,128)(2,1)}, f32[8,3,256,128]{3,2,1,0:T(...) custom-call(bf16[64,5632]{1,0:T(8,128)(2,1)} %gate_ref.1, bf16[64,5632]{1,0:T(8,128)(2,1)} %up_ref.1, ...), custom_call_target="tpu_custom_call" | custom-call | bytes 234000000 | tf_op jit(solution)/shard_map/pallas_call | solution.py:263
  96.7 1.6 fusion
  98.2 0.0 all-gather.2.cloned.1.call-done.wo_ref
  98.2 102.1 %shard_map.231 = (bf16[8,256,2048]{2,1,0:T(8,128)(2,1)}, bf16[8,256,768]{2,1,0:T(8,128)(2,1)}, bf16[8,256,256]{2,1,0:T(8,128)(2,1)}, f32[256,2048]{1,0:T(8,128)}...) custom-call(bf16[8,256,2048]{2,1,0:T(8,128)(2,1)} %get-tuple-element.51.x_ref, ...), custom_call_target="tpu_custom_call" | custom-call | bytes 360000000 | tf_op jit(solution)/shard_map/pallas_call | solution.py:972
  200.4 0.0 copy-start.3
  200.4 54.4 %shard_map.232 = (f32[8,256,1408]{2,1,0:T(8,128)}, bf16[8,256,704]{2,1,0:T(8,128)(2,1)}, bf16[704,2048]{1,0:T(8,128)(2,1)}, bf16[8,256,2048]{2,1,0:T(8,128)(2,1)}, bf16[4,176,2048]{2,1,0:T(8,128)(2,1)}) custom-call(bf16[8,256,2048]{2,1,0:T(8,128)(2,1)} %get-tuple-element.57.h_ref, bf16[2048,1408]{1,0:T(8,128)(2,1)} %bitcast.32, bf16[256,2048]{1,0:T(8,128)(2,1)} %g_ref.3, ...), custom_call_target="tpu_custom_call" | custom-call | bytes 198000000 | tf_op jit(solution)/shard_map/pallas_call | solution.py:589
  254.8 0.0 copy-start
  254.8 0.0 reduce-scatter.4.cloned.1.call-update
  254.8 0.0 reduce-scatter.6.cloned.1.call-start
  254.8 0.0 copy-done.3
  254.9 1.1 copy-done
  256.0 55.7 %shard_map.233 = (f32[256,2048]{1,0:T(8,128)}, f32[16,2048]{1,0:T(8,128)S(1)}, bf16[256,2048]{1,0:T(8,128)(2,1)S(1)}, bf16[2048,1408]{1,0:T(8,128)(2,1)}) custom-call(f32[8,256,1408]{2,1,0:T(8,128)} %get-tuple-element.59.pre_ref, bf16[8,256,2048]{2,1,0:T(8,128)(2,1)} %get-tuple-element.60.g_all_ref, bf16[2048,2048]{1,0:T(8,128)(2,1)} %bitcast.31, ...), custom_call_target="tpu_custom_call" | custom-call | bytes 216000000 | tf_op jit(solution)/shard_map/pallas_call | solution.py:732
  311.7 0.0 copy-start.1
  311.7 1.0 copy-done.1
  312.7 0.0 copy-start.2
  312.7 0.7 copy-done.2
  313.3 0.0 reduce-scatter.6.cloned.1.call-update
  313.4 0.0 reduce-scatter.8.cloned.1.call-start
  313.4 1.7 copy-done.5
  315.2 10.8 %convolution_convert_fusion = bf16[2048,2048]{1,0:T(8,128)(2,1)} fusion(bf16[2048,704]{1,0:T(8,128)(2,1)} %bitcast.48, bf16[704,2048]{1,0:T(8,128)(2,1)S(1)} %bitcast.39), kind=kOutput, calls=%fused_computation | convolution fusion | flops 5909774336 | bytes 14155776 | tf_op jit(solution)/shard_map/dot_general | solution.py:837
  325.9 0.0 reduce-scatter.4.cloned.1.call-done._
  325.9 77.1 %shard_map.234 = (bf16[8,256,768]{2,1,0:T(8,128)(2,1)}, bf16[8,256,2048]{2,1,0:T(8,128)(2,1)}, f32[8,1,768]{2,1,0:T(1,128)}, bf16[256,2048]{1,0:T(8,128)(2,1)}, f32[256,2048]{1,0:T(8,128)}) custom-call(bf16[256,2048]{1,0:T(8,128)(2,1)} %copy-done.1, bf16[256,2048]{1,0:T(8,128)(2,1)} %all-gather.2.cloned.1.call-done.wo_ref, bf16[2048,768]{1,0:T(8,128)(2,1)} %bitcast.35, ...), custom_call_target="tpu_custom_call" | custom-call | bytes 234000000 | tf_op jit(solution)/shard_map/pallas_call | solution.py:1065
  403.1 11.4 %bitcast_convert_fusion._ = bf16[2048,768]{1,0:T(8,128)(2,1)} fusion(bf16[8,256,2048]{2,1,0:T(8,128)(2,1)} %get-tuple-element.71, bf16[8,256,768]{2,1,0:T(8,128)(2,1)} %get-tuple-element.72), kind=kOutput, calls=%fused_computation.1 | convolution fusion | flops 6444023808 | bytes 14680064 | tf_op jit(solution)/shard_map/dot_general | solution.py:837
  414.4 0.6 reduce-scatter.6.cloned.1.call-done
  415.0 0.0 reduce-scatter.8.cloned.1.call-update
  415.1 1.0 copy-done.7
  416.1 1.1 convert_element_type.25
  417.2 0.0 copy-done.4
  417.2 1.3 convert_element_type.27
  418.4 69.7 %shard_map.235 = (f32[256,2048]{1,0:T(8,128)}, bf16[8,64,1408]{2,1,0:T(8,128)(2,1)}, bf16[4,64,2048]{2,1,0:T(8,128)(2,1)}, f32[4,8,128]{2,1,0:T(8,128)}) custom-call(bf16[8,256,2048]{2,1,0:T(8,128)(2,1)} %get-tuple-element.74.part_ref, bf16[256,2048]{1,0:T(8,128)(2,1)} %x_ref.3, f32[1,2048]{1,0:T(1,128)} %get-tuple-element.93.gain_ref, ...), custom_call_target="tpu_custom_call" | custom-call | bytes 208800000 | tf_op jit(solution)/shard_map/pallas_call | solution.py:814
  488.1 3.3 shard_map.236
  491.4 0.0 copy-done.6
  491.4 3.2 add.13._
  494.6 0.3 reduce-scatter.8.cloned.1.call-done
  494.9 17.1 %shard_map.237 = (bf16[8,64,768]{2,1,0:T(8,128)(2,1)}, f32[8,128]{1,0:T(8,128)}) custom-call(bf16[8,64,768]{2,1,0:T(8,128)(2,1)} %bitcast.43, f32[4,8,128]{2,1,0:T(8,128)} %get-tuple-element.81.block_ref, f32[256,2048]{1,0:T(8,128)} %add.13._, f32[64,5632]{1,0:T(8,128)} %get-tuple-element.49.__), custom_call_target="tpu_custom_call" | custom-call | bytes 57600000 | tf_op jit(solution)/shard_map/pallas_call | solution.py:355
  512.1 0.7 slice.33
  512.8 1.4 slice_bitcast_fusion
  514.1 0.6 reshape.79
  514.7 3.1 shard_map.238
  (4 shorter events, 0.0 us)
Async XLA Ops:
  7.2 91.1 %all-gather.2.cloned.1.call-start = ((), (), s32[]{:S(2)}) async-start(), calls=%async_computation.3 | async-start | bytes 1310720 | tf_op jit(solution)/shard_map/all_gather | solution.py:1113
  7.9 318.0 %reduce-scatter.4.cloned.1.call-start = ((), (), s32[]{:S(2)}) async-start(), calls=%async_computation.4 | async-start | bytes 3604480 | tf_op jit(solution)/shard_map/reduce_scatter | solution.py:1111
  200.4 54.5 %copy-start.3 = (f32[1,2048]{1,0:T(1,128)S(1)}, f32[1,2048]{1,0:T(1,128)}, u32[]{:S(2)}) copy-start(f32[1,2048]{1,0:T(1,128)} %get-tuple-element.91.gain_two_ref.gain_ref) | copy-start | bytes 24580
  254.8 1.2 copy-start
  254.8 160.2 %reduce-scatter.6.cloned.1.call-start = ((), (), s32[]{:S(2)}) async-start(), calls=%async_computation.5 | async-start | bytes 7208960 | tf_op jit(solution)/shard_map/reduce_scatter | solution.py:1111
  311.7 1.0 copy-start.1
  312.7 0.7 copy-start.2
  313.3 1.8 copy-start.5
  313.4 181.6 %reduce-scatter.8.cloned.1.call-start = ((), (), s32[]{:S(2)}) async-start(), calls=%async_computation.6 | async-start | bytes 3932160 | tf_op jit(solution)/shard_map/reduce_scatter | solution.py:1111
  414.4 1.6 copy-start.7
  415.0 2.2 copy-start.4
  418.4 72.9 %copy-start.6 = (f32[256,2048]{1,0:T(8,128)S(1)}, f32[256,2048]{1,0:T(8,128)}, u32[]{:S(2)}) copy-start(f32[256,2048]{1,0:T(8,128)} %get-tuple-element.69) | copy-start | bytes 6291460
Sparse Core Ops, SparseCore 0:
  9.6 33.2 all-gather.1
  254.9 55.6 reduce-scatter.3
  313.5 101.4 reduce-scatter.5
  417.2 77.7 reduce-scatter.7

commit v5 on v4

--- a/solution.py
+++ b/solution.py
@@ -171,31 +171,9 @@
     return jnp.concatenate([ref[:, i * size : (i + 1) * size] for i in pieces], axis=1)
 
 
-def open_kernel(planes, w_ref, pieces_ref, made, *sems):
-    swap = Swap(made, pieces_ref, sems)
-    for i in range(TEAM):
-        made[i] = slices(w_ref, [s * HEADS + z * TEAM + i for s in range(3) for z in range(planes)], HEAD_DIM)
-    greet(swap.near)
-    swap.start()
-    swap.finish()
-
-
-def opening(weight, planes, cid):
-    shape = (TEAM, weight.shape[0], weight.shape[1] // TEAM)
-    return pl.pallas_call(
-        functools.partial(open_kernel, planes),
-        out_shape=jax.ShapeDtypeStruct(shape, BF16),
-        in_specs=[VMEM],
-        out_specs=ANY,
-        scratch_shapes=[pltpu.VMEM(shape, BF16)] + Swap.sems,
-        cost_estimate=lasting(17),
-        compiler_params=params(cid),
-    )(weight)
-
-
-def second_kernel(
-    planes, gate_ref, up_ref, x_ref, small_ref, place_ref, qkv_ref, rate_ref,
-    pieces_ref, x_all_ref, w_qkv_ref, tab_ref, norm_ref, b_ref, made, all_ref, places_ref, tables, *sems,
+def opening_kernel(
+    planes, qkv_ref, gate_ref, up_ref, x_ref, out_weight_ref, small_ref, place_ref, rate_ref,
+    pieces_ref, x_all_ref, w_qkv_ref, w_out_ref, tab_ref, norm_ref, b_ref, cut, landed, made, all_ref, places_ref, tables, *sems,
 ):
     mine, base, _, _ = place()
     plane = base // TEAM
@@ -203,20 +181,28 @@
     vectors = Swap(small_ref, all_ref.at[plane], sems[10:13], same=True)
     places = Swap(place_ref, places_ref, sems[13:16], same=True, near_first=True)
     line = Line(planes, all_ref.at[plane], all_ref, sems[16:19], same=True, within=True)
-    rows = LineGather(planes, qkv_ref, w_qkv_ref, sems[19:22])
+    rows, heads = LineGather(planes, landed, w_qkv_ref, sems[19:22]), Swap(cut, landed, sems[22:25])
+    outs = LineGather(planes, out_weight_ref, w_out_ref, sems[25:28])
+    for i in range(TEAM):
+        cut[i] = slices(qkv_ref, [s * HEADS + z * TEAM + i for s in range(3) for z in range(planes)], HEAD_DIM)
     greet(swap.near + line.near)
-    rows.start()
+    outs.start()
+    heads.start()
     vectors.start()
     places.start()
-    gather.start()
     size = gate_ref.shape[1] // (planes * TEAM)
     for i in range(TEAM):
         units = [z * TEAM + i for z in range(planes)]
         made[i] = jnp.concatenate([slices(gate_ref, units, size), slices(up_ref, units, size)], axis=1)
+    outs.stage(2)
+    heads.finish()
+    rows.start()
+    gather.start()
     swap.start()
     vectors.finish()
     line.start()
-    rows.stage(2)
+    for stage in range(3, planes):
+        outs.stage(stage)
     places.finish()
     square = (128, 128)
 
@@ -232,8 +218,9 @@
             token = lax.broadcasted_iota(jnp.int32, square, 0) + part * 128
             tables[i, 2, here, :] = token.astype(F32) - at
 
-    store = pltpu.make_async_copy(tables, tab_ref, sems[22])
+    store = pltpu.make_async_copy(tables, tab_ref, sems[28])
     store.start()
+    rows.stage(2)
     gather.middle()
     for stage in range(3, planes):
         rows.stage(stage)
@@ -242,7 +229,7 @@
     each = [all_ref[z, i].astype(F32) for z in range(planes) for i in range(TEAM)]
     for i in range(4):
         norm_ref[i : i + 1, :] = jnp.concatenate([known[i : i + 1, :depth] for known in each], axis=1)
-    per = qkv_ref.shape[1] * TEAM // (planes * TEAM * depth)
+    per = qkv_ref.shape[1] // (planes * TEAM * depth)
     bias = []
     for part in range(3):
         for z in range(planes):
@@ -254,25 +241,30 @@
     gather.finish()
     swap.finish()
     rows.finish()
+    outs.finish()
     store.wait()
 
 
-def second(gate, up, inputs, small, positions, qkv, rate, planes, cid):
+def opening(qkv, gate, up, inputs, out_weight, small, positions, rate, planes, cid):
     shape = (TEAM, gate.shape[0], 2 * gate.shape[1] // TEAM)
+    heads = (TEAM, qkv.shape[0], qkv.shape[1] // TEAM)
     tables = (TEAM, 3, inputs.shape[0], 128)
     return pl.pallas_call(
-        functools.partial(second_kernel, planes),
+        functools.partial(opening_kernel, planes),
         out_shape=[
             jax.ShapeDtypeStruct(shape, BF16),
             jax.ShapeDtypeStruct((TEAM,) + inputs.shape, BF16),
-            jax.ShapeDtypeStruct((planes,) + qkv.shape, BF16),
+            jax.ShapeDtypeStruct((planes,) + heads, BF16),
+            jax.ShapeDtypeStruct((planes,) + out_weight.shape, BF16),
             jax.ShapeDtypeStruct(tables, F32),
             jax.ShapeDtypeStruct((4, inputs.shape[1]), F32),
-            jax.ShapeDtypeStruct((1, qkv.shape[1]), F32),
+            jax.ShapeDtypeStruct((1, heads[2]), F32),
         ],
-        in_specs=[VMEM] * 7,
-        out_specs=[ANY] * 4 + [VMEM] * 2,
+        in_specs=[VMEM] * 8,
+        out_specs=[ANY] * 5 + [VMEM] * 2,
         scratch_shapes=[
+            pltpu.VMEM(heads, BF16),
+            pltpu.VMEM(heads, BF16),
             pltpu.VMEM(shape, BF16),
             pltpu.VMEM((planes, TEAM) + small.shape, BF16),
             pltpu.VMEM((TEAM,) + positions.shape, BF16),
@@ -283,10 +275,12 @@
         + Swap.sems * 2
         + Line.sems(planes)
         + LineGather.sems(planes)
+        + Swap.sems
+        + LineGather.sems(planes)
         + [pltpu.SemaphoreType.DMA],
-        cost_estimate=lasting(65),
+        cost_estimate=lasting(80),
         compiler_params=params(cid),
-    )(gate, up, inputs, small, positions, qkv, rate)
+    )(qkv, gate, up, inputs, out_weight, small, positions, rate)
 
 
 def unslice(held, parts, planes, outs):
@@ -297,40 +291,38 @@
         out[:, first * TEAM * size : (first + 1) * TEAM * size] = row.astype(F32)
 
 
-def both_kernel(planes, held_ref, gate_ref, up_ref):
+def first_kernel(planes, held_ref, far_ref, gate_ref, up_ref, wo_ref):
     unslice(held_ref, 2, planes, [gate_ref, up_ref])
-
-
-def both_grads(held, planes):
+    wo_ref[...] = added(far_ref)
+
+
+def first_grads(held, far):
     _, depth, width = held.shape
     return pl.pallas_call(
-        functools.partial(both_kernel, planes),
-        out_shape=[jax.ShapeDtypeStruct((depth, width * TEAM // 2), F32)] * 2,
-        in_specs=[VMEM],
-        out_specs=[VMEM] * 2,
-        cost_estimate=lasting(4),
-        compiler_params=params(),
-    )(held)
-
-
-def rest_kernel(planes, held_ref, far_ref, w_ref, wo_ref):
-    unslice(held_ref, 3, planes, [w_ref])
-    wo_ref[...] = added(far_ref)
-
-
-def rest_grads(held, far):
-    _, depth, width = held.shape
-    return pl.pallas_call(
-        functools.partial(rest_kernel, far.shape[0]),
-        out_shape=[
-            jax.ShapeDtypeStruct((depth, width * TEAM), F32),
-            jax.ShapeDtypeStruct(far.shape[1:], F32),
-        ],
+        functools.partial(first_kernel, far.shape[0]),
+        out_shape=[jax.ShapeDtypeStruct((depth, width * TEAM // 2), F32)] * 2
+        + [jax.ShapeDtypeStruct(far.shape[1:], F32)],
         in_specs=[VMEM] * 2,
-        out_specs=[VMEM] * 2,
+        out_specs=[VMEM] * 3,
         cost_estimate=lasting(4),
         compiler_params=params(),
     )(held, far)
+
+
+def rest_kernel(planes, held_ref, w_ref):
+    unslice(held_ref, 3, planes, [w_ref])
+
+
+def rest_grads(held, planes):
+    _, depth, width = held.shape
+    return pl.pallas_call(
+        functools.partial(rest_kernel, planes),
+        out_shape=jax.ShapeDtypeStruct((depth, width * TEAM), F32),
+        in_specs=[VMEM],
+        out_specs=VMEM,
+        cost_estimate=lasting(3),
+        compiler_params=params(),
+    )(held)
 
 
 def added(ref):
@@ -340,30 +332,23 @@
     return total
 
 
-def close_kernel(planes, w_ref, block_ref, _, __, held_ref, vector_ref, beyond, *sems):
-    swap, outer = Swap(w_ref, held_ref, sems[:3]), Line(planes, block_ref, beyond, sems[3:])
-    greet(swap.near + outer.near)
-    outer.start()
+def close_kernel(w_ref, _, __, ___, held_ref, *sems):
+    swap = Swap(w_ref, held_ref, sems)
+    greet(swap.near)
     swap.start()
-    outer.finish()
     swap.finish()
-    vector_ref[...] = added(beyond)
-
-
-def closing(blocks, sums, after, cid):
-    planes = sums.shape[0]
+
+
+def closing(blocks, after, cid):
     return pl.pallas_call(
-        functools.partial(close_kernel, planes),
-        out_shape=[
-            jax.ShapeDtypeStruct(blocks.shape, BF16),
-            jax.ShapeDtypeStruct(sums.shape[1:], F32),
-        ],
-        in_specs=[VMEM, VMEM, ANY, ANY],
-        out_specs=[ANY, VMEM],
-        scratch_shapes=[pltpu.VMEM(sums.shape, F32)] + Swap.sems + Line.sems(planes),
-        cost_estimate=lasting(16),
+        close_kernel,
+        out_shape=jax.ShapeDtypeStruct(blocks.shape, BF16),
+        in_specs=[VMEM, ANY, ANY, ANY],
+        out_specs=ANY,
+        scratch_shapes=Swap.sems,
+        cost_estimate=lasting(14),
         compiler_params=params(cid),
-    )(blocks, sums, *after)
+    )(blocks, *after)
 
 
 class Gather:
@@ -613,7 +598,7 @@
 
 
 def mlp_back_kernel(
-    pre_ref, g_all_ref, h_ref, wd_ref, w_ref, resid_ref, g_ref, gain_ref, _,
+    pre_ref, g_all_ref, h_ref, wd_ref, w_ref, resid_ref, g_ref, norm_ref, _,
     out_ref, sums_ref, block_ref, grad_w_ref,
     pre, g_all, turned, made, grads, away, w, resid, own_grad, *scratch,
 ):
@@ -715,7 +700,7 @@
         normed, inverse = normalize(resid[rows, :])
         sums_ref[:8, :] += fold(value * normed)
         sums_ref[8:, :] += fold(value)
-        grad = own_grad[rows, :].astype(F32) + norm_back(value * gain_ref[...], normed, inverse)
+        grad = own_grad[rows, :].astype(F32) + norm_back(value * norm_ref[2:3, :], normed, inverse)
         out_ref[rows, :] = grad
         block_ref[rows, :] = grad.astype(BF16)
 
@@ -777,24 +762,25 @@
 
 
 def last_kernel(
-    planes, part_ref, x_ref, gain_ref, both_ref, branch_ref, sums_two_ref, bias_ref, _,
-    out_ref, held_ref, far_ref, vector_ref, sums, shared, got, *scratch,
+    planes, part_ref, x_ref, norm_ref, both_ref, branch_ref, sums_two_ref, bias_ref, _,
+    out_ref, held_ref, far_ref, vector_ref, sums, shared, got, block, beyond, *scratch,
 ):
     total, swap = Sum(part_ref, scratch[:4], scratch[4:11]), Swap(both_ref, held_ref, scratch[11:14])
-    line, inner = Line(planes, branch_ref, far_ref, scratch[14:17]), Swap(shared, got, scratch[17:])
+    line, inner = Line(planes, branch_ref, far_ref, scratch[14:17]), Swap(shared, got, scratch[17:20])
+    outer = Line(planes, block, beyond, scratch[20:])
     greet(swap.near + line.near)
     total.start()
     line.start()
     total.middle()
+    total.middle_two()
     swap.start()
-    total.middle_two()
     sums[...] = jnp.zeros_like(sums)
 
     def use(rows, value):
         normed, inverse = normalize(x_ref[rows, :].astype(F32))
         sums[:8, :] += fold(value * normed)
         sums[8:, :] += fold(value)
-        out_ref[rows, :] = norm_back(value * gain_ref[...], normed, inverse)
+        out_ref[rows, :] = norm_back(value * norm_ref[0:1, :], normed, inverse)
 
     total.finish(use)
     vectors = [sums[:8, :], sums[8:, :], sums_two_ref[:8, :], sums_two_ref[8:, :]]
@@ -802,7 +788,10 @@
     share(shared, vectors, added(bias_ref), planes, bias_ref.shape[2] // (planes * depth), depth)
     inner.start()
     inner.finish()
-    vector_ref[...] = added(got)
+    block[...] = added(got)
+    outer.start()
+    outer.finish()
+    vector_ref[...] = added(beyond)
     swap.finish()
     line.finish()
 
@@ -817,17 +806,19 @@
             jax.ShapeDtypeStruct((rows, width), F32),
             jax.ShapeDtypeStruct(both.shape, BF16),
             jax.ShapeDtypeStruct(branch.shape, BF16),
-            jax.ShapeDtypeStruct(vectors[1:], F32),
+            jax.ShapeDtypeStruct(vectors[2:], F32),
         ],
         in_specs=[ANY, VMEM, VMEM, VMEM, VMEM, VMEM, VMEM, ANY],
         out_specs=[VMEM, ANY, ANY, VMEM],
         scratch_shapes=[pltpu.VMEM((16, width), F32)]
         + [pltpu.VMEM(vectors, F32)] * 2
+        + [pltpu.VMEM(vectors[1:], F32)] * 2
         + Sum.scratch(rows, width)
         + Sum.sems
         + Swap.sems
         + Line.sems(planes)
-        + Swap.sems,
+        + Swap.sems
+        + Line.sems(planes),
         cost_estimate=lasting(58),
         compiler_params=params(cid),
     )(part, inputs, gain, both, branch, sums_two, bias, after)
@@ -889,24 +880,27 @@
 
 
 def attend_kernel(
-    planes, x_ref, gain_ref, bias_ref, w_ref, b_ref, wo_ref, tab_ref, gain_two_ref, bias_two_ref, both_ref,
-    h_ref, qkv_ref, attn_ref, resid_ref, h_two_ref, w_both_ref, block, away, *scratch,
+    planes, x_ref, norm_ref, w_ref, b_ref, wo_ref, tab_ref, both_ref,
+    h_ref, qkv_ref, attn_ref, resid_ref, h_two_ref, w_both_ref, block, away, w, *scratch,
 ):
     total, gather = Sum(None, scratch[:4], scratch[4:11], away), Gather(block, h_two_ref, scratch[11:18])
-    line = LineGather(planes, both_ref, w_both_ref, scratch[18:])
+    line = LineGather(planes, both_ref, w_both_ref, scratch[18:21])
     step = pl.program_id(0)
 
     @pl.when(step == 0)
     def _():
         greet(total.near + line.near)
         line.start()
+        weights = pltpu.make_async_copy(w_ref, w, scratch[21])
+        weights.start()
+        weights.wait()
 
     pl.when(step == TEAM - 2)(functools.partial(line.stage, 2))
     stream = x_ref[0].astype(F32)
     normed, _ = normalize(stream)
-    h_one = (normed * gain_ref[...] + bias_ref[...]).astype(BF16)
+    h_one = (normed * norm_ref[0:1, :] + norm_ref[1:2, :]).astype(BF16)
     h_ref[0] = h_one
-    qkv = dot(h_one, w_ref[...]) + b_ref[...]
+    qkv = dot(h_one, w[...]) + b_ref[...]
     width = LOCAL * HEAD_DIM
     cosine, sine = wide(tab_ref[0, 0]), wide(tab_ref[0, 1])
     query = turn(qkv[:, :width], cosine, sine).astype(BF16)
@@ -941,7 +935,7 @@
         resid = x_ref[0, rows, :].astype(F32) + value
         resid_ref[rows, :] = resid
         normed, _ = normalize(resid)
-        block[rows, :] = (normed * gain_two_ref[...] + bias_two_ref[...]).astype(BF16)
+        block[rows, :] = (normed * norm_ref[2:3, :] + norm_ref[3:4, :]).astype(BF16)
 
     @pl.when(step == TEAM - 1)
     def _():
@@ -962,7 +956,7 @@
     return pl.BlockSpec(shape, lambda s: (0,) * len(shape))
 
 
-def attend(x_all, gain, bias, w_qkv, b_qkv, w_out, tables, gain_two, bias_two, both, planes, cid):
+def attend(x_all, norms, w_qkv, b_qkv, w_out, tables, both, planes, cid):
     seqs, rows, _ = x_all.shape
     width = LOCAL * HEAD_DIM
 
@@ -974,14 +968,11 @@
         grid=(seqs,),
         in_specs=[
             far_first(rows, D),
-            whole(1, D),
-            whole(1, D),
-            whole(D, 3 * width),
+            whole(4, D),
+            ANY,
             whole(1, 3 * width),
             whole(width, D),
             far_first(3, rows, 128),
-            whole(1, D),
-            whole(1, D),
             VMEM,
         ],
         out_specs=[far_first(rows, D), far_first(rows, 3 * width), far_first(rows, width), whole(rows, D), ANY, ANY],
@@ -993,29 +984,45 @@
             jax.ShapeDtypeStruct((seqs, rows, D), BF16),
             jax.ShapeDtypeStruct((planes,) + both.shape, BF16),
         ],
-        scratch_shapes=[pltpu.VMEM((rows, D), BF16), pltpu.VMEM((4, rows, D), BF16)]
+        scratch_shapes=[
+            pltpu.VMEM((rows, D), BF16),
+            pltpu.VMEM((4, rows, D), BF16),
+            pltpu.VMEM((D, 3 * width), BF16),
+        ]
         + Sum.scratch(rows, D)
         + Sum.sems
         + Gather.sems
-        + LineGather.sems(planes),
+        + LineGather.sems(planes)
+        + [pltpu.SemaphoreType.DMA],
         cost_estimate=lasting(100),
         compiler_params=params(cid),
-    )(x_all, gain, bias, w_qkv, b_qkv, w_out, tables, gain_two, bias_two, both)
+    )(x_all, norms, w_qkv, b_qkv, w_out, tables, both)
 
 
 def attend_back_kernel(
-    block_ref, wo_ref, w_ref, qkv_ref, tab_ref, attn_ref, down_ref, resid_ref, _,
-    gqkv_ref, part_ref, gb_ref, wo_grad_ref, out_ref, held, wo_grad, *scratch,
+    block_ref, wo_ref, w_ref, qkv_ref, tab_ref, attn_ref, hidden_ref, wd_ref, resid_ref, _,
+    gqkv_ref, part_ref, gb_ref, wo_grad_ref, out_ref, held, wo_grad, away, *scratch,
 ):
-    gather, block = Gather(block_ref, held, scratch[:7]), Sum(down_ref, scratch[7:11], scratch[11:])
+    gather, block = Gather(block_ref, held, scratch[:7]), Sum(None, scratch[7:11], scratch[11:], away)
     step = pl.program_id(0)
 
     @pl.when(step == 0)
     def _():
         greet(gather.near)
         gather.start()
-        block.start()
         wo_grad[...] = jnp.zeros_like(wo_grad)
+
+    part = dot(hidden_ref[0], wd_ref[...]).astype(BF16)
+    k = 3 - step // 2
+
+    @pl.when(lax.rem(step, 2) == 0)
+    def _():
+        away[k] = part
+        block.near_copy(k).start()
+
+    @pl.when(lax.rem(step, 2) == 1)
+    def _():
+        block.own[k] = part
 
     for i in range(TEAM):
         pl.when(step == i)(functools.partial(gather.ready, i))
@@ -1049,8 +1056,8 @@
         out_ref[rows, :] = resid_ref[rows, :] + value
 
     pl.when(step == 1)(gather.middle)
-    pl.when(step == 3)(block.middle)
-    pl.when(step == 6)(block.middle_two)
+    for at, advance in ((1, block.middle_a), (3, block.middle_b), (5, block.middle_c), (6, block.middle_two)):
+        pl.when(step == at)(advance)
 
     @pl.when(step == TEAM - 1)
     def _():
@@ -1059,9 +1066,13 @@
         gather.sent()
 
 
-def attend_back(block, w_out, w_qkv, qkv, tables, attn, down, resid, after, cid):
+def attend_back(block, w_out, w_qkv, qkv, tables, attn, hidden, w_down, resid, after, cid):
     seqs, rows, _ = qkv.shape
     width = LOCAL * HEAD_DIM
+
+    def far_first(*shape):
+        return pl.BlockSpec((1,) + shape, lambda s: (seqs - 1 - s,) + (0,) * len(shape))
+
     return pl.pallas_call(
         attend_back_kernel,
         grid=(seqs,),
@@ -1072,8 +1083,9 @@
             per_seq(rows, 3 * width),
             per_seq(3, rows, 128),
             per_seq(rows, width),
-            ANY,
-            whole(rows, D),
+            far_first(rows, hidden.shape[2]),
+            VMEM,
+            VMEM,
             ANY,
         ],
         out_specs=[per_seq(rows, 3 * width), per_seq(rows, D), per_seq(1, 3 * width), whole(width, D), whole(rows, D)],
@@ -1084,13 +1096,17 @@
             jax.ShapeDtypeStruct((width, D), BF16),
             jax.ShapeDtypeStruct((rows, D), F32),
         ],
-        scratch_shapes=[pltpu.VMEM((seqs, rows, D), BF16), pltpu.VMEM((width, D), F32)]
+        scratch_shapes=[
+            pltpu.VMEM((seqs, rows, D), BF16),
+            pltpu.VMEM((width, D), F32),
+            pltpu.VMEM((4, rows, D), BF16),
+        ]
         + Gather.sems
         + Sum.scratch(rows, D)
         + Sum.sems,
         cost_estimate=lasting(65),
-        compiler_params=params(cid),
-    )(block, w_out, w_qkv, qkv, tables, attn, down, resid, after)
+        compiler_params=params(cid, 54),
+    )(block, w_out, w_qkv, qkv, tables, attn, hidden, w_down, resid, after)
 
 
 def team_shards(
@@ -1110,9 +1126,6 @@
     def line_sum(x):
         return lax.psum_scatter(x, "fsdp", scatter_dimension=0, tiled=True, axis_index_groups=lines)
 
-    w_out = lax.all_gather(out_weight, "fsdp", axis=0, tiled=True, axis_index_groups=lines)
-    pieces = opening(qkv_weight, planes, 0)
-    pieces = pieces.reshape(TEAM * depth, 3 * width)
     small = jnp.stack([norm1_gain, norm1_bias, norm2_gain, norm2_bias])
     small = jnp.concatenate([small, qkv_bias.reshape(-1, depth)])
     small = jnp.pad(small, ((0, 16 - small.shape[0]), (0, 128 - depth)))
@@ -1120,41 +1133,39 @@
     half = ROT // 2
     rate = 10000.0 ** (-np.arange(half) / half)
     rate = np.tile(np.concatenate([rate, rate, np.zeros(HEAD_DIM - ROT)]), 128 // HEAD_DIM)[None].astype(np.float32)
-    both, x_all, w_qkv, tables, norms, b_qkv = second(
-        gate_weight, up_weight, inputs, small, places, pieces, jnp.asarray(rate), planes, 1
-    )
+    both, x_all, w_qkv, w_out, tables, norms, b_qkv = opening(
+        qkv_weight, gate_weight, up_weight, inputs, out_weight, small, places, jnp.asarray(rate), planes, 1
+    )
+    w_out = w_out.reshape(width, D)
     w_qkv = w_qkv.reshape(D, 3 * width)
-    gain_one, bias_one, gain_two, bias_two = (norms[i : i + 1] for i in range(4))
     both = both.reshape(TEAM * depth, 2 * planes * ff)
     h_one, qkv, attn_low, resid, h_two, w_both = attend(
-        x_all, gain_one, bias_one, w_qkv, b_qkv, w_out, tables, gain_two, bias_two, both, planes, 2
+        x_all, norms, w_qkv, b_qkv, w_out, tables, both, planes, 2
     )
     w_both = w_both.reshape(D, 2 * planes * ff)
     pre, hidden, grad_down, g_all, w_down = expand(h_two, w_both, out_grad, down_weight, planes, 3)
-    hidden, w_down = hidden.reshape(tokens, planes * ff), w_down.reshape(planes * ff, D)
+    w_down = w_down.reshape(planes * ff, D)
     grad_resid, sums_two, block, grad_w_both = mlp_back(
-        pre, g_all, h_two.reshape(tokens, D), w_down, w_both, resid, out_grad, gain_two, grad_down, 5
+        pre, g_all, h_two.reshape(tokens, D), w_down, w_both, resid, out_grad, norms, grad_down, 5
     )
     grad_down = line_sum(grad_down)
     grad_w_both = line_sum(grad_w_both)
-    down = dot(hidden, w_down).astype(BF16).reshape(TEAM, rows, D)
     grad_qkv, part, grad_bias, grad_out, block_out = attend_back(
-        block, w_out, w_qkv, qkv, tables, attn_low, down, resid, grad_down, 6
+        block, w_out, w_qkv, qkv, tables, attn_low, hidden, w_down, resid, grad_down, 6
     )
     grad_qkv = grad_qkv.reshape(tokens, 3 * width)
     grad_w_qkv = dot(h_one.reshape(tokens, D), grad_qkv, TN).astype(BF16)
-    part, grad_w_qkv, grad_w_both = lax.optimization_barrier((part, grad_w_qkv, grad_w_both))
+    part, grad_w_qkv = lax.optimization_barrier((part, grad_w_qkv))
     blocks = grad_w_both.reshape(TEAM, depth, 2 * planes * ff)
     branch = grad_out.reshape(planes, depth, D)
-    norm_part, blocks, branch, shared = last(
-        part, inputs, gain_one, blocks, branch, sums_two, grad_bias, grad_w_qkv, 7
+    norm_part, blocks, branch, sums = last(
+        part, inputs, norms, blocks, branch, sums_two, grad_bias, grad_w_qkv, 7
     )
     grad_w_qkv = line_sum(grad_w_qkv)
     block_out, input_grad = block_out.astype(BF16), grad_resid + norm_part
-    grad_gate_w, grad_up_w = both_grads(blocks, planes)
-    blocks = grad_w_qkv.reshape(TEAM, depth, 3 * width)
-    blocks, sums = closing(blocks, shared, (input_grad, grad_up_w), 8)
-    grad_w_qkv, grad_out = rest_grads(blocks, branch)
+    grad_gate_w, grad_up_w, grad_out = first_grads(blocks, branch)
+    blocks = closing(grad_w_qkv.reshape(TEAM, depth, 3 * width), (input_grad, grad_up_w, sums), 8)
+    grad_w_qkv = rest_grads(blocks, planes)
 
     return (
         block_out,

time: 525 us -> 511 us (0.973)
  matrix products: 22.1 us -> 11.4 us
  Pallas kernels: 468 us -> 459 us
  waiting for transfers between devices: 1.64 us -> 8.12 us
    dot_general x2 -> x1, matrix products: 22.1 us -> 11.4 us  [dot(): return lax.dot_general(a, b, (dims, ((), ())), preferred_element_type=F32)]
    reduce_scatter x3, waiting for transfers between devices: 0.9 us -> 8.07 us  [line_sum(): lax.psum_scatter(x, 'fsdp', scatter_dimension=0, tiled=True, axis_index_g...]
    pallas_call x5 -> x4, Pallas kernels: 109 us -> 102 us  [the longest x1 82.6 us: opening(): pl.pallas_call(functools.partial(opening_kernel, planes), out_shape=[jax....]
  transfers between devices with their start and end apart: 4 -> 3, of which waited for: 2 -> 2; matrix products, arithmetic and copies ran while one was open for 6% -> 4% of each run, Pallas kernels for 56% -> 41%
where the time goes in v5:
time: 511 us; the launch traced here: 507 us
  Pallas kernels  459 us (90%)
  between operations  13.9 us (3%)
  matrix products  11.4 us (2%)
  local copies, waits for them, and re-layouts  8.84 us (2%)
  waiting for transfers between devices  8.12 us (2%)
  other arithmetic  6.21 us (1%)
    pallas_call x1, Pallas kernels, attend(): pl.pallas_call(functools.partial(attend_kernel, planes), grid=(seqs,), in...  101 us
    pallas_call x1, Pallas kernels, opening(): pl.pallas_call(functools.partial(opening_kernel, planes), out_shape=[jax....  82.6 us
    pallas_call x1, Pallas kernels, attend_back(): pl.pallas_call(attend_back_kernel, grid=(seqs,), in_specs=[ANY, whole(wid...  78.2 us
    pallas_call x1, Pallas kernels, last(): pl.pallas_call(functools.partial(last_kernel, planes), out_shape=[jax.Sha...  68.3 us
    pallas_call x1, Pallas kernels, mlp_back(): pl.pallas_call(mlp_back_kernel, out_shape=[jax.ShapeDtypeStruct((rows, wi...  55.5 us
    pallas_call x1, Pallas kernels, expand(): pl.pallas_call(functools.partial(expand_kernel, planes), grid=(seqs,), in...  54 us
    pallas_call x1, Pallas kernels, closing(): pl.pallas_call(close_kernel, out_shape=jax.ShapeDtypeStruct(blocks.shape,...  13.3 us
    dot_general x1, matrix products, dot(): return lax.dot_general(a, b, (dims, ((), ())), preferred_element_type=F32)  11.4 us
  transfers between devices with their start and end apart: 3, of which 2 were waited for; matrix products, arithmetic and copies ran while one was open for 4% of the time, Pallas kernels for 41%

profile of v5, /device:TPU:0, one launch (start us, length us, event | category | flops | bytes accessed | tf_op | source)
XLA Modules:
  0.0 507.4 jit_solution(823344241105301730)
XLA Ops:
  7.2 0.0 reduce-scatter.4.cloned.1.call-start
  7.2 0.7 convert_bitcast_fusion
  7.9 0.7 reshape.61
  8.6 0.7 concatenate.3
  9.4 0.6 pad.8.small_ref
  10.0 0.6 pad.9.place_ref
  10.6 82.6 %shard_map.229 = (bf16[8,64,1408]{2,1,0:T(8,128)(2,1)}, bf16[8,256,2048]{2,1,0:T(8,128)(2,1)}, bf16[4,8,64,768]{3,2,1,0:T(8,128)(2,1)}, bf16[4,64,2048]{2,1,0:T(...) custom-call(bf16[64,6144]{1,0:T(8,128)(2,1)} %qkv_ref.1, bf16[64,5632]{1,0:T(8,128)(2,1)} %gate_ref.1, ...), custom_call_target="tpu_custom_call" | custom-call | bytes 288000000 | tf_op jit(solution)/shard_map/pallas_call | solution.py:252
  93.2 100.7 %shard_map.230 = (bf16[8,256,2048]{2,1,0:T(8,128)(2,1)}, bf16[8,256,768]{2,1,0:T(8,128)(2,1)}, bf16[8,256,256]{2,1,0:T(8,128)(2,1)}, f32[256,2048]{1,0:T(8,128)}...) custom-call(bf16[8,256,2048]{2,1,0:T(8,128)(2,1)} %get-tuple-element.48.x_ref, ...), custom_call_target="tpu_custom_call" | custom-call | bytes 360000000 | tf_op jit(solution)/shard_map/pallas_call | solution.py:966
  193.8 0.0 copy-start.2
  193.9 54.0 %shard_map.231 = (f32[8,256,1408]{2,1,0:T(8,128)}, bf16[8,256,704]{2,1,0:T(8,128)(2,1)}, bf16[704,2048]{1,0:T(8,128)(2,1)}, bf16[8,256,2048]{2,1,0:T(8,128)(2,1)}, bf16[4,176,2048]{2,1,0:T(8,128)(2,1)}) custom-call(bf16[8,256,2048]{2,1,0:T(8,128)(2,1)} %get-tuple-element.55.h_ref, bf16[2048,1408]{1,0:T(8,128)(2,1)} %bitcast.28, bf16[256,2048]{1,0:T(8,128)(2,1)} %g_ref.3, ...), custom_call_target="tpu_custom_call" | custom-call | bytes 198000000 | tf_op jit(solution)/shard_map/pallas_call | solution.py:574
  247.9 0.0 copy-start
  247.9 0.0 reduce-scatter.4.cloned.1.call-update
  247.9 0.0 reduce-scatter.6.cloned.1.call-start
  248.0 0.0 copy-done.2
  248.0 1.1 copy-done
  249.1 55.5 %shard_map.232 = (f32[256,2048]{1,0:T(8,128)}, f32[16,2048]{1,0:T(8,128)S(1)}, bf16[256,2048]{1,0:T(8,128)(2,1)S(1)}, bf16[2048,1408]{1,0:T(8,128)(2,1)}) custom-call(f32[8,256,1408]{2,1,0:T(8,128)} %get-tuple-element.57.pre_ref, bf16[8,256,2048]{2,1,0:T(8,128)(2,1)} %get-tuple-element.58.g_all_ref, bf16[2048,2048]{1,0:T(8,128)(2,1)} %bitcast.27, ...), custom_call_target="tpu_custom_call" | custom-call | bytes 216000000 | tf_op jit(solution)/shard_map/pallas_call | solution.py:717
  304.7 0.0 copy-start.1
  304.7 1.0 copy-done.1
  305.6 0.0 copy-start.3
  305.6 0.7 copy-done.3
  306.3 0.0 reduce-scatter.6.cloned.1.call-update
  306.3 0.0 reduce-scatter.8.cloned.1.call-start
  306.4 0.0 reduce-scatter.4.cloned.1.call-done._
  306.4 78.2 %shard_map.233 = (bf16[8,256,768]{2,1,0:T(8,128)(2,1)}, bf16[8,256,2048]{2,1,0:T(8,128)(2,1)}, f32[8,1,768]{2,1,0:T(1,128)}, bf16[256,2048]{1,0:T(8,128)(2,1)}, f32[256,2048]{1,0:T(8,128)}) custom-call(bf16[256,2048]{1,0:T(8,128)(2,1)} %copy-done.1, bf16[256,2048]{1,0:T(8,128)(2,1)} %bitcast.35, bf16[2048,768]{1,0:T(8,128)(2,1)} %bitcast.31, ...), custom_call_target="tpu_custom_call" | custom-call | bytes 234000000 | tf_op jit(solution)/shard_map/pallas_call | solution.py:1076
  384.6 11.4 %bitcast_convert_fusion._ = bf16[2048,768]{1,0:T(8,128)(2,1)} fusion(bf16[8,256,2048]{2,1,0:T(8,128)(2,1)} %get-tuple-element.69, bf16[8,256,768]{2,1,0:T(8,128)(2,1)} %get-tuple-element.70), kind=kOutput, calls=%fused_computation | convolution fusion | flops 6444023808 | bytes 14680064 | tf_op jit(solution)/shard_map/dot_general | solution.py:828
  396.0 0.0 copy-start.6
  396.0 0.0 copy-start.4
  396.0 0.0 reduce-scatter.8.cloned.1.call-update
  396.0 1.6 copy-done.6
  397.5 1.1 convert_element_type.21
  398.7 0.0 copy-done.4
  398.7 1.3 convert_element_type.23
  399.9 7.4 %reduce-scatter.6.cloned.1.call-done = bf16[512,1408]{1,0:T(8,128)(2,1)} async-done(((bf16[2048,1408]{1,0:T(8,128)(2,1)}), bf16[512,1408]{1,0:T(8,128)(2,1)}) %reduce-scatter.6.cloned.1.call-update) | async-done | bytes 1441808 | tf_op jit(solution)/shard_map/reduce_scatter | solution.py:1127
  407.3 0.0 copy-start.5
  407.3 68.3 %shard_map.234 = (f32[256,2048]{1,0:T(8,128)}, bf16[8,64,1408]{2,1,0:T(8,128)(2,1)}, bf16[4,64,2048]{2,1,0:T(8,128)(2,1)}, f32[8,128]{1,0:T(8,128)}) custom-call(bf16[8,256,2048]{2,1,0:T(8,128)(2,1)} %get-tuple-element.71.part_ref, bf16[256,2048]{1,0:T(8,128)(2,1)} %x_ref.3, f32[4,2048]{1,0:T(4,128)} %get-tuple-element.49.norm_ref, ...), custom_call_target="tpu_custom_call" | custom-call | bytes 208800000 | tf_op jit(solution)/shard_map/pallas_call | solution.py:803
  475.6 0.7 slice.17
  476.3 0.6 reshape.71
  476.9 0.0 copy-done.5
  476.9 0.0 copy-start.7
  476.9 3.2 add.13._
  480.1 3.8 shard_map.235
  483.9 0.0 copy-done.7
  483.9 0.5 slice_bitcast_fusion
  484.4 0.7 reduce-scatter.8.cloned.1.call-done
  485.1 13.3 %shard_map.236.held_ref = bf16[8,64,768]{2,1,0:T(8,128)(2,1)} custom-call(bf16[8,64,768]{2,1,0:T(8,128)(2,1)} %bitcast.39, f32[256,2048]{1,0:T(8,128)} %add.13._, f32[64,5632]{1,0:T(8,128)} %get-tuple-element.46.__, f32[8,128]{1,0:T(8,128)} %get-tuple-element.78.___), custom_call_target="tpu_custom_call" | custom-call | bytes 50400000 | tf_op jit(solution)/shard_map/pallas_call | solution.py:343
  498.3 2.5 shard_map.237
Async XLA Ops:
  7.2 299.2 %reduce-scatter.4.cloned.1.call-start = ((), (), s32[]{:S(2)}) async-start(), calls=%async_computation.3 | async-start | bytes 3604480 | tf_op jit(solution)/shard_map/reduce_scatter | solution.py:1127
  193.8 54.1 %copy-start.2 = (f32[4,2048]{1,0:T(4,128)S(1)}, f32[4,2048]{1,0:T(4,128)}, u32[]{:S(2)}) copy-start(f32[4,2048]{1,0:T(4,128)} %get-tuple-element.49.norm_ref) | copy-start | bytes 98308
  247.9 1.2 copy-start
  247.9 159.4 %reduce-scatter.6.cloned.1.call-start = ((), (), s32[]{:S(2)}) async-start(), calls=%async_computation.4 | async-start | bytes 7208960 | tf_op jit(solution)/shard_map/reduce_scatter | solution.py:1127
  304.7 1.0 copy-start.1
  305.6 0.7 copy-start.3
  306.3 178.7 %reduce-scatter.8.cloned.1.call-start = ((), (), s32[]{:S(2)}) async-start(), calls=%async_computation.5 | async-start | bytes 3932160 | tf_op jit(solution)/shard_map/reduce_scatter | solution.py:1127
  396.0 1.6 copy-start.6
  396.0 2.7 copy-start.4
  407.3 69.6 %copy-start.5 = (f32[256,2048]{1,0:T(8,128)S(1)}, f32[256,2048]{1,0:T(8,128)}, u32[]{:S(2)}) copy-start(f32[256,2048]{1,0:T(8,128)} %get-tuple-element.67) | copy-start | bytes 6291460
  476.9 7.0 %copy-start.7 = (f32[8,128]{1,0:T(8,128)S(1)}, f32[8,128]{1,0:T(8,128)}, u32[]{:S(2)}) copy-start(f32[8,128]{1,0:T(8,128)} %get-tuple-element.78.___) | copy-start | bytes 12292
Sparse Core Ops, SparseCore 0:
  248.0 54.3 reduce-scatter.3
  306.4 100.8 reduce-scatter.5
  409.6 75.3 reduce-scatter.7

commit v6 on v5

--- a/solution.py
+++ b/solution.py
@@ -172,9 +172,12 @@
 
 
 def opening_kernel(
-    planes, qkv_ref, gate_ref, up_ref, x_ref, out_weight_ref, small_ref, place_ref, rate_ref,
-    pieces_ref, x_all_ref, w_qkv_ref, w_out_ref, tab_ref, norm_ref, b_ref, cut, landed, made, all_ref, places_ref, tables, *sems,
+    planes, qkv_ref, gate_ref, up_ref, x_ref, out_weight_ref, position_ref, bias_ref, *refs
 ):
+    vector_refs, rate_ref = refs[:4], refs[4]
+    pieces_ref, x_all_ref, w_qkv_ref, w_out_ref, tab_ref, norm_ref, b_ref = refs[5:12]
+    cut, landed, made, small_ref, place_ref, all_ref, places_ref, tables = refs[12:20]
+    sems = refs[20:]
     mine, base, _, _ = place()
     plane = base // TEAM
     swap, gather = Swap(made, pieces_ref, sems[:3]), Gather(x_ref, x_all_ref, sems[3:10])
@@ -183,6 +186,15 @@
     line = Line(planes, all_ref.at[plane], all_ref, sems[16:19], same=True, within=True)
     rows, heads = LineGather(planes, landed, w_qkv_ref, sems[19:22]), Swap(cut, landed, sems[22:25])
     outs = LineGather(planes, out_weight_ref, w_out_ref, sems[25:28])
+    depth = gate_ref.shape[0]
+    for row, ref in enumerate(vector_refs):
+        small_ref[row : row + 1, :depth] = ref[...].astype(F32).reshape(1, depth)
+    bias = bias_ref[...].astype(F32).reshape(1, bias_ref.shape[0])
+    for i in range(bias_ref.shape[0] // depth):
+        small_ref[4 + i : 5 + i, :depth] = bias[:, i * depth : (i + 1) * depth]
+    known = position_ref[...].astype(F32).reshape(1, position_ref.shape[0])
+    for i in range(position_ref.shape[0] // 128):
+        place_ref[i : i + 1, :] = known[:, i * 128 : (i + 1) * 128]
     for i in range(TEAM):
         cut[i] = slices(qkv_ref, [s * HEADS + z * TEAM + i for s in range(3) for z in range(planes)], HEAD_DIM)
     greet(swap.near + line.near)
@@ -208,7 +220,7 @@
 
     @pl.loop(0, TEAM)
     def _(i):
-        known = places_ref[i].astype(F32)
+        known = places_ref[i]
         for part in range(tables.shape[2] // 128):
             at = jnp.transpose(jnp.broadcast_to(known[part : part + 1, :], square))
             here = pl.ds(part * 128, 128)
@@ -225,8 +237,7 @@
     for stage in range(3, planes):
         rows.stage(stage)
     line.finish()
-    depth = gate_ref.shape[0]
-    each = [all_ref[z, i].astype(F32) for z in range(planes) for i in range(TEAM)]
+    each = [all_ref[z, i] for z in range(planes) for i in range(TEAM)]
     for i in range(4):
         norm_ref[i : i + 1, :] = jnp.concatenate([known[i : i + 1, :depth] for known in each], axis=1)
     per = qkv_ref.shape[1] // (planes * TEAM * depth)
@@ -234,7 +245,7 @@
     for part in range(3):
         for z in range(planes):
             head = part * HEADS + z * TEAM + mine
-            known = all_ref[head // per // TEAM, lax.rem(head // per, TEAM)].astype(F32)
+            known = all_ref[head // per // TEAM, lax.rem(head // per, TEAM)]
             row = lax.broadcasted_iota(jnp.int32, known.shape, 0) == 4 + lax.rem(head, per)
             bias.append(jnp.sum(jnp.where(row, known, 0.0), axis=0, keepdims=True)[:, :depth])
     b_ref[...] = jnp.concatenate(bias, axis=1)
@@ -245,7 +256,7 @@
     store.wait()
 
 
-def opening(qkv, gate, up, inputs, out_weight, small, positions, rate, planes, cid):
+def opening(qkv, gate, up, inputs, out_weight, positions, bias, vectors, rate, planes, cid):
     shape = (TEAM, gate.shape[0], 2 * gate.shape[1] // TEAM)
     heads = (TEAM, qkv.shape[0], qkv.shape[1] // TEAM)
     tables = (TEAM, 3, inputs.shape[0], 128)
@@ -260,14 +271,16 @@
             jax.ShapeDtypeStruct((4, inputs.shape[1]), F32),
             jax.ShapeDtypeStruct((1, heads[2]), F32),
         ],
-        in_specs=[VMEM] * 8,
+        in_specs=[VMEM] * 12,
         out_specs=[ANY] * 5 + [VMEM] * 2,
         scratch_shapes=[
             pltpu.VMEM(heads, BF16),
             pltpu.VMEM(heads, BF16),
             pltpu.VMEM(shape, BF16),
-            pltpu.VMEM((planes, TEAM) + small.shape, BF16),
-            pltpu.VMEM((TEAM,) + positions.shape, BF16),
+            pltpu.VMEM((8, 128), F32),
+            pltpu.VMEM((8, 128), F32),
+            pltpu.VMEM((planes, TEAM, 8, 128), F32),
+            pltpu.VMEM((TEAM, 8, 128), F32),
             pltpu.VMEM(tables, F32),
         ]
         + Swap.sems
@@ -280,7 +293,7 @@
         + [pltpu.SemaphoreType.DMA],
         cost_estimate=lasting(80),
         compiler_params=params(cid),
-    )(qkv, gate, up, inputs, out_weight, small, positions, rate)
+    )(qkv, gate, up, inputs, out_weight, positions, bias, *vectors, rate)
 
 
 def unslice(held, parts, planes, outs):
@@ -337,6 +350,36 @@
     greet(swap.near)
     swap.start()
     swap.finish()
+
+
+def both_close_kernel(planes, w_ref, shared_ref, _, __, held_ref, vector_ref, got, block, beyond, *sems):
+    swap, inner = Swap(w_ref, held_ref, sems[:3]), Swap(shared_ref, got, sems[3:6])
+    outer = Line(planes, block, beyond, sems[6:])
+    greet(swap.near + outer.near)
+    inner.start()
+    swap.start()
+    inner.finish()
+    block[...] = added(got)
+    outer.start()
+    outer.finish()
+    vector_ref[...] = added(beyond)
+    swap.finish()
+
+
+def both_closing(blocks, shared, after, cid):
+    planes = shared.shape[1]
+    return pl.pallas_call(
+        functools.partial(both_close_kernel, planes),
+        out_shape=[jax.ShapeDtypeStruct(blocks.shape, BF16), jax.ShapeDtypeStruct(shared.shape[2:], F32)],
+        in_specs=[VMEM, VMEM, ANY, ANY],
+        out_specs=[ANY, VMEM],
+        scratch_shapes=[pltpu.VMEM(shared.shape, F32)]
+        + [pltpu.VMEM(shared.shape[1:], F32)] * 2
+        + Swap.sems * 2
+        + Line.sems(planes),
+        cost_estimate=lasting(22),
+        compiler_params=params(cid),
+    )(blocks, shared, *after)
 
 
 def closing(blocks, after, cid):
@@ -543,7 +586,7 @@
     hidden = (gate_pre * jax.nn.sigmoid(gate_pre) * up_pre).astype(BF16)
     hidden_ref[0] = hidden
     held[step] = hidden
-    pl.when(step == TEAM - 2)(functools.partial(line.stage, 2))
+    pl.when(step == TEAM - 3)(functools.partial(line.stage, 2))
 
     @pl.when(step == TEAM - 1)
     def _():
@@ -600,7 +643,7 @@
 def mlp_back_kernel(
     pre_ref, g_all_ref, h_ref, wd_ref, w_ref, resid_ref, g_ref, norm_ref, _,
     out_ref, sums_ref, block_ref, grad_w_ref,
-    pre, g_all, turned, made, grads, away, w, resid, own_grad, *scratch,
+    pre, g_all, turned, made, grads, away, w, resid, own_grad, wd, *scratch,
 ):
     pre_sem, g_sem, turned_sem, made_sem, late_sem = scratch[11:]
     total = Sum(None, scratch[:4], scratch[4:11], away)
@@ -628,7 +671,7 @@
         copy.start()
     late = [
         pltpu.make_async_copy(src, dst, late_sem.at[i])
-        for i, (src, dst) in enumerate(((w_ref, w), (resid_ref, resid), (g_ref, own_grad)))
+        for i, (src, dst) in enumerate(((wd_ref, wd), (w_ref, w), (resid_ref, resid), (g_ref, own_grad)))
     ]
     for copy in late:
         copy.start()
@@ -646,7 +689,8 @@
 
         for copy in loads(i):
             copy.wait()
-        grad_hidden = dot(g_all[slot], wd_ref[...], NT)
+        pl.when(i == 0)(late[0].wait)
+        grad_hidden = dot(g_all[slot], wd[...], NT)
         gate_pre, up_pre = pre[slot, :, :ff], pre[slot, :, ff:]
         sigmoid = jax.nn.sigmoid(gate_pre)
         grad_gate = grad_hidden * up_pre * sigmoid * (1.0 + gate_pre * (1.0 - sigmoid))
@@ -657,7 +701,7 @@
         def make(to):
             to[k] = dot(grads[part, :], w[...], NT).astype(BF16)
 
-        pl.when(i == 0)(late[0].wait)
+        pl.when(i == 0)(late[1].wait)
 
         @pl.when(lax.rem(i, 2) == 0)
         def _():
@@ -693,7 +737,7 @@
         store_chunk(i).start()
 
     sums_ref[...] = jnp.zeros_like(sums_ref)
-    for copy in late[1:]:
+    for copy in late[2:]:
         copy.wait()
 
     def use(rows, value):
@@ -722,7 +766,7 @@
             jax.ShapeDtypeStruct((rows, width), BF16),
             jax.ShapeDtypeStruct((width, both), BF16),
         ],
-        in_specs=[ANY, ANY, ANY, VMEM, ANY, ANY, ANY, VMEM, ANY],
+        in_specs=[ANY, ANY, ANY, ANY, ANY, ANY, ANY, VMEM, ANY],
         out_specs=[VMEM, VMEM, VMEM, ANY],
         scratch_shapes=[
             pltpu.VMEM((2, rows, both), F32),
@@ -734,11 +778,12 @@
             pltpu.VMEM((width, both), BF16),
             pltpu.VMEM((rows, width), F32),
             pltpu.VMEM((rows, width), BF16),
+            pltpu.VMEM((both // 2, width), BF16),
         ]
         + Sum.scratch(rows, width)
         + Sum.sems
         + [two] * 4
-        + [pltpu.SemaphoreType.DMA((3,))],
+        + [pltpu.SemaphoreType.DMA((4,))],
         cost_estimate=lasting(60),
         compiler_params=params(cid, 50),
     )(pre, g_all, h_two, w_down, w_both, resid, out_grad, gain, after)
@@ -762,18 +807,15 @@
 
 
 def last_kernel(
-    planes, part_ref, x_ref, norm_ref, both_ref, branch_ref, sums_two_ref, bias_ref, _,
-    out_ref, held_ref, far_ref, vector_ref, sums, shared, got, block, beyond, *scratch,
+    planes, part_ref, x_ref, norm_ref, branch_ref, sums_two_ref, bias_ref, _,
+    out_ref, far_ref, shared_ref, sums, *scratch,
 ):
-    total, swap = Sum(part_ref, scratch[:4], scratch[4:11]), Swap(both_ref, held_ref, scratch[11:14])
-    line, inner = Line(planes, branch_ref, far_ref, scratch[14:17]), Swap(shared, got, scratch[17:20])
-    outer = Line(planes, block, beyond, scratch[20:])
-    greet(swap.near + line.near)
+    total, line = Sum(part_ref, scratch[:4], scratch[4:11]), Line(planes, branch_ref, far_ref, scratch[11:])
+    greet(total.near + line.near)
+    line.start()
     total.start()
-    line.start()
     total.middle()
     total.middle_two()
-    swap.start()
     sums[...] = jnp.zeros_like(sums)
 
     def use(rows, value):
@@ -785,18 +827,11 @@
     total.finish(use)
     vectors = [sums[:8, :], sums[8:, :], sums_two_ref[:8, :], sums_two_ref[8:, :]]
     depth = part_ref.shape[2] // (planes * TEAM)
-    share(shared, vectors, added(bias_ref), planes, bias_ref.shape[2] // (planes * depth), depth)
-    inner.start()
-    inner.finish()
-    block[...] = added(got)
-    outer.start()
-    outer.finish()
-    vector_ref[...] = added(beyond)
-    swap.finish()
+    share(shared_ref, vectors, added(bias_ref), planes, bias_ref.shape[2] // (planes * depth), depth)
     line.finish()
 
 
-def last(part, inputs, gain, both, branch, sums_two, bias, after, cid):
+def last(part, inputs, gain, branch, sums_two, bias, after, cid):
     rows, width = inputs.shape
     planes = branch.shape[0]
     vectors = (TEAM, planes, 8, 128)
@@ -804,24 +839,18 @@
         functools.partial(last_kernel, planes),
         out_shape=[
             jax.ShapeDtypeStruct((rows, width), F32),
-            jax.ShapeDtypeStruct(both.shape, BF16),
             jax.ShapeDtypeStruct(branch.shape, BF16),
-            jax.ShapeDtypeStruct(vectors[2:], F32),
+            jax.ShapeDtypeStruct(vectors, F32),
         ],
-        in_specs=[ANY, VMEM, VMEM, VMEM, VMEM, VMEM, VMEM, ANY],
-        out_specs=[VMEM, ANY, ANY, VMEM],
+        in_specs=[ANY, VMEM, VMEM, VMEM, VMEM, VMEM, ANY],
+        out_specs=[VMEM, ANY, VMEM],
         scratch_shapes=[pltpu.VMEM((16, width), F32)]
-        + [pltpu.VMEM(vectors, F32)] * 2
-        + [pltpu.VMEM(vectors[1:], F32)] * 2
         + Sum.scratch(rows, width)
         + Sum.sems
-        + Swap.sems
-        + Line.sems(planes)
-        + Swap.sems
         + Line.sems(planes),
         cost_estimate=lasting(58),
         compiler_params=params(cid),
-    )(part, inputs, gain, both, branch, sums_two, bias, after)
+    )(part, inputs, gain, branch, sums_two, bias, after)
 
 
 def dot(a, b, dims=((1,), (0,))):
@@ -1126,15 +1155,12 @@
     def line_sum(x):
         return lax.psum_scatter(x, "fsdp", scatter_dimension=0, tiled=True, axis_index_groups=lines)
 
-    small = jnp.stack([norm1_gain, norm1_bias, norm2_gain, norm2_bias])
-    small = jnp.concatenate([small, qkv_bias.reshape(-1, depth)])
-    small = jnp.pad(small, ((0, 16 - small.shape[0]), (0, 128 - depth)))
-    places = jnp.pad(positions.reshape(-1, 128).astype(BF16), ((0, 16 - rows // 128), (0, 0)))
     half = ROT // 2
     rate = 10000.0 ** (-np.arange(half) / half)
     rate = np.tile(np.concatenate([rate, rate, np.zeros(HEAD_DIM - ROT)]), 128 // HEAD_DIM)[None].astype(np.float32)
     both, x_all, w_qkv, w_out, tables, norms, b_qkv = opening(
-        qkv_weight, gate_weight, up_weight, inputs, out_weight, small, places, jnp.asarray(rate), planes, 1
+        qkv_weight, gate_weight, up_weight, inputs, out_weight, positions, qkv_bias,
+        (norm1_gain, norm1_bias, norm2_gain, norm2_bias), jnp.asarray(rate), planes, 1,
     )
     w_out = w_out.reshape(width, D)
     w_qkv = w_qkv.reshape(D, 3 * width)
@@ -1156,12 +1182,11 @@
     grad_qkv = grad_qkv.reshape(tokens, 3 * width)
     grad_w_qkv = dot(h_one.reshape(tokens, D), grad_qkv, TN).astype(BF16)
     part, grad_w_qkv = lax.optimization_barrier((part, grad_w_qkv))
+    branch = grad_out.reshape(planes, depth, D)
+    norm_part, branch, shared = last(part, inputs, norms, branch, sums_two, grad_bias, grad_w_qkv, 7)
+    grad_w_qkv = line_sum(grad_w_qkv)
     blocks = grad_w_both.reshape(TEAM, depth, 2 * planes * ff)
-    branch = grad_out.reshape(planes, depth, D)
-    norm_part, blocks, branch, sums = last(
-        part, inputs, norms, blocks, branch, sums_two, grad_bias, grad_w_qkv, 7
-    )
-    grad_w_qkv = line_sum(grad_w_qkv)
+    blocks, sums = both_closing(blocks, shared, (norm_part, branch), 9)
     block_out, input_grad = block_out.astype(BF16), grad_resid + norm_part
     grad_gate_w, grad_up_w, grad_out = first_grads(blocks, branch)
     blocks = closing(grad_w_qkv.reshape(TEAM, depth, 3 * width), (input_grad, grad_up_w, sums), 8)

time: 511 us -> 501 us (0.980)
  waiting for transfers between devices: 8.12 us -> 1.14 us
    pallas_call x0 -> x1, Pallas kernels: none -> 23.5 us  [both_closing(): pl.pallas_call(functools.partial(both_close_kernel, planes), out_shape=[j...]
    pallas_call x1, Pallas kernels: 68.3 us -> 48.4 us  [last(): pl.pallas_call(functools.partial(last_kernel, planes), out_shape=[jax.Sha...]
    reduce_scatter x3, waiting for transfers between devices: 8.07 us -> 1.09 us  [line_sum(): lax.psum_scatter(x, 'fsdp', scatter_dimension=0, tiled=True, axis_index_g...]
  transfers between devices with their start and end apart: 3 -> 3, of which waited for: 2 -> 1; matrix products, arithmetic and copies ran while one was open for 4% -> 4% of each run, Pallas kernels for 41% -> 42%
where the time goes in v6:
time: 501 us; the launch traced here: 500 us
  Pallas kernels  461 us (92%)
  between operations  13.9 us (3%)
  matrix products  11.4 us (2%)
  local copies, waits for them, and re-layouts  7 us (1%)
  other arithmetic  5.69 us (1%)
    pallas_call x1, Pallas kernels, attend(): pl.pallas_call(functools.partial(attend_kernel, planes), grid=(seqs,), in...  101 us
    pallas_call x1, Pallas kernels, opening(): pl.pallas_call(functools.partial(opening_kernel, planes), out_shape=[jax....  82.6 us
    pallas_call x1, Pallas kernels, attend_back(): pl.pallas_call(attend_back_kernel, grid=(seqs,), in_specs=[ANY, whole(wid...  79.5 us
    pallas_call x1, Pallas kernels, expand(): pl.pallas_call(functools.partial(expand_kernel, planes), grid=(seqs,), in...  53.7 us
    pallas_call x1, Pallas kernels, mlp_back(): pl.pallas_call(mlp_back_kernel, out_shape=[jax.ShapeDtypeStruct((rows, wi...  53.3 us
    pallas_call x1, Pallas kernels, last(): pl.pallas_call(functools.partial(last_kernel, planes), out_shape=[jax.Sha...  48.4 us
    pallas_call x1, Pallas kernels, both_closing(): pl.pallas_call(functools.partial(both_close_kernel, planes), out_shape=[j...  23.5 us
    pallas_call x1, Pallas kernels, closing(): pl.pallas_call(close_kernel, out_shape=jax.ShapeDtypeStruct(blocks.shape,...  13.3 us
  transfers between devices with their start and end apart: 3, of which 1 were waited for; matrix products, arithmetic and copies ran while one was open for 4% of the time, Pallas kernels for 42%

profile of v6, /device:TPU:0, one launch (start us, length us, event | category | flops | bytes accessed | tf_op | source)
XLA Modules:
  0.0 500.4 jit_solution(5426922551711943286)
XLA Ops:
  7.2 0.0 reduce-scatter.4.cloned.1.call-start
  7.2 82.6 %shard_map.229 = (bf16[8,64,1408]{2,1,0:T(8,128)(2,1)}, bf16[8,256,2048]{2,1,0:T(8,128)(2,1)}, bf16[4,8,64,768]{3,2,1,0:T(8,128)(2,1)}, bf16[4,64,2048]{2,1,0:T(...) custom-call(bf16[64,6144]{1,0:T(8,128)(2,1)} %qkv_ref.1, bf16[64,5632]{1,0:T(8,128)(2,1)} %gate_ref.1, ...), custom_call_target="tpu_custom_call" | custom-call | bytes 288000000 | tf_op jit(solution)/shard_map/pallas_call | solution.py:263
  89.9 100.7 %shard_map.230 = (bf16[8,256,2048]{2,1,0:T(8,128)(2,1)}, bf16[8,256,768]{2,1,0:T(8,128)(2,1)}, bf16[8,256,256]{2,1,0:T(8,128)(2,1)}, f32[256,2048]{1,0:T(8,128)}...) custom-call(bf16[8,256,2048]{2,1,0:T(8,128)(2,1)} %get-tuple-element.49.x_ref, ...), custom_call_target="tpu_custom_call" | custom-call | bytes 360000000 | tf_op jit(solution)/shard_map/pallas_call | solution.py:995
  190.6 0.0 copy-start.2
  190.6 53.7 %shard_map.231 = (f32[8,256,1408]{2,1,0:T(8,128)}, bf16[8,256,704]{2,1,0:T(8,128)(2,1)}, bf16[704,2048]{1,0:T(8,128)(2,1)}, bf16[8,256,2048]{2,1,0:T(8,128)(2,1)}, bf16[4,176,2048]{2,1,0:T(8,128)(2,1)}) custom-call(bf16[8,256,2048]{2,1,0:T(8,128)(2,1)} %get-tuple-element.56.h_ref, bf16[2048,1408]{1,0:T(8,128)(2,1)} %bitcast.22, bf16[256,2048]{1,0:T(8,128)(2,1)} %g_ref.3, ...), custom_call_target="tpu_custom_call" | custom-call | bytes 198000000 | tf_op jit(solution)/shard_map/pallas_call | solution.py:617
  244.3 0.0 copy-start
  244.3 0.0 reduce-scatter.4.cloned.1.call-update
  244.3 0.0 reduce-scatter.6.cloned.1.call-start
  244.3 0.0 copy-done.2
  244.4 1.1 copy-done
  245.5 53.3 %shard_map.232 = (f32[256,2048]{1,0:T(8,128)}, f32[16,2048]{1,0:T(8,128)S(1)}, bf16[256,2048]{1,0:T(8,128)(2,1)S(1)}, bf16[2048,1408]{1,0:T(8,128)(2,1)}) custom-call(f32[8,256,1408]{2,1,0:T(8,128)} %get-tuple-element.58.pre_ref, bf16[8,256,2048]{2,1,0:T(8,128)(2,1)} %get-tuple-element.59.g_all_ref, bf16[2048,2048]{1,0:T(8,128)(2,1)} %bitcast.21, ...), custom_call_target="tpu_custom_call" | custom-call | bytes 216000000 | tf_op jit(solution)/shard_map/pallas_call | solution.py:761
  298.8 0.0 copy-start.1
  298.8 1.0 copy-done.1
  299.7 0.0 copy-start.3
  299.7 0.7 copy-done.3
  300.4 0.0 reduce-scatter.6.cloned.1.call-update
  300.4 0.0 reduce-scatter.8.cloned.1.call-start
  300.5 0.0 reduce-scatter.4.cloned.1.call-done._
  300.5 79.5 %shard_map.233 = (bf16[8,256,768]{2,1,0:T(8,128)(2,1)}, bf16[8,256,2048]{2,1,0:T(8,128)(2,1)}, f32[8,1,768]{2,1,0:T(1,128)}, bf16[256,2048]{1,0:T(8,128)(2,1)}, f32[256,2048]{1,0:T(8,128)}) custom-call(bf16[256,2048]{1,0:T(8,128)(2,1)} %copy-done.1, bf16[256,2048]{1,0:T(8,128)(2,1)} %bitcast.29, bf16[2048,768]{1,0:T(8,128)(2,1)} %bitcast.25, ...), custom_call_target="tpu_custom_call" | custom-call | bytes 234000000 | tf_op jit(solution)/shard_map/pallas_call | solution.py:1105
  380.0 11.4 %bitcast_convert_fusion._ = bf16[2048,768]{1,0:T(8,128)(2,1)} fusion(bf16[8,256,2048]{2,1,0:T(8,128)(2,1)} %get-tuple-element.70, bf16[8,256,768]{2,1,0:T(8,128)(2,1)} %get-tuple-element.71), kind=kOutput, calls=%fused_computation | convolution fusion | flops 6444023808 | bytes 14680064 | tf_op jit(solution)/shard_map/dot_general | solution.py:857
  391.4 0.0 copy-start.6
  391.4 0.0 reduce-scatter.8.cloned.1.call-update
  391.4 1.6 copy-done.6
  393.0 1.1 convert_element_type.9
  394.1 0.0 copy-start.5
  394.1 48.4 %shard_map.234 = (f32[256,2048]{1,0:T(8,128)}, bf16[4,64,2048]{2,1,0:T(8,128)(2,1)}, f32[8,4,8,128]{3,2,1,0:T(8,128)}) custom-call(bf16[8,256,2048]{2,1,0:T(8,128)(2,1)} %get-tuple-element.72.part_ref, bf16[256,2048]{1,0:T(8,128)(2,1)} %x_ref.3, f32[4,2048]{1,0:T(4,128)} %get-tuple-element.50.norm_ref, bf16[4,64,2048]{2,1,0:T(8,128)(2,1)} %bitcast.32, ...), custom_call_target="tpu_custom_call" | custom-call | bytes 208800000 | tf_op jit(solution)/shard_map/pallas_call | solution.py:838
  442.5 0.0 copy-done.5
  442.5 0.0 copy-start.4
  442.5 3.3 add.9._
  445.8 0.0 copy-done.4
  445.8 1.3 convert_element_type.11
  447.1 0.0 reduce-scatter.6.cloned.1.call-done
  447.1 23.5 %shard_map.235 = (bf16[8,64,1408]{2,1,0:T(8,128)(2,1)}, f32[8,128]{1,0:T(8,128)}) custom-call(bf16[8,64,1408]{2,1,0:T(8,128)(2,1)} %bitcast.30, f32[8,4,8,128]{3,2,1,0:T(8,128)} %get-tuple-element.79.shared_ref, f32[256,2048]{1,0:T(8,128)} %get-tuple-element.77._, bf16[4,64,2048]{2,1,0:T(8,128)(2,1)} %get-tuple-element.80.__.far_ref), custom_call_target="tpu_custom_call" | custom-call | bytes 79200000 | tf_op jit(solution)/shard_map/pallas_call | solution.py:371
  470.6 0.7 slice.17
  471.2 0.6 reshape.65
  471.9 3.7 shard_map.236
  475.6 1.3 slice_bitcast_fusion
  477.0 1.1 reduce-scatter.8.cloned.1.call-done
  478.0 13.3 %shard_map.237.held_ref = bf16[8,64,768]{2,1,0:T(8,128)(2,1)} custom-call(bf16[8,64,768]{2,1,0:T(8,128)(2,1)} %bitcast.33, f32[256,2048]{1,0:T(8,128)} %add.9._, f32[64,5632]{1,0:T(8,128)} %get-tuple-element.47.__, f32[8,128]{1,0:T(8,128)} %get-tuple-element.81.___), custom_call_target="tpu_custom_call" | custom-call | bytes 50400000 | tf_op jit(solution)/shard_map/pallas_call | solution.py:386
  491.3 2.5 shard_map.238
Async XLA Ops:
  7.2 293.3 %reduce-scatter.4.cloned.1.call-start = ((), (), s32[]{:S(2)}) async-start(), calls=%async_computation.3 | async-start | bytes 3604480 | tf_op jit(solution)/shard_map/reduce_scatter | solution.py:1156
  190.6 53.8 %copy-start.2 = (f32[4,2048]{1,0:T(4,128)S(1)}, f32[4,2048]{1,0:T(4,128)}, u32[]{:S(2)}) copy-start(f32[4,2048]{1,0:T(4,128)} %get-tuple-element.50.norm_ref) | copy-start | bytes 98308
  244.3 1.2 copy-start
  244.3 202.8 %reduce-scatter.6.cloned.1.call-start = ((), (), s32[]{:S(2)}) async-start(), calls=%async_computation.4 | async-start | bytes 7208960 | tf_op jit(solution)/shard_map/reduce_scatter | solution.py:1156
  298.8 1.0 copy-start.1
  299.7 0.7 copy-start.3
  300.4 177.6 %reduce-scatter.8.cloned.1.call-start = ((), (), s32[]{:S(2)}) async-start(), calls=%async_computation.5 | async-start | bytes 3932160 | tf_op jit(solution)/shard_map/reduce_scatter | solution.py:1156
  391.4 1.6 copy-start.6
  394.1 48.4 %copy-start.5 = (f32[256,2048]{1,0:T(8,128)S(1)}, f32[256,2048]{1,0:T(8,128)}, u32[]{:S(2)}) copy-start(f32[256,2048]{1,0:T(8,128)} %get-tuple-element.68) | copy-start | bytes 6291460
  442.5 3.3 copy-start.4
Sparse Core Ops, SparseCore 0:
  244.4 53.6 reduce-scatter.3
  300.5 110.7 reduce-scatter.5
  413.6 64.3 reduce-scatter.7

commit v7 on v6

--- a/solution.py
+++ b/solution.py
@@ -169,131 +169,6 @@
 
 def slices(ref, pieces, size):
     return jnp.concatenate([ref[:, i * size : (i + 1) * size] for i in pieces], axis=1)
-
-
-def opening_kernel(
-    planes, qkv_ref, gate_ref, up_ref, x_ref, out_weight_ref, position_ref, bias_ref, *refs
-):
-    vector_refs, rate_ref = refs[:4], refs[4]
-    pieces_ref, x_all_ref, w_qkv_ref, w_out_ref, tab_ref, norm_ref, b_ref = refs[5:12]
-    cut, landed, made, small_ref, place_ref, all_ref, places_ref, tables = refs[12:20]
-    sems = refs[20:]
-    mine, base, _, _ = place()
-    plane = base // TEAM
-    swap, gather = Swap(made, pieces_ref, sems[:3]), Gather(x_ref, x_all_ref, sems[3:10])
-    vectors = Swap(small_ref, all_ref.at[plane], sems[10:13], same=True)
-    places = Swap(place_ref, places_ref, sems[13:16], same=True, near_first=True)
-    line = Line(planes, all_ref.at[plane], all_ref, sems[16:19], same=True, within=True)
-    rows, heads = LineGather(planes, landed, w_qkv_ref, sems[19:22]), Swap(cut, landed, sems[22:25])
-    outs = LineGather(planes, out_weight_ref, w_out_ref, sems[25:28])
-    depth = gate_ref.shape[0]
-    for row, ref in enumerate(vector_refs):
-        small_ref[row : row + 1, :depth] = ref[...].astype(F32).reshape(1, depth)
-    bias = bias_ref[...].astype(F32).reshape(1, bias_ref.shape[0])
-    for i in range(bias_ref.shape[0] // depth):
-        small_ref[4 + i : 5 + i, :depth] = bias[:, i * depth : (i + 1) * depth]
-    known = position_ref[...].astype(F32).reshape(1, position_ref.shape[0])
-    for i in range(position_ref.shape[0] // 128):
-        place_ref[i : i + 1, :] = known[:, i * 128 : (i + 1) * 128]
-    for i in range(TEAM):
-        cut[i] = slices(qkv_ref, [s * HEADS + z * TEAM + i for s in range(3) for z in range(planes)], HEAD_DIM)
-    greet(swap.near + line.near)
-    outs.start()
-    heads.start()
-    vectors.start()
-    places.start()
-    size = gate_ref.shape[1] // (planes * TEAM)
-    for i in range(TEAM):
-        units = [z * TEAM + i for z in range(planes)]
-        made[i] = jnp.concatenate([slices(gate_ref, units, size), slices(up_ref, units, size)], axis=1)
-    outs.stage(2)
-    heads.finish()
-    rows.start()
-    gather.start()
-    swap.start()
-    vectors.finish()
-    line.start()
-    for stage in range(3, planes):
-        outs.stage(stage)
-    places.finish()
-    square = (128, 128)
-
-    @pl.loop(0, TEAM)
-    def _(i):
-        known = places_ref[i]
-        for part in range(tables.shape[2] // 128):
-            at = jnp.transpose(jnp.broadcast_to(known[part : part + 1, :], square))
-            here = pl.ds(part * 128, 128)
-            angle = at * rate_ref[...]
-            tables[i, 0, here, :] = jnp.cos(angle)
-            tables[i, 1, here, :] = jnp.sin(angle)
-            token = lax.broadcasted_iota(jnp.int32, square, 0) + part * 128
-            tables[i, 2, here, :] = token.astype(F32) - at
-
-    store = pltpu.make_async_copy(tables, tab_ref, sems[28])
-    store.start()
-    rows.stage(2)
-    gather.middle()
-    for stage in range(3, planes):
-        rows.stage(stage)
-    line.finish()
-    each = [all_ref[z, i] for z in range(planes) for i in range(TEAM)]
-    for i in range(4):
-        norm_ref[i : i + 1, :] = jnp.concatenate([known[i : i + 1, :depth] for known in each], axis=1)
-    per = qkv_ref.shape[1] // (planes * TEAM * depth)
-    bias = []
-    for part in range(3):
-        for z in range(planes):
-            head = part * HEADS + z * TEAM + mine
-            known = all_ref[head // per // TEAM, lax.rem(head // per, TEAM)]
-            row = lax.broadcasted_iota(jnp.int32, known.shape, 0) == 4 + lax.rem(head, per)
-            bias.append(jnp.sum(jnp.where(row, known, 0.0), axis=0, keepdims=True)[:, :depth])
-    b_ref[...] = jnp.concatenate(bias, axis=1)
-    gather.finish()
-    swap.finish()
-    rows.finish()
-    outs.finish()
-    store.wait()
-
-
-def opening(qkv, gate, up, inputs, out_weight, positions, bias, vectors, rate, planes, cid):
-    shape = (TEAM, gate.shape[0], 2 * gate.shape[1] // TEAM)
-    heads = (TEAM, qkv.shape[0], qkv.shape[1] // TEAM)
-    tables = (TEAM, 3, inputs.shape[0], 128)
-    return pl.pallas_call(
-        functools.partial(opening_kernel, planes),
-        out_shape=[
-            jax.ShapeDtypeStruct(shape, BF16),
-            jax.ShapeDtypeStruct((TEAM,) + inputs.shape, BF16),
-            jax.ShapeDtypeStruct((planes,) + heads, BF16),
-            jax.ShapeDtypeStruct((planes,) + out_weight.shape, BF16),
-            jax.ShapeDtypeStruct(tables, F32),
-            jax.ShapeDtypeStruct((4, inputs.shape[1]), F32),
-            jax.ShapeDtypeStruct((1, heads[2]), F32),
-        ],
-        in_specs=[VMEM] * 12,
-        out_specs=[ANY] * 5 + [VMEM] * 2,
-        scratch_shapes=[
-            pltpu.VMEM(heads, BF16),
-            pltpu.VMEM(heads, BF16),
-            pltpu.VMEM(shape, BF16),
-            pltpu.VMEM((8, 128), F32),
-            pltpu.VMEM((8, 128), F32),
-            pltpu.VMEM((planes, TEAM, 8, 128), F32),
-            pltpu.VMEM((TEAM, 8, 128), F32),
-            pltpu.VMEM(tables, F32),
-        ]
-        + Swap.sems
-        + Gather.sems
-        + Swap.sems * 2
-        + Line.sems(planes)
-        + LineGather.sems(planes)
-        + Swap.sems
-        + LineGather.sems(planes)
-        + [pltpu.SemaphoreType.DMA],
-        cost_estimate=lasting(80),
-        compiler_params=params(cid),
-    )(qkv, gate, up, inputs, out_weight, positions, bias, *vectors, rate)
 
 
 def unslice(held, parts, planes, outs):
@@ -908,44 +783,122 @@
     return exponent / jnp.sum(exponent, axis=-1, keepdims=True)
 
 
-def attend_kernel(
-    planes, x_ref, norm_ref, w_ref, b_ref, wo_ref, tab_ref, both_ref,
-    h_ref, qkv_ref, attn_ref, resid_ref, h_two_ref, w_both_ref, block, away, w, *scratch,
-):
-    total, gather = Sum(None, scratch[:4], scratch[4:11], away), Gather(block, h_two_ref, scratch[11:18])
-    line = LineGather(planes, both_ref, w_both_ref, scratch[18:21])
+def attend_kernel(planes, qkv_w_ref, gate_ref, up_ref, x_ref, out_weight_ref, position_ref, bias_ref, *refs):
+    vector_refs, rate_ref = refs[:4], refs[4]
+    h_ref, qkv_ref, attn_ref, resid_ref, h_two_ref, w_both_ref, w_qkv_ref, w_out_ref, tab_ref, norm_ref = refs[5:15]
+    cut, landed, made, both, small_ref, place_ref, all_ref, places_ref, tables = refs[15:24]
+    x_all, w, wo, norms, b, block, away = refs[24:31]
+    sems, scratch = refs[31:60], refs[60:]
+    mine, base, _, _ = place()
+    plane = base // TEAM
+    swap, gather = Swap(made, both, sems[:3]), Gather(x_ref, x_all, sems[3:10])
+    vectors = Swap(small_ref, all_ref.at[plane], sems[10:13], same=True)
+    places = Swap(place_ref, places_ref, sems[13:16], same=True, near_first=True)
+    line = Line(planes, all_ref.at[plane], all_ref, sems[16:19], same=True, within=True)
+    rows, heads = LineGather(planes, landed, w, sems[19:22]), Swap(cut, landed, sems[22:25])
+    outs = LineGather(planes, out_weight_ref, wo, sems[25:28])
+    total, spread = Sum(None, scratch[:4], scratch[4:11], away), Gather(block, h_two_ref, scratch[11:18])
+    wide_line = LineGather(planes, both, w_both_ref, scratch[18:21])
+    stores = [
+        pltpu.make_async_copy(src, dst, scratch[21].at[i])
+        for i, (src, dst) in enumerate(((w, w_qkv_ref), (wo, w_out_ref), (tables, tab_ref)))
+    ]
     step = pl.program_id(0)
+    slot = TEAM - 1 - step
 
     @pl.when(step == 0)
     def _():
-        greet(total.near + line.near)
+        depth = gate_ref.shape[0]
+        for row, ref in enumerate(vector_refs):
+            small_ref[row : row + 1, :depth] = ref[...].astype(F32).reshape(1, depth)
+        bias = bias_ref[...].astype(F32).reshape(1, bias_ref.shape[0])
+        for i in range(bias_ref.shape[0] // depth):
+            small_ref[4 + i : 5 + i, :depth] = bias[:, i * depth : (i + 1) * depth]
+        known = position_ref[...].astype(F32).reshape(1, position_ref.shape[0])
+        for i in range(position_ref.shape[0] // 128):
+            place_ref[i : i + 1, :] = known[:, i * 128 : (i + 1) * 128]
+        for i in range(TEAM):
+            cut[i] = slices(qkv_w_ref, [s * HEADS + z * TEAM + i for s in range(3) for z in range(planes)], HEAD_DIM)
+        greet(swap.near + line.near)
+        outs.start()
+        heads.start()
+        vectors.start()
+        places.start()
+        size = gate_ref.shape[1] // (planes * TEAM)
+        for i in range(TEAM):
+            units = [z * TEAM + i for z in range(planes)]
+            made[i] = jnp.concatenate([slices(gate_ref, units, size), slices(up_ref, units, size)], axis=1)
+        outs.stage(2)
+        heads.finish()
+        rows.start()
+        gather.start()
+        swap.start()
+        vectors.finish()
         line.start()
-        weights = pltpu.make_async_copy(w_ref, w, scratch[21])
-        weights.start()
-        weights.wait()
-
-    pl.when(step == TEAM - 2)(functools.partial(line.stage, 2))
-    stream = x_ref[0].astype(F32)
+        for stage in range(3, planes):
+            outs.stage(stage)
+        places.finish()
+        square = (128, 128)
+
+        @pl.loop(0, TEAM)
+        def _(i):
+            known = places_ref[i]
+            for part in range(tables.shape[2] // 128):
+                at = jnp.transpose(jnp.broadcast_to(known[part : part + 1, :], square))
+                here = pl.ds(part * 128, 128)
+                angle = at * rate_ref[...]
+                tables[i, 0, here, :] = jnp.cos(angle)
+                tables[i, 1, here, :] = jnp.sin(angle)
+                token = lax.broadcasted_iota(jnp.int32, square, 0) + part * 128
+                tables[i, 2, here, :] = token.astype(F32) - at
+
+        rows.stage(2)
+        gather.middle()
+        for stage in range(3, planes):
+            rows.stage(stage)
+        line.finish()
+        each = [all_ref[z, i] for z in range(planes) for i in range(TEAM)]
+        for i in range(4):
+            norms[i : i + 1, :] = jnp.concatenate([known[i : i + 1, :depth] for known in each], axis=1)
+        per = qkv_w_ref.shape[1] // (planes * TEAM * depth)
+        bias = []
+        for part in range(3):
+            for z in range(planes):
+                head = part * HEADS + z * TEAM + mine
+                known = all_ref[head // per // TEAM, lax.rem(head // per, TEAM)]
+                row = lax.broadcasted_iota(jnp.int32, known.shape, 0) == 4 + lax.rem(head, per)
+                bias.append(jnp.sum(jnp.where(row, known, 0.0), axis=0, keepdims=True)[:, :depth])
+        b[...] = jnp.concatenate(bias, axis=1)
+        gather.finish()
+        swap.finish()
+        rows.finish()
+        outs.finish()
+        wide_line.start()
+        for copy in stores:
+            copy.start()
+
+    pl.when(step == TEAM - 2)(functools.partial(wide_line.stage, 2))
+    stream = x_all[slot].astype(F32)
     normed, _ = normalize(stream)
-    h_one = (normed * norm_ref[0:1, :] + norm_ref[1:2, :]).astype(BF16)
+    h_one = (normed * norms[0:1, :] + norms[1:2, :]).astype(BF16)
     h_ref[0] = h_one
-    qkv = dot(h_one, w[...]) + b_ref[...]
+    qkv = dot(h_one, w[...].reshape(-1, w.shape[-1])) + b[...]
     width = LOCAL * HEAD_DIM
-    cosine, sine = wide(tab_ref[0, 0]), wide(tab_ref[0, 1])
+    cosine, sine = wide(tables[slot, 0]), wide(tables[slot, 1])
     query = turn(qkv[:, :width], cosine, sine).astype(BF16)
     key = turn(qkv[:, width : 2 * width], cosine, sine).astype(BF16)
     value = qkv[:, 2 * width :].astype(BF16)
     qkv_ref[0, :, :width] = query
     qkv_ref[0, :, width : 2 * width] = key
     qkv_ref[0, :, 2 * width :] = value
-    allowed = visible(tab_ref[0, 2])
+    allowed = visible(tables[slot, 2])
     mixed = jnp.zeros((query.shape[0], width), F32)
     for h in range(LOCAL):
         probs = soft(head_of(query, h), key, allowed).astype(BF16)
         mixed = mixed + dot(probs, head_of(value, h))
     attn_low = mixed.astype(BF16)
     attn_ref[0] = attn_low
-    part = dot(attn_low, wo_ref[...]).astype(BF16)
+    part = dot(attn_low, wo[...].reshape(-1, D)).astype(BF16)
     k = 3 - step // 2
 
     @pl.when(lax.rem(step, 2) == 0)
@@ -961,20 +914,23 @@
         pl.when(step == at)(advance)
 
     def use(rows, value):
-        resid = x_ref[0, rows, :].astype(F32) + value
+        resid = x_all[0, rows, :].astype(F32) + value
         resid_ref[rows, :] = resid
         normed, _ = normalize(resid)
-        block[rows, :] = (normed * norm_ref[2:3, :] + norm_ref[3:4, :]).astype(BF16)
+        block[rows, :] = (normed * norms[2:3, :] + norms[3:4, :]).astype(BF16)
 
     @pl.when(step == TEAM - 1)
     def _():
         total.finish(use)
-        gather.start()
+        spread.start()
         for stage in range(3, planes):
-            line.stage(stage)
-        gather.middle()
-        gather.finish()
-        line.finish()
+            wide_line.stage(stage)
+        spread.middle()
+        norm_ref[...] = norms[...]
+        spread.finish()
+        wide_line.finish()
+        for copy in stores:
+            copy.wait()
 
 
 def per_seq(*shape):
@@ -985,47 +941,71 @@
     return pl.BlockSpec(shape, lambda s: (0,) * len(shape))
 
 
-def attend(x_all, norms, w_qkv, b_qkv, w_out, tables, both, planes, cid):
-    seqs, rows, _ = x_all.shape
-    width = LOCAL * HEAD_DIM
+def attend(qkv, gate, up, inputs, out_weight, positions, bias, vectors, rate, planes, cid):
+    rows, _ = inputs.shape
+    depth, width = qkv.shape[0], LOCAL * HEAD_DIM
+    heads, units = (TEAM, depth, 3 * width), (TEAM, depth, 2 * gate.shape[1] // TEAM)
+    tables = (TEAM, 3, rows, 128)
+    known = [
+        jax.ShapeDtypeStruct((planes,) + units, BF16),
+        jax.ShapeDtypeStruct((planes,) + heads, BF16),
+        jax.ShapeDtypeStruct((planes,) + out_weight.shape, BF16),
+        jax.ShapeDtypeStruct(tables, F32),
+    ]
 
     def far_first(*shape):
-        return pl.BlockSpec((1,) + shape, lambda s: (seqs - 1 - s,) + (0,) * len(shape))
+        return pl.BlockSpec((1,) + shape, lambda s: (TEAM - 1 - s,) + (0,) * len(shape))
 
     return pl.pallas_call(
         functools.partial(attend_kernel, planes),
-        grid=(seqs,),
-        in_specs=[
-            far_first(rows, D),
-            whole(4, D),
-            ANY,
-            whole(1, 3 * width),
-            whole(width, D),
-            far_first(3, rows, 128),
-            VMEM,
-        ],
-        out_specs=[far_first(rows, D), far_first(rows, 3 * width), far_first(rows, width), whole(rows, D), ANY, ANY],
+        grid=(TEAM,),
+        in_specs=[VMEM] * 12,
+        out_specs=[far_first(rows, D), far_first(rows, 3 * width), far_first(rows, width), whole(rows, D)]
+        + [ANY] * 5
+        + [whole(4, D)],
         out_shape=[
-            jax.ShapeDtypeStruct((seqs, rows, D), BF16),
-            jax.ShapeDtypeStruct((seqs, rows, 3 * width), BF16),
-            jax.ShapeDtypeStruct((seqs, rows, width), BF16),
+            jax.ShapeDtypeStruct((TEAM, rows, D), BF16),
+            jax.ShapeDtypeStruct((TEAM, rows, 3 * width), BF16),
+            jax.ShapeDtypeStruct((TEAM, rows, width), BF16),
             jax.ShapeDtypeStruct((rows, D), F32),
-            jax.ShapeDtypeStruct((seqs, rows, D), BF16),
-            jax.ShapeDtypeStruct((planes,) + both.shape, BF16),
-        ],
+            jax.ShapeDtypeStruct((TEAM, rows, D), BF16),
+        ]
+        + known
+        + [jax.ShapeDtypeStruct((4, D), F32)],
         scratch_shapes=[
+            pltpu.VMEM(heads, BF16),
+            pltpu.VMEM(heads, BF16),
+            pltpu.VMEM(units, BF16),
+            pltpu.VMEM(units, BF16),
+            pltpu.VMEM((8, 128), F32),
+            pltpu.VMEM((8, 128), F32),
+            pltpu.VMEM((planes, TEAM, 8, 128), F32),
+            pltpu.VMEM((TEAM, 8, 128), F32),
+            pltpu.VMEM(tables, F32),
+            pltpu.VMEM((TEAM, rows, D), BF16),
+            pltpu.VMEM((planes,) + heads, BF16),
+            pltpu.VMEM((planes,) + out_weight.shape, BF16),
+            pltpu.VMEM((4, D), F32),
+            pltpu.VMEM((1, 3 * width), F32),
             pltpu.VMEM((rows, D), BF16),
             pltpu.VMEM((4, rows, D), BF16),
-            pltpu.VMEM((D, 3 * width), BF16),
         ]
+        + Swap.sems
+        + Gather.sems
+        + Swap.sems * 2
+        + Line.sems(planes)
+        + LineGather.sems(planes)
+        + Swap.sems
+        + LineGather.sems(planes)
+        + [pltpu.SemaphoreType.DMA]
         + Sum.scratch(rows, D)
         + Sum.sems
         + Gather.sems
         + LineGather.sems(planes)
-        + [pltpu.SemaphoreType.DMA],
-        cost_estimate=lasting(100),
+        + [pltpu.SemaphoreType.DMA((3,))],
+        cost_estimate=lasting(180),
         compiler_params=params(cid),
-    )(x_all, norms, w_qkv, b_qkv, w_out, tables, both)
+    )(qkv, gate, up, inputs, out_weight, positions, bias, *vectors, rate)
 
 
 def attend_back_kernel(
@@ -1158,17 +1138,12 @@
     half = ROT // 2
     rate = 10000.0 ** (-np.arange(half) / half)
     rate = np.tile(np.concatenate([rate, rate, np.zeros(HEAD_DIM - ROT)]), 128 // HEAD_DIM)[None].astype(np.float32)
-    both, x_all, w_qkv, w_out, tables, norms, b_qkv = opening(
+    h_one, qkv, attn_low, resid, h_two, w_both, w_qkv, w_out, tables, norms = attend(
         qkv_weight, gate_weight, up_weight, inputs, out_weight, positions, qkv_bias,
         (norm1_gain, norm1_bias, norm2_gain, norm2_bias), jnp.asarray(rate), planes, 1,
     )
+    w_both, w_qkv = w_both.reshape(D, 2 * planes * ff), w_qkv.reshape(D, 3 * width)
     w_out = w_out.reshape(width, D)
-    w_qkv = w_qkv.reshape(D, 3 * width)
-    both = both.reshape(TEAM * depth, 2 * planes * ff)
-    h_one, qkv, attn_low, resid, h_two, w_both = attend(
-        x_all, norms, w_qkv, b_qkv, w_out, tables, both, planes, 2
-    )
-    w_both = w_both.reshape(D, 2 * planes * ff)
     pre, hidden, grad_down, g_all, w_down = expand(h_two, w_both, out_grad, down_weight, planes, 3)
     w_down = w_down.reshape(planes * ff, D)
     grad_resid, sums_two, block, grad_w_both = mlp_back(

time: 501 us -> 500 us (level)
    pallas_call x2 -> x1, Pallas kernels: 183 us -> 178 us  [attend(): pl.pallas_call(functools.partial(attend_kernel, planes), grid=(TEAM,), in...]
  transfers between devices with their start and end apart: 3 -> 3, of which waited for: 1 -> 2; matrix products, arithmetic and copies ran while one was open for 4% -> 4% of each run, Pallas kernels for 42% -> 42%
where the time goes in v7:
time: 500 us; the launch traced here: 499 us
  Pallas kernels  456 us (91%)
  between operations  13.9 us (3%)
  matrix products  11.5 us (2%)
  local copies, waits for them, and re-layouts  7.01 us (1%)
  other arithmetic  5.69 us (1%)
    pallas_call x1, Pallas kernels, attend(): pl.pallas_call(functools.partial(attend_kernel, planes), grid=(TEAM,), in...  178 us
    pallas_call x1, Pallas kernels, attend_back(): pl.pallas_call(attend_back_kernel, grid=(seqs,), in_specs=[ANY, whole(wid...  79.1 us
    pallas_call x1, Pallas kernels, expand(): pl.pallas_call(functools.partial(expand_kernel, planes), grid=(seqs,), in...  54 us
    pallas_call x1, Pallas kernels, mlp_back(): pl.pallas_call(mlp_back_kernel, out_shape=[jax.ShapeDtypeStruct((rows, wi...  52.7 us
    pallas_call x1, Pallas kernels, last(): pl.pallas_call(functools.partial(last_kernel, planes), out_shape=[jax.Sha...  48.7 us
    pallas_call x1, Pallas kernels, both_closing(): pl.pallas_call(functools.partial(both_close_kernel, planes), out_shape=[j...  23.9 us
    pallas_call x1, Pallas kernels, closing(): pl.pallas_call(close_kernel, out_shape=jax.ShapeDtypeStruct(blocks.shape,...  13.3 us
    dot_general x1, matrix products, dot(): return lax.dot_general(a, b, (dims, ((), ())), preferred_element_type=F32)  11.5 us
  transfers between devices with their start and end apart: 3, of which 2 were waited for; matrix products, arithmetic and copies ran while one was open for 4% of the time, Pallas kernels for 42%

profile of v7, /device:TPU:0, one launch (start us, length us, event | category | flops | bytes accessed | tf_op | source)
XLA Modules:
  0.0 498.9 jit_solution(4912385726479815714)
XLA Ops:
  7.2 0.0 reduce-scatter.4.cloned.1.call-start
  7.2 178.0 %shard_map.229 = (bf16[8,256,2048]{2,1,0:T(8,128)(2,1)}, bf16[8,256,768]{2,1,0:T(8,128)(2,1)}, bf16[8,256,256]{2,1,0:T(8,128)(2,1)}, f32[256,2048]{1,0:T(8,128)}...) custom-call(bf16[64,6144]{1,0:T(8,128)(2,1)} %qkv_w_ref.1, ...), custom_call_target="tpu_custom_call" | custom-call | bytes 648000000 | tf_op jit(solution)/shard_map/pallas_call | solution.py:959
  185.2 0.0 copy-start.3
  185.2 54.0 %shard_map.230 = (f32[8,256,1408]{2,1,0:T(8,128)}, bf16[8,256,704]{2,1,0:T(8,128)(2,1)}, bf16[704,2048]{1,0:T(8,128)(2,1)}, bf16[8,256,2048]{2,1,0:T(8,128)(2,1)}, bf16[4,176,2048]{2,1,0:T(8,128)(2,1)}) custom-call(bf16[8,256,2048]{2,1,0:T(8,128)(2,1)} %get-tuple-element.46.h_ref, bf16[2048,1408]{1,0:T(8,128)(2,1)} %bitcast.21, bf16[256,2048]{1,0:T(8,128)(2,1)} %g_ref.3, ...), custom_call_target="tpu_custom_call" | custom-call | bytes 198000000 | tf_op jit(solution)/shard_map/pallas_call | solution.py:492
  239.2 0.0 copy-start
  239.2 0.0 reduce-scatter.4.cloned.1.call-update
  239.2 0.0 reduce-scatter.6.cloned.1.call-start
  239.3 0.0 copy-done.3
  239.3 1.1 copy-done
  240.4 52.7 %shard_map.231 = (f32[256,2048]{1,0:T(8,128)}, f32[16,2048]{1,0:T(8,128)S(1)}, bf16[256,2048]{1,0:T(8,128)(2,1)S(1)}, bf16[2048,1408]{1,0:T(8,128)(2,1)}) custom-call(f32[8,256,1408]{2,1,0:T(8,128)} %get-tuple-element.48.pre_ref, bf16[8,256,2048]{2,1,0:T(8,128)(2,1)} %get-tuple-element.49.g_all_ref, bf16[2048,2048]{1,0:T(8,128)(2,1)} %bitcast.20, ...), custom_call_target="tpu_custom_call" | custom-call | bytes 216000000 | tf_op jit(solution)/shard_map/pallas_call | solution.py:636
  293.1 0.0 copy-start.1
  293.2 1.0 copy-done.1
  294.1 0.0 copy-start.2
  294.1 0.7 copy-done.2
  294.8 0.0 reduce-scatter.6.cloned.1.call-update
  294.8 0.0 reduce-scatter.8.cloned.1.call-start
  294.8 1.4 reduce-scatter.4.cloned.1.call-done._
  296.3 79.1 %shard_map.232 = (bf16[8,256,768]{2,1,0:T(8,128)(2,1)}, bf16[8,256,2048]{2,1,0:T(8,128)(2,1)}, f32[8,1,768]{2,1,0:T(1,128)}, bf16[256,2048]{1,0:T(8,128)(2,1)}, f32[256,2048]{1,0:T(8,128)}) custom-call(bf16[256,2048]{1,0:T(8,128)(2,1)} %copy-done.1, bf16[256,2048]{1,0:T(8,128)(2,1)} %bitcast.28, bf16[2048,768]{1,0:T(8,128)(2,1)} %bitcast.25, ...), custom_call_target="tpu_custom_call" | custom-call | bytes 234000000 | tf_op jit(solution)/shard_map/pallas_call | solution.py:1085
  375.4 11.5 %bitcast_convert_fusion._ = bf16[2048,768]{1,0:T(8,128)(2,1)} fusion(bf16[8,256,2048]{2,1,0:T(8,128)(2,1)} %get-tuple-element.64, bf16[8,256,768]{2,1,0:T(8,128)(2,1)} %get-tuple-element.65), kind=kOutput, calls=%fused_computation | convolution fusion | flops 6444023808 | bytes 14680064 | tf_op jit(solution)/shard_map/dot_general | solution.py:732
  386.9 0.0 copy-start.6
  386.9 0.0 reduce-scatter.8.cloned.1.call-update
  386.9 1.6 copy-done.6
  388.5 1.1 convert_element_type.9
  389.6 0.0 copy-start.5
  389.6 48.7 %shard_map.233 = (f32[256,2048]{1,0:T(8,128)}, bf16[4,64,2048]{2,1,0:T(8,128)(2,1)}, f32[8,4,8,128]{3,2,1,0:T(8,128)}) custom-call(bf16[8,256,2048]{2,1,0:T(8,128)(2,1)} %get-tuple-element.66.part_ref, bf16[256,2048]{1,0:T(8,128)(2,1)} %x_ref.3, f32[4,2048]{1,0:T(4,128)} %get-tuple-element.52.norm_ref, bf16[4,64,2048]{2,1,0:T(8,128)(2,1)} %bitcast.27, ...), custom_call_target="tpu_custom_call" | custom-call | bytes 208800000 | tf_op jit(solution)/shard_map/pallas_call | solution.py:713
  438.4 0.0 copy-done.5
  438.4 0.0 copy-start.4
  438.4 3.3 add.9._
  441.7 0.0 copy-done.4
  441.7 1.3 convert_element_type.11
  443.0 0.0 reduce-scatter.6.cloned.1.call-done
  443.0 23.9 %shard_map.234 = (bf16[8,64,1408]{2,1,0:T(8,128)(2,1)}, f32[8,128]{1,0:T(8,128)}) custom-call(bf16[8,64,1408]{2,1,0:T(8,128)(2,1)} %bitcast.26, f32[8,4,8,128]{3,2,1,0:T(8,128)} %get-tuple-element.73.shared_ref, f32[256,2048]{1,0:T(8,128)} %get-tuple-element.71._, bf16[4,64,2048]{2,1,0:T(8,128)(2,1)} %get-tuple-element.74.__.far_ref), custom_call_target="tpu_custom_call" | custom-call | bytes 79200000 | tf_op jit(solution)/shard_map/pallas_call | solution.py:246
  466.8 0.7 slice.17
  467.5 0.6 reshape.61
  468.2 3.7 shard_map.235
  471.9 1.4 slice_bitcast_fusion
  473.3 3.3 reduce-scatter.8.cloned.1.call-done
  476.5 13.3 %shard_map.236.held_ref = bf16[8,64,768]{2,1,0:T(8,128)(2,1)} custom-call(bf16[8,64,768]{2,1,0:T(8,128)(2,1)} %bitcast.29, f32[256,2048]{1,0:T(8,128)} %add.9._, f32[64,5632]{1,0:T(8,128)} %get-tuple-element.44.__, f32[8,128]{1,0:T(8,128)} %get-tuple-element.75.___), custom_call_target="tpu_custom_call" | custom-call | bytes 50400000 | tf_op jit(solution)/shard_map/pallas_call | solution.py:261
  489.8 2.5 shard_map.237
Async XLA Ops:
  7.2 289.1 %reduce-scatter.4.cloned.1.call-start = ((), (), s32[]{:S(2)}) async-start(), calls=%async_computation.3 | async-start | bytes 3604480 | tf_op jit(solution)/shard_map/reduce_scatter | solution.py:1136
  185.2 54.1 %copy-start.3 = (f32[4,2048]{1,0:T(4,128)S(1)}, f32[4,2048]{1,0:T(4,128)}, u32[]{:S(2)}) copy-start(f32[4,2048]{1,0:T(4,128)} %get-tuple-element.52.norm_ref) | copy-start | bytes 98308
  239.2 1.2 copy-start
  239.2 203.7 %reduce-scatter.6.cloned.1.call-start = ((), (), s32[]{:S(2)}) async-start(), calls=%async_computation.4 | async-start | bytes 7208960 | tf_op jit(solution)/shard_map/reduce_scatter | solution.py:1136
  293.1 1.0 copy-start.1
  294.1 0.7 copy-start.2
  294.8 181.7 %reduce-scatter.8.cloned.1.call-start = ((), (), s32[]{:S(2)}) async-start(), calls=%async_computation.5 | async-start | bytes 3932160 | tf_op jit(solution)/shard_map/reduce_scatter | solution.py:1136
  386.9 1.6 copy-start.6
  389.6 48.8 %copy-start.5 = (f32[256,2048]{1,0:T(8,128)S(1)}, f32[256,2048]{1,0:T(8,128)}, u32[]{:S(2)}) copy-start(f32[256,2048]{1,0:T(8,128)} %get-tuple-element.62) | copy-start | bytes 6291460
  438.4 3.3 copy-start.4
Sparse Core Ops, SparseCore 0:
  239.4 56.8 reduce-scatter.3
  298.6 110.9 reduce-scatter.5
  411.9 64.5 reduce-scatter.7

commit v8 on v7

--- a/solution.py
+++ b/solution.py
@@ -871,9 +871,9 @@
         b[...] = jnp.concatenate(bias, axis=1)
         gather.finish()
         swap.finish()
+        wide_line.start()
         rows.finish()
         outs.finish()
-        wide_line.start()
         for copy in stores:
             copy.start()
 

time: 500 us -> 496 us (level)
  transfers between devices with their start and end apart: 3 -> 3, of which waited for: 2 -> 1; matrix products, arithmetic and copies ran while one was open for 4% -> 4% of each run, Pallas kernels for 42% -> 42%
where the time goes in v8:
time: 496 us; the launch traced here: 495 us
  Pallas kernels  455 us (92%)
  between operations  13.9 us (3%)
  matrix products  11.4 us (2%)
  local copies, waits for them, and re-layouts  7.01 us (1%)
  other arithmetic  5.69 us (1%)
    pallas_call x1, Pallas kernels, attend(): pl.pallas_call(functools.partial(attend_kernel, planes), grid=(TEAM,), in...  177 us
    pallas_call x1, Pallas kernels, attend_back(): pl.pallas_call(attend_back_kernel, grid=(seqs,), in_specs=[ANY, whole(wid...  79.3 us
    pallas_call x1, Pallas kernels, expand(): pl.pallas_call(functools.partial(expand_kernel, planes), grid=(seqs,), in...  54.2 us
    pallas_call x1, Pallas kernels, mlp_back(): pl.pallas_call(mlp_back_kernel, out_shape=[jax.ShapeDtypeStruct((rows, wi...  53.4 us
    pallas_call x1, Pallas kernels, last(): pl.pallas_call(functools.partial(last_kernel, planes), out_shape=[jax.Sha...  48.3 us
    pallas_call x1, Pallas kernels, both_closing(): pl.pallas_call(functools.partial(both_close_kernel, planes), out_shape=[j...  23.5 us
    pallas_call x1, Pallas kernels, closing(): pl.pallas_call(close_kernel, out_shape=jax.ShapeDtypeStruct(blocks.shape,...  13.3 us
    dot_general x1, matrix products, dot(): return lax.dot_general(a, b, (dims, ((), ())), preferred_element_type=F32)  11.4 us
  transfers between devices with their start and end apart: 3, of which 1 were waited for; matrix products, arithmetic and copies ran while one was open for 4% of the time, Pallas kernels for 42%

profile of v8, /device:TPU:0, one launch (start us, length us, event | category | flops | bytes accessed | tf_op | source)
XLA Modules:
  0.0 495.1 jit_solution(7405342295307445989)
XLA Ops:
  7.2 0.0 reduce-scatter.4.cloned.1.call-start
  7.2 176.9 %shard_map.229 = (bf16[8,256,2048]{2,1,0:T(8,128)(2,1)}, bf16[8,256,768]{2,1,0:T(8,128)(2,1)}, bf16[8,256,256]{2,1,0:T(8,128)(2,1)}, f32[256,2048]{1,0:T(8,128)}...) custom-call(bf16[64,6144]{1,0:T(8,128)(2,1)} %qkv_w_ref.1, ...), custom_call_target="tpu_custom_call" | custom-call | bytes 648000000 | tf_op jit(solution)/shard_map/pallas_call | solution.py:959
  184.2 0.0 copy-start.3
  184.2 54.2 %shard_map.230 = (f32[8,256,1408]{2,1,0:T(8,128)}, bf16[8,256,704]{2,1,0:T(8,128)(2,1)}, bf16[704,2048]{1,0:T(8,128)(2,1)}, bf16[8,256,2048]{2,1,0:T(8,128)(2,1)}, bf16[4,176,2048]{2,1,0:T(8,128)(2,1)}) custom-call(bf16[8,256,2048]{2,1,0:T(8,128)(2,1)} %get-tuple-element.46.h_ref, bf16[2048,1408]{1,0:T(8,128)(2,1)} %bitcast.21, bf16[256,2048]{1,0:T(8,128)(2,1)} %g_ref.3, ...), custom_call_target="tpu_custom_call" | custom-call | bytes 198000000 | tf_op jit(solution)/shard_map/pallas_call | solution.py:492
  238.4 0.0 copy-start
  238.4 0.0 reduce-scatter.4.cloned.1.call-update
  238.4 0.0 reduce-scatter.6.cloned.1.call-start
  238.5 0.0 copy-done.3
  238.5 1.1 copy-done
  239.6 53.4 %shard_map.231 = (f32[256,2048]{1,0:T(8,128)}, f32[16,2048]{1,0:T(8,128)S(1)}, bf16[256,2048]{1,0:T(8,128)(2,1)S(1)}, bf16[2048,1408]{1,0:T(8,128)(2,1)}) custom-call(f32[8,256,1408]{2,1,0:T(8,128)} %get-tuple-element.48.pre_ref, bf16[8,256,2048]{2,1,0:T(8,128)(2,1)} %get-tuple-element.49.g_all_ref, bf16[2048,2048]{1,0:T(8,128)(2,1)} %bitcast.20, ...), custom_call_target="tpu_custom_call" | custom-call | bytes 216000000 | tf_op jit(solution)/shard_map/pallas_call | solution.py:636
  293.0 0.0 copy-start.1
  293.0 1.0 copy-done.1
  294.0 0.0 copy-start.2
  294.0 0.7 copy-done.2
  294.7 0.0 reduce-scatter.6.cloned.1.call-update
  294.7 0.0 reduce-scatter.8.cloned.1.call-start
  294.7 0.0 reduce-scatter.4.cloned.1.call-done._
  294.8 79.3 %shard_map.232 = (bf16[8,256,768]{2,1,0:T(8,128)(2,1)}, bf16[8,256,2048]{2,1,0:T(8,128)(2,1)}, f32[8,1,768]{2,1,0:T(1,128)}, bf16[256,2048]{1,0:T(8,128)(2,1)}, f32[256,2048]{1,0:T(8,128)}) custom-call(bf16[256,2048]{1,0:T(8,128)(2,1)} %copy-done.1, bf16[256,2048]{1,0:T(8,128)(2,1)} %bitcast.28, bf16[2048,768]{1,0:T(8,128)(2,1)} %bitcast.25, ...), custom_call_target="tpu_custom_call" | custom-call | bytes 234000000 | tf_op jit(solution)/shard_map/pallas_call | solution.py:1085
  374.1 11.4 %bitcast_convert_fusion._ = bf16[2048,768]{1,0:T(8,128)(2,1)} fusion(bf16[8,256,2048]{2,1,0:T(8,128)(2,1)} %get-tuple-element.64, bf16[8,256,768]{2,1,0:T(8,128)(2,1)} %get-tuple-element.65), kind=kOutput, calls=%fused_computation | convolution fusion | flops 6444023808 | bytes 14680064 | tf_op jit(solution)/shard_map/dot_general | solution.py:732
  385.5 0.0 copy-start.6
  385.5 0.0 reduce-scatter.8.cloned.1.call-update
  385.5 1.6 copy-done.6
  387.1 1.1 convert_element_type.9
  388.2 0.0 copy-start.5
  388.2 48.3 %shard_map.233 = (f32[256,2048]{1,0:T(8,128)}, bf16[4,64,2048]{2,1,0:T(8,128)(2,1)}, f32[8,4,8,128]{3,2,1,0:T(8,128)}) custom-call(bf16[8,256,2048]{2,1,0:T(8,128)(2,1)} %get-tuple-element.66.part_ref, bf16[256,2048]{1,0:T(8,128)(2,1)} %x_ref.3, f32[4,2048]{1,0:T(4,128)} %get-tuple-element.52.norm_ref, bf16[4,64,2048]{2,1,0:T(8,128)(2,1)} %bitcast.27, ...), custom_call_target="tpu_custom_call" | custom-call | bytes 208800000 | tf_op jit(solution)/shard_map/pallas_call | solution.py:713
  436.5 0.0 copy-done.5
  436.5 0.0 copy-start.4
  436.5 3.3 add.9._
  439.8 0.0 copy-done.4
  439.8 1.3 convert_element_type.11
  441.1 0.0 reduce-scatter.6.cloned.1.call-done
  441.1 23.5 %shard_map.234 = (bf16[8,64,1408]{2,1,0:T(8,128)(2,1)}, f32[8,128]{1,0:T(8,128)}) custom-call(bf16[8,64,1408]{2,1,0:T(8,128)(2,1)} %bitcast.26, f32[8,4,8,128]{3,2,1,0:T(8,128)} %get-tuple-element.73.shared_ref, f32[256,2048]{1,0:T(8,128)} %get-tuple-element.71._, bf16[4,64,2048]{2,1,0:T(8,128)(2,1)} %get-tuple-element.74.__.far_ref), custom_call_target="tpu_custom_call" | custom-call | bytes 79200000 | tf_op jit(solution)/shard_map/pallas_call | solution.py:246
  464.6 0.7 slice.17
  465.3 0.6 reshape.61
  465.9 3.7 shard_map.235
  469.7 1.4 slice_bitcast_fusion
  471.0 1.7 reduce-scatter.8.cloned.1.call-done
  472.7 13.3 %shard_map.236.held_ref = bf16[8,64,768]{2,1,0:T(8,128)(2,1)} custom-call(bf16[8,64,768]{2,1,0:T(8,128)(2,1)} %bitcast.29, f32[256,2048]{1,0:T(8,128)} %add.9._, f32[64,5632]{1,0:T(8,128)} %get-tuple-element.44.__, f32[8,128]{1,0:T(8,128)} %get-tuple-element.75.___), custom_call_target="tpu_custom_call" | custom-call | bytes 50400000 | tf_op jit(solution)/shard_map/pallas_call | solution.py:261
  486.0 2.5 shard_map.237
Async XLA Ops:
  7.2 287.6 %reduce-scatter.4.cloned.1.call-start = ((), (), s32[]{:S(2)}) async-start(), calls=%async_computation.3 | async-start | bytes 3604480 | tf_op jit(solution)/shard_map/reduce_scatter | solution.py:1136
  184.2 54.3 %copy-start.3 = (f32[4,2048]{1,0:T(4,128)S(1)}, f32[4,2048]{1,0:T(4,128)}, u32[]{:S(2)}) copy-start(f32[4,2048]{1,0:T(4,128)} %get-tuple-element.52.norm_ref) | copy-start | bytes 98308
  238.4 1.2 copy-start
  238.4 202.6 %reduce-scatter.6.cloned.1.call-start = ((), (), s32[]{:S(2)}) async-start(), calls=%async_computation.4 | async-start | bytes 7208960 | tf_op jit(solution)/shard_map/reduce_scatter | solution.py:1136
  293.0 1.0 copy-start.1
  294.0 0.7 copy-start.2
  294.7 178.0 %reduce-scatter.8.cloned.1.call-start = ((), (), s32[]{:S(2)}) async-start(), calls=%async_computation.5 | async-start | bytes 3932160 | tf_op jit(solution)/shard_map/reduce_scatter | solution.py:1136
  385.5 1.6 copy-start.6
  388.2 48.3 %copy-start.5 = (f32[256,2048]{1,0:T(8,128)S(1)}, f32[256,2048]{1,0:T(8,128)}, u32[]{:S(2)}) copy-start(f32[256,2048]{1,0:T(8,128)} %get-tuple-element.62) | copy-start | bytes 6291460
  436.5 3.3 copy-start.4
Sparse Core Ops, SparseCore 0:
  238.6 54.0 reduce-scatter.3
  295.0 110.9 reduce-scatter.5
  408.3 64.2 reduce-scatter.7

commit v9 on v8

--- a/solution.py
+++ b/solution.py
@@ -869,9 +869,9 @@
                 row = lax.broadcasted_iota(jnp.int32, known.shape, 0) == 4 + lax.rem(head, per)
                 bias.append(jnp.sum(jnp.where(row, known, 0.0), axis=0, keepdims=True)[:, :depth])
         b[...] = jnp.concatenate(bias, axis=1)
-        gather.finish()
         swap.finish()
         wide_line.start()
+        gather.finish()
         rows.finish()
         outs.finish()
         for copy in stores:

time: 496 us -> 496 us (level)
  no operation moved by 1% of the time
where the time goes in v9:
time: 496 us; the launch traced here: 495 us
  Pallas kernels  455 us (92%)
  between operations  13.9 us (3%)
  matrix products  11.4 us (2%)
  local copies, waits for them, and re-layouts  7.01 us (1%)
  other arithmetic  5.69 us (1%)
    pallas_call x1, Pallas kernels, attend(): pl.pallas_call(functools.partial(attend_kernel, planes), grid=(TEAM,), in...  177 us
    pallas_call x1, Pallas kernels, attend_back(): pl.pallas_call(attend_back_kernel, grid=(seqs,), in_specs=[ANY, whole(wid...  79.3 us
    pallas_call x1, Pallas kernels, expand(): pl.pallas_call(functools.partial(expand_kernel, planes), grid=(seqs,), in...  54.2 us
    pallas_call x1, Pallas kernels, mlp_back(): pl.pallas_call(mlp_back_kernel, out_shape=[jax.ShapeDtypeStruct((rows, wi...  53.4 us
    pallas_call x1, Pallas kernels, last(): pl.pallas_call(functools.partial(last_kernel, planes), out_shape=[jax.Sha...  48.3 us
    pallas_call x1, Pallas kernels, both_closing(): pl.pallas_call(functools.partial(both_close_kernel, planes), out_shape=[j...  23.5 us
    pallas_call x1, Pallas kernels, closing(): pl.pallas_call(close_kernel, out_shape=jax.ShapeDtypeStruct(blocks.shape,...  13.3 us
    dot_general x1, matrix products, dot(): return lax.dot_general(a, b, (dims, ((), ())), preferred_element_type=F32)  11.4 us
  transfers between devices with their start and end apart: 3, of which 1 were waited for; matrix products, arithmetic and copies ran while one was open for 4% of the time, Pallas kernels for 42%

profile of v9, /device:TPU:0, one launch (start us, length us, event | category | flops | bytes accessed | tf_op | source)
XLA Modules:
  0.0 495.1 jit_solution(16256686388849874025)
XLA Ops:
  7.2 0.0 reduce-scatter.4.cloned.1.call-start
  7.2 176.9 %shard_map.229 = (bf16[8,256,2048]{2,1,0:T(8,128)(2,1)}, bf16[8,256,768]{2,1,0:T(8,128)(2,1)}, bf16[8,256,256]{2,1,0:T(8,128)(2,1)}, f32[256,2048]{1,0:T(8,128)}...) custom-call(bf16[64,6144]{1,0:T(8,128)(2,1)} %qkv_w_ref.1, ...), custom_call_target="tpu_custom_call" | custom-call | bytes 648000000 | tf_op jit(solution)/shard_map/pallas_call | solution.py:959
  184.2 0.0 copy-start.3
  184.2 54.2 %shard_map.230 = (f32[8,256,1408]{2,1,0:T(8,128)}, bf16[8,256,704]{2,1,0:T(8,128)(2,1)}, bf16[704,2048]{1,0:T(8,128)(2,1)}, bf16[8,256,2048]{2,1,0:T(8,128)(2,1)}, bf16[4,176,2048]{2,1,0:T(8,128)(2,1)}) custom-call(bf16[8,256,2048]{2,1,0:T(8,128)(2,1)} %get-tuple-element.46.h_ref, bf16[2048,1408]{1,0:T(8,128)(2,1)} %bitcast.21, bf16[256,2048]{1,0:T(8,128)(2,1)} %g_ref.3, ...), custom_call_target="tpu_custom_call" | custom-call | bytes 198000000 | tf_op jit(solution)/shard_map/pallas_call | solution.py:492
  238.4 0.0 copy-start
  238.4 0.0 reduce-scatter.4.cloned.1.call-update
  238.4 0.0 reduce-scatter.6.cloned.1.call-start
  238.5 0.0 copy-done.3
  238.5 1.1 copy-done
  239.6 53.4 %shard_map.231 = (f32[256,2048]{1,0:T(8,128)}, f32[16,2048]{1,0:T(8,128)S(1)}, bf16[256,2048]{1,0:T(8,128)(2,1)S(1)}, bf16[2048,1408]{1,0:T(8,128)(2,1)}) custom-call(f32[8,256,1408]{2,1,0:T(8,128)} %get-tuple-element.48.pre_ref, bf16[8,256,2048]{2,1,0:T(8,128)(2,1)} %get-tuple-element.49.g_all_ref, bf16[2048,2048]{1,0:T(8,128)(2,1)} %bitcast.20, ...), custom_call_target="tpu_custom_call" | custom-call | bytes 216000000 | tf_op jit(solution)/shard_map/pallas_call | solution.py:636
  293.0 0.0 copy-start.1
  293.0 1.0 copy-done.1
  294.0 0.0 copy-start.2
  294.0 0.7 copy-done.2
  294.7 0.0 reduce-scatter.6.cloned.1.call-update
  294.7 0.0 reduce-scatter.8.cloned.1.call-start
  294.7 0.0 reduce-scatter.4.cloned.1.call-done._
  294.8 79.3 %shard_map.232 = (bf16[8,256,768]{2,1,0:T(8,128)(2,1)}, bf16[8,256,2048]{2,1,0:T(8,128)(2,1)}, f32[8,1,768]{2,1,0:T(1,128)}, bf16[256,2048]{1,0:T(8,128)(2,1)}, f32[256,2048]{1,0:T(8,128)}) custom-call(bf16[256,2048]{1,0:T(8,128)(2,1)} %copy-done.1, bf16[256,2048]{1,0:T(8,128)(2,1)} %bitcast.28, bf16[2048,768]{1,0:T(8,128)(2,1)} %bitcast.25, ...), custom_call_target="tpu_custom_call" | custom-call | bytes 234000000 | tf_op jit(solution)/shard_map/pallas_call | solution.py:1085
  374.1 11.4 %bitcast_convert_fusion._ = bf16[2048,768]{1,0:T(8,128)(2,1)} fusion(bf16[8,256,2048]{2,1,0:T(8,128)(2,1)} %get-tuple-element.64, bf16[8,256,768]{2,1,0:T(8,128)(2,1)} %get-tuple-element.65), kind=kOutput, calls=%fused_computation | convolution fusion | flops 6444023808 | bytes 14680064 | tf_op jit(solution)/shard_map/dot_general | solution.py:732
  385.5 0.0 copy-start.6
  385.5 0.0 reduce-scatter.8.cloned.1.call-update
  385.5 1.6 copy-done.6
  387.1 1.1 convert_element_type.9
  388.2 0.0 copy-start.5
  388.2 48.3 %shard_map.233 = (f32[256,2048]{1,0:T(8,128)}, bf16[4,64,2048]{2,1,0:T(8,128)(2,1)}, f32[8,4,8,128]{3,2,1,0:T(8,128)}) custom-call(bf16[8,256,2048]{2,1,0:T(8,128)(2,1)} %get-tuple-element.66.part_ref, bf16[256,2048]{1,0:T(8,128)(2,1)} %x_ref.3, f32[4,2048]{1,0:T(4,128)} %get-tuple-element.52.norm_ref, bf16[4,64,2048]{2,1,0:T(8,128)(2,1)} %bitcast.27, ...), custom_call_target="tpu_custom_call" | custom-call | bytes 208800000 | tf_op jit(solution)/shard_map/pallas_call | solution.py:713
  436.5 0.0 copy-done.5
  436.5 0.0 copy-start.4
  436.5 3.3 add.9._
  439.8 0.0 copy-done.4
  439.8 1.3 convert_element_type.11
  441.1 0.0 reduce-scatter.6.cloned.1.call-done
  441.1 23.5 %shard_map.234 = (bf16[8,64,1408]{2,1,0:T(8,128)(2,1)}, f32[8,128]{1,0:T(8,128)}) custom-call(bf16[8,64,1408]{2,1,0:T(8,128)(2,1)} %bitcast.26, f32[8,4,8,128]{3,2,1,0:T(8,128)} %get-tuple-element.73.shared_ref, f32[256,2048]{1,0:T(8,128)} %get-tuple-element.71._, bf16[4,64,2048]{2,1,0:T(8,128)(2,1)} %get-tuple-element.74.__.far_ref), custom_call_target="tpu_custom_call" | custom-call | bytes 79200000 | tf_op jit(solution)/shard_map/pallas_call | solution.py:246
  464.6 0.7 slice.17
  465.3 0.6 reshape.61
  465.9 3.7 shard_map.235
  469.7 1.4 slice_bitcast_fusion
  471.0 1.7 reduce-scatter.8.cloned.1.call-done
  472.7 13.3 %shard_map.236.held_ref = bf16[8,64,768]{2,1,0:T(8,128)(2,1)} custom-call(bf16[8,64,768]{2,1,0:T(8,128)(2,1)} %bitcast.29, f32[256,2048]{1,0:T(8,128)} %add.9._, f32[64,5632]{1,0:T(8,128)} %get-tuple-element.44.__, f32[8,128]{1,0:T(8,128)} %get-tuple-element.75.___), custom_call_target="tpu_custom_call" | custom-call | bytes 50400000 | tf_op jit(solution)/shard_map/pallas_call | solution.py:261
  486.0 2.5 shard_map.237
Async XLA Ops:
  7.2 287.6 %reduce-scatter.4.cloned.1.call-start = ((), (), s32[]{:S(2)}) async-start(), calls=%async_computation.3 | async-start | bytes 3604480 | tf_op jit(solution)/shard_map/reduce_scatter | solution.py:1136
  184.2 54.3 %copy-start.3 = (f32[4,2048]{1,0:T(4,128)S(1)}, f32[4,2048]{1,0:T(4,128)}, u32[]{:S(2)}) copy-start(f32[4,2048]{1,0:T(4,128)} %get-tuple-element.52.norm_ref) | copy-start | bytes 98308
  238.4 1.2 copy-start
  238.4 202.6 %reduce-scatter.6.cloned.1.call-start = ((), (), s32[]{:S(2)}) async-start(), calls=%async_computation.4 | async-start | bytes 7208960 | tf_op jit(solution)/shard_map/reduce_scatter | solution.py:1136
  293.0 1.0 copy-start.1
  294.0 0.7 copy-start.2
  294.7 178.0 %reduce-scatter.8.cloned.1.call-start = ((), (), s32[]{:S(2)}) async-start(), calls=%async_computation.5 | async-start | bytes 3932160 | tf_op jit(solution)/shard_map/reduce_scatter | solution.py:1136
  385.5 1.6 copy-start.6
  388.2 48.3 %copy-start.5 = (f32[256,2048]{1,0:T(8,128)S(1)}, f32[256,2048]{1,0:T(8,128)}, u32[]{:S(2)}) copy-start(f32[256,2048]{1,0:T(8,128)} %get-tuple-element.62) | copy-start | bytes 6291460
  436.5 3.3 copy-start.4
Sparse Core Ops, SparseCore 0:
  238.6 54.0 reduce-scatter.3
  295.0 110.9 reduce-scatter.5
  408.3 64.2 reduce-scatter.7
